TPU v7x, 32 devices: a whole 2x2x4 slice. The times are simulated.
32 devices in a mesh: section: 2 (over x), ctx: 4 (over z), fsdp: 4 (over y, core).
Axes of the slice: x: 2, y: 2, z: 4, core: 2. Of those that a mesh axis runs over, the one named last changes fastest.
Arguments:
- inputs: bfloat16 [4, 512, 2, 1536], P(None, ('ctx', 'fsdp')), may hold values from -6 to 6
- cotangent: bfloat16 [4, 512, 2, 1536], P(None, ('ctx', 'fsdp')), may hold values from -6 to 6
- attn_gain: bfloat16 [2, 1536], P('section', 'fsdp'), may hold values from 0.099609375 to 1.8984375
- qkv_weight: bfloat16 [2, 1536, 2048], P('section', 'fsdp'), may hold values from -0.15625 to 0.15625
- qkv_bias: bfloat16 [2, 2048], P('section', 'fsdp'), may hold values from -1.75 to 1.75
- out_weight: bfloat16 [2, 1536, 1536], P('section', 'fsdp'), may hold values from -0.5 to 0.5
- mlp_gain: bfloat16 [2, 1536], P('section', 'fsdp'), may hold values from 0.099609375 to 1.8984375
- gate_weight: bfloat16 [2, 8960, 1536], P('section', 'fsdp'), may hold values from -0.15625 to 0.15625
- up_weight: bfloat16 [2, 8960, 1536], P('section', 'fsdp'), may hold values from -0.15625 to 0.15625
- down_weight: bfloat16 [2, 8960, 1536], P('section', 'fsdp'), may hold values from -0.0625 to 0.0625
Outputs:
- layer_outputs: bfloat16 [2, 4, 512, 2, 1536], P('section', None, ('ctx', 'fsdp'))
- input_grads: bfloat16 [2, 4, 512, 2, 1536], P('section', None, ('ctx', 'fsdp'))
- attn_gain_grad: float32 [2, 1536], P('section', 'fsdp')
- qkv_weight_grad: float32 [2, 1536, 2048], P('section', 'fsdp')
- qkv_bias_grad: float32 [2, 1792], P('section', 'fsdp')
- value_bias_grad: float32 [2, 256], P('section', 'fsdp')
- out_weight_grad: float32 [2, 1536, 1536], P('section', 'fsdp')
- mlp_gain_grad: float32 [2, 1536], P('section', 'fsdp')
- gate_weight_grad: float32 [2, 8960, 1536], P('section', 'fsdp')
- up_weight_grad: float32 [2, 8960, 1536], P('section', 'fsdp')
- down_weight_grad: float32 [2, 8960, 1536], P('section', 'fsdp')
All inputs are finite; a program needn't handle non-finite values.
Results may differ from a plain program's by a relative error of at most 0.028.
Values may be sent and summed in bfloat16 or wider, within the bound.
No kernel may reach another device: no remote copies, remote signals or barrier semaphores. Data moves between devices by JAX's collectives and lax.ppermute only.
A program may use at most 512 MiB of HBM per device.

v0:
```python
import math

import jax
import jax.numpy as jnp
from jax import lax
from jax.sharding import PartitionSpec as P

HEADS = 12
KV_HEADS = 2
HEAD_DIM = 128


epsilon = 1e-06
rope_base = 1000000.0
negative = -1e30


def passed_along(block, axis, distance):
    devices = range(lax.axis_size(axis))
    route = [(i - distance, i) for i in devices if i - distance in devices]
    return lax.ppermute(block, axis, route)


def storage_place(indices, span_rows, half_rows):
    second = 2 * half_rows - span_rows * (indices // span_rows + 1) + indices % span_rows
    return jnp.stack([indices, second], axis=-1)


def rotate(values, places, direction):
    half_width = values.shape[-1] // 2
    frequency = rope_base ** (-(jnp.arange(half_width, dtype=jnp.float32) * 2.0) / (2 * half_width))
    angles = places.astype(jnp.float32)[..., None, None] * frequency
    cosine = jnp.cos(angles)
    sine_part = jnp.sin(angles) * direction
    leading = values[..., :half_width]
    trailing = values[..., half_width:]
    return jnp.concatenate(
        [leading * cosine - trailing * sine_part, trailing * cosine + leading * sine_part], axis=-1
    )


def inverse_rms(values):
    return lax.rsqrt(jnp.mean(values * values, axis=-1, keepdims=True) + epsilon)


def matmul(former, latter):
    return jnp.dot(former, latter, preferred_element_type=jnp.float32)


def matmul_trans(former, latter):
    return lax.dot_general(
        former, latter, (((1,), (1,)), ((), ())), preferred_element_type=jnp.float32
    )


def matmul_rows(former, latter):
    return lax.dot_general(
        former, latter, (((0,), (0,)), ((), ())), preferred_element_type=jnp.float32
    )


def norm_backward(grad_normed, values, inverse, gain):
    scaled = grad_normed * gain
    grad_values = inverse * scaled - values * inverse**3 * jnp.mean(
        scaled * values, axis=-1, keepdims=True
    )
    grad_gain = jnp.sum(grad_normed * values * inverse, axis=0)
    return (grad_values, grad_gain)


def key_layout(keys_all, values_all, span_rows, half_rows):
    kv_heads = keys_all.shape[-1] // HEAD_DIM
    block_len = math.gcd(half_rows, 512)
    blocks = half_rows // block_len
    key_places = storage_place(jnp.arange(half_rows, dtype=jnp.int32), span_rows, half_rows)
    key_blocks = keys_all.reshape(blocks, block_len, 2, kv_heads, HEAD_DIM)
    value_blocks = values_all.reshape(blocks, block_len, 2, kv_heads, HEAD_DIM)
    place_blocks = jnp.swapaxes(key_places.reshape(blocks, block_len, 2), 1, 2)
    return (key_blocks, value_blocks, place_blocks)


def attend_forward(queries, keys_all, values_all, own_places, span_rows, half_rows):
    rows_here = queries.shape[0]
    kv_heads = keys_all.shape[-1] // HEAD_DIM
    group_size = HEADS // kv_heads
    query_five = queries.reshape(rows_here, 2, kv_heads, group_size, HEAD_DIM)
    key_blocks, value_blocks, place_blocks = key_layout(keys_all, values_all, span_rows, half_rows)
    score_scale = HEAD_DIM ** (-0.5)
    stat_shape = (kv_heads, group_size, rows_here, 2)

    def visit_block(state_now, pieces):
        running_max, running_sum, running_acc = state_now
        key_block, value_block, place_block = pieces
        scores = (
            jnp.einsum(
                "rhgjd,kegd->gjrhek", query_five, key_block, preferred_element_type=jnp.float32
            )
            * score_scale
        )
        allowed = place_block[None, None] <= own_places[:, :, None, None]
        scores = jnp.where(allowed, scores, negative)
        new_max = jnp.maximum(running_max, jnp.max(scores, axis=(-2, -1)))
        weights = jnp.where(allowed, jnp.exp(scores - new_max[..., None, None]), 0.0)
        factor = jnp.exp(running_max - new_max)
        running_sum = running_sum * factor + jnp.sum(weights, axis=(-2, -1))
        running_acc = running_acc * factor[..., None] + jnp.einsum(
            "gjrhek,kegd->gjrhd",
            weights.astype(jnp.bfloat16),
            value_block,
            preferred_element_type=jnp.float32,
        )
        return ((new_max, running_sum, running_acc), None)

    start_state = (
        jnp.full(stat_shape, negative, jnp.float32),
        jnp.zeros(stat_shape, jnp.float32),
        jnp.zeros(stat_shape + (HEAD_DIM,), jnp.float32),
    )
    (final_max, final_sum, final_acc), unused = lax.scan(
        visit_block, start_state, (key_blocks, value_blocks, place_blocks)
    )
    attended = jnp.transpose(final_acc / final_sum[..., None], (2, 3, 0, 1, 4)).reshape(
        rows_here, 2, HEADS * HEAD_DIM
    )
    return (attended, final_max + jnp.log(final_sum))


def attend_backward(
    queries, keys_all, values_all, own_places, span_rows, half_rows, grad_att, attended, log_total
):
    rows_here = queries.shape[0]
    kv_heads = keys_all.shape[-1] // HEAD_DIM
    group_size = HEADS // kv_heads
    query_five = queries.reshape(rows_here, 2, kv_heads, group_size, HEAD_DIM)
    grad_five = grad_att.reshape(rows_here, 2, kv_heads, group_size, HEAD_DIM)
    key_blocks, value_blocks, place_blocks = key_layout(keys_all, values_all, span_rows, half_rows)
    score_scale = HEAD_DIM ** (-0.5)
    products = (grad_att.astype(jnp.float32) * attended).reshape(
        rows_here, 2, kv_heads, group_size, HEAD_DIM
    )
    delta_rows = jnp.transpose(jnp.sum(products, axis=-1), (2, 3, 0, 1))

    def visit_block(query_grad, pieces):
        key_block, value_block, place_block = pieces
        scores = (
            jnp.einsum(
                "rhgjd,kegd->gjrhek", query_five, key_block, preferred_element_type=jnp.float32
            )
            * score_scale
        )
        allowed = place_block[None, None] <= own_places[:, :, None, None]
        probs_now = jnp.where(allowed, jnp.exp(scores - log_total[..., None, None]), 0.0)
        grad_probs = jnp.einsum(
            "rhgjd,kegd->gjrhek", grad_five, value_block, preferred_element_type=jnp.float32
        )
        grad_scores = (probs_now * (grad_probs - delta_rows[..., None, None]) * score_scale).astype(
            jnp.bfloat16
        )
        query_grad = query_grad + jnp.einsum(
            "gjrhek,kegd->rhgjd", grad_scores, key_block, preferred_element_type=jnp.float32
        )
        grad_keys = jnp.einsum(
            "gjrhek,rhgjd->kegd", grad_scores, query_five, preferred_element_type=jnp.float32
        )
        grad_values = jnp.einsum(
            "gjrhek,rhgjd->kegd",
            probs_now.astype(jnp.bfloat16),
            grad_five,
            preferred_element_type=jnp.float32,
        )
        block_len = key_block.shape[0]
        kv_term = jnp.concatenate(
            [grad_keys.reshape(block_len, 2, -1), grad_values.reshape(block_len, 2, -1)], axis=-1
        )
        return (query_grad, kv_term)

    start_grad = jnp.zeros((rows_here, 2, kv_heads, group_size, HEAD_DIM), jnp.float32)
    query_grad, kv_terms = lax.scan(
        visit_block, start_grad, (key_blocks, value_blocks, place_blocks)
    )
    return (query_grad.reshape(rows_here, 2, HEADS, HEAD_DIM), kv_terms.reshape(half_rows, 2, -1))


def swiglu(gate_pre, up_pre):
    return (jax.nn.sigmoid(gate_pre) * gate_pre * up_pre).astype(jnp.bfloat16)


def layer_forward(block_in, attn_parts, mlp_parts, own_places, span_rows, half_rows):
    attn_full, qkv_full, bias_full, out_full, mlp_full = attn_parts
    gate_full, up_full, down_full = mlp_parts
    rows_here = block_in.shape[0]
    token_count = rows_here * 2
    source = block_in.astype(jnp.float32).reshape(token_count, -1)
    normed = (source * inverse_rms(source) * attn_full.astype(jnp.float32)).astype(jnp.bfloat16)
    projected = matmul(normed, qkv_full) + bias_full.astype(jnp.float32)
    query_cols = HEADS * HEAD_DIM
    kv_cols = (projected.shape[1] - query_cols) // 2
    queries = rotate(
        projected[:, :query_cols].reshape(rows_here, 2, HEADS, HEAD_DIM), own_places, 1.0
    ).astype(jnp.bfloat16)
    keys = (
        rotate(
            projected[:, query_cols : query_cols + kv_cols].reshape(
                rows_here, 2, kv_cols // HEAD_DIM, HEAD_DIM
            ),
            own_places,
            1.0,
        )
        .astype(jnp.bfloat16)
        .reshape(rows_here, 2, kv_cols)
    )
    values = (
        projected[:, query_cols + kv_cols :].astype(jnp.bfloat16).reshape(rows_here, 2, kv_cols)
    )
    keys_all, values_all = (
        lax.all_gather(keys, ("ctx", "fsdp"), axis=0, tiled=True),
        lax.all_gather(values, ("ctx", "fsdp"), axis=0, tiled=True),
    )
    attended, log_total = attend_forward(
        queries, keys_all, values_all, own_places, span_rows, half_rows
    )
    hidden = source + matmul(attended.astype(jnp.bfloat16).reshape(token_count, -1), out_full)
    normed_two = (hidden * inverse_rms(hidden) * mlp_full.astype(jnp.float32)).astype(jnp.bfloat16)
    gate_pre = matmul_trans(normed_two, gate_full)
    up_pre = matmul_trans(normed_two, up_full)
    branch = matmul(swiglu(gate_pre, up_pre), down_full)
    output = hidden + branch
    saved = (
        block_in,
        queries,
        keys,
        values,
        attended,
        log_total,
        hidden,
        normed_two,
        gate_pre,
        up_pre,
    )
    return (output, saved)


def layer_backward(grad_y, saved, attn_parts, mlp_parts, own_places, span_rows, half_rows):
    block_in, queries, keys, values, attended, log_total, hidden, normed_ffn, gate_pre, up_pre = (
        saved
    )
    attn_full, qkv_full, bias_full, out_full, mlp_full = attn_parts
    gate_full, up_full, down_full = mlp_parts
    rows_here = block_in.shape[0]
    token_count = rows_here * 2
    source = block_in.astype(jnp.float32).reshape(token_count, -1)
    scale_one = inverse_rms(source)
    attn_gain32 = attn_full.astype(jnp.float32)
    normed = (source * scale_one * attn_gain32).astype(jnp.bfloat16)
    scale_two = inverse_rms(hidden)
    sigmoid_gate = jax.nn.sigmoid(gate_pre)
    silu_gate = gate_pre * sigmoid_gate
    activated = (silu_gate * up_pre).astype(jnp.bfloat16)
    grad_low = grad_y.astype(jnp.bfloat16)
    grad_act = matmul_trans(grad_low, down_full)
    grad_gate = (grad_act * up_pre * sigmoid_gate * (1.0 + gate_pre * (1.0 - sigmoid_gate))).astype(
        jnp.bfloat16
    )
    grad_up = (grad_act * silu_gate).astype(jnp.bfloat16)
    grad_normed_two = matmul(grad_gate, gate_full) + matmul(grad_up, up_full)
    grad_from_two, grad_mlp_gain = norm_backward(
        grad_normed_two, hidden, scale_two, mlp_full.astype(jnp.float32)
    )
    grad_hidden = grad_y + grad_from_two
    grad_branch = grad_hidden.astype(jnp.bfloat16)
    attended_low = attended.astype(jnp.bfloat16).reshape(token_count, -1)
    grad_att = matmul_trans(grad_branch, out_full).astype(jnp.bfloat16).reshape(rows_here, 2, -1)
    keys_all, values_all = (
        lax.all_gather(keys, ("ctx", "fsdp"), axis=0, tiled=True),
        lax.all_gather(values, ("ctx", "fsdp"), axis=0, tiled=True),
    )
    query_grad, kv_terms = attend_backward(
        queries,
        keys_all,
        values_all,
        own_places,
        span_rows,
        half_rows,
        grad_att,
        attended,
        log_total,
    )
    kv_sums = lax.psum_scatter(kv_terms, ("ctx", "fsdp"), scatter_dimension=0, tiled=True)
    kv_cols = keys.shape[-1]
    grad_queries = rotate(query_grad, own_places, -1.0)
    grad_keys = rotate(
        kv_sums[..., :kv_cols].reshape(rows_here, 2, kv_cols // HEAD_DIM, HEAD_DIM),
        own_places,
        -1.0,
    )
    grad_values = kv_sums[..., kv_cols:]
    grad_mixed = jnp.concatenate(
        [
            grad_queries.reshape(token_count, -1),
            grad_keys.reshape(token_count, -1),
            grad_values.reshape(token_count, -1),
        ],
        axis=-1,
    ).astype(jnp.bfloat16)
    grad_bias = jnp.sum(grad_mixed.astype(jnp.float32), axis=0)
    grad_normed = matmul_trans(grad_mixed, qkv_full)
    grad_source, grad_attn_gain = norm_backward(grad_normed, source, scale_one, attn_gain32)
    grad_in = grad_hidden + grad_source
    small_grads = (grad_attn_gain, grad_bias, grad_mlp_gain)
    factor_rows = (
        normed,
        grad_mixed,
        attended_low,
        grad_branch,
        activated,
        grad_low,
        normed_ffn,
        grad_gate,
        grad_up,
    )
    return (grad_in, small_grads, factor_rows)


def body(
    inputs,
    cotangent,
    attn_gain,
    qkv_weight,
    qkv_bias,
    out_weight,
    mlp_gain,
    gate_weight,
    up_weight,
    down_weight,
):
    first_section = lax.axis_index("section") == 0
    micro_count = inputs.shape[0]
    rows_here = inputs.shape[1]
    token_count = rows_here * 2
    span_rows = rows_here * lax.axis_size("fsdp")
    half_rows = span_rows * lax.axis_size("ctx")
    own_index = lax.axis_index(("ctx", "fsdp")) * rows_here + jnp.arange(rows_here, dtype=jnp.int32)
    own_places = storage_place(own_index, span_rows, half_rows)
    attn_parts = (
        lax.all_gather(attn_gain[0], "fsdp", axis=0, tiled=True),
        lax.all_gather(qkv_weight[0], "fsdp", axis=0, tiled=True),
        lax.all_gather(qkv_bias[0], "fsdp", axis=0, tiled=True),
        lax.all_gather(out_weight[0], "fsdp", axis=0, tiled=True),
        lax.all_gather(mlp_gain[0], "fsdp", axis=0, tiled=True),
    )
    mlp_parts = (
        lax.all_gather(gate_weight[0], "fsdp", axis=0, tiled=True),
        lax.all_gather(up_weight[0], "fsdp", axis=0, tiled=True),
        lax.all_gather(down_weight[0], "fsdp", axis=0, tiled=True),
    )
    received = jnp.zeros(inputs.shape[1:], jnp.bfloat16)
    outputs_tick = []
    saved_tick = []
    for moment in range(micro_count + 1):
        block_in = jnp.where(first_section, inputs[min(moment, micro_count - 1)], received)
        output, saved = layer_forward(
            block_in, attn_parts, mlp_parts, own_places, span_rows, half_rows
        )
        output_low = output.astype(jnp.bfloat16).reshape(inputs.shape[1:])
        received = passed_along(output_low, "section", 1)
        outputs_tick.append(output_low)
        saved_tick.append(saved)
    grad_received = jnp.zeros(inputs.shape[1:], jnp.bfloat16)
    grad_ticks = []
    small_total = None
    rows_ticks = []
    for moment in range(micro_count + 1):
        micro_here = jnp.where(first_section, moment - 1, moment)
        in_range = jnp.logical_and(micro_here >= 0, micro_here < micro_count)
        grad_y = (
            jnp.where(first_section, grad_received, cotangent[min(moment, micro_count - 1)])
            .astype(jnp.float32)
            .reshape(token_count, -1)
        )
        grad_y = jnp.where(in_range, grad_y, 0.0)
        saved = jax.tree.map(
            lambda earlier, later: jnp.where(first_section, earlier, later),
            saved_tick[max(moment - 1, 0)],
            saved_tick[min(moment + 1, micro_count)],
        )
        grad_in, small_grads, factor_rows = layer_backward(
            grad_y, saved, attn_parts, mlp_parts, own_places, span_rows, half_rows
        )
        grad_low = grad_in.astype(jnp.bfloat16).reshape(inputs.shape[1:])
        grad_received = passed_along(grad_low, "section", -1)
        grad_ticks.append(grad_low)
        rows_ticks.append(factor_rows)
        if small_total is None:
            small_total = small_grads
        else:
            small_total = tuple((summed + added for summed, added in zip(small_total, small_grads)))
    joined = [jnp.concatenate([ticks[index] for ticks in rows_ticks], axis=0) for index in range(9)]
    (
        normed_all,
        mixed_all,
        attended_all,
        branch_all,
        activated_all,
        grad_rows_all,
        ffn_all,
        gate_all,
        up_all,
    ) = joined
    grad_attn_gain, grad_bias, grad_mlp_gain = small_total
    leading_cols = (HEADS + KV_HEADS) * HEAD_DIM
    grad_bias_lead = grad_bias[:leading_cols]
    grad_bias_value = grad_bias[leading_cols:]
    grad_qkv = matmul_rows(normed_all, mixed_all)
    grad_out = matmul_rows(attended_all, branch_all)
    grad_down = matmul_rows(activated_all, grad_rows_all)
    grad_gate = matmul_rows(gate_all, ffn_all)
    grad_up = matmul_rows(up_all, ffn_all)
    grad_down = lax.psum_scatter(
        grad_down.astype(jnp.bfloat16), "fsdp", scatter_dimension=0, tiled=True
    ).astype(jnp.float32)
    grad_gate, grad_up = (
        lax.psum_scatter(
            grad_gate.astype(jnp.bfloat16), "fsdp", scatter_dimension=0, tiled=True
        ).astype(jnp.float32),
        lax.psum_scatter(
            grad_up.astype(jnp.bfloat16), "fsdp", scatter_dimension=0, tiled=True
        ).astype(jnp.float32),
    )
    grad_attn_gain, grad_qkv, grad_bias_lead, grad_bias_value, grad_out, grad_mlp_gain = (
        lax.psum_scatter(
            grad_attn_gain.astype(jnp.bfloat16), "fsdp", scatter_dimension=0, tiled=True
        ).astype(jnp.float32),
        lax.psum_scatter(
            grad_qkv.astype(jnp.bfloat16), "fsdp", scatter_dimension=0, tiled=True
        ).astype(jnp.float32),
        lax.psum_scatter(
            grad_bias_lead.astype(jnp.bfloat16), "fsdp", scatter_dimension=0, tiled=True
        ).astype(jnp.float32),
        lax.psum_scatter(
            grad_bias_value.astype(jnp.bfloat16), "fsdp", scatter_dimension=0, tiled=True
        ).astype(jnp.float32),
        lax.psum_scatter(
            grad_out.astype(jnp.bfloat16), "fsdp", scatter_dimension=0, tiled=True
        ).astype(jnp.float32),
        lax.psum_scatter(
            grad_mlp_gain.astype(jnp.bfloat16), "fsdp", scatter_dimension=0, tiled=True
        ).astype(jnp.float32),
    )
    (
        grad_attn_gain,
        grad_qkv,
        grad_bias_lead,
        grad_bias_value,
        grad_out,
        grad_mlp_gain,
        grad_gate,
        grad_up,
        grad_down,
    ) = (
        lax.psum(grad_attn_gain.astype(jnp.bfloat16), "ctx").astype(jnp.float32),
        lax.psum(grad_qkv.astype(jnp.bfloat16), "ctx").astype(jnp.float32),
        lax.psum(grad_bias_lead.astype(jnp.bfloat16), "ctx").astype(jnp.float32),
        lax.psum(grad_bias_value.astype(jnp.bfloat16), "ctx").astype(jnp.float32),
        lax.psum(grad_out.astype(jnp.bfloat16), "ctx").astype(jnp.float32),
        lax.psum(grad_mlp_gain.astype(jnp.bfloat16), "ctx").astype(jnp.float32),
        lax.psum(grad_gate.astype(jnp.bfloat16), "ctx").astype(jnp.float32),
        lax.psum(grad_up.astype(jnp.bfloat16), "ctx").astype(jnp.float32),
        lax.psum(grad_down.astype(jnp.bfloat16), "ctx").astype(jnp.float32),
    )
    layer_outputs = jnp.stack(
        [
            jnp.where(first_section, outputs_tick[micro], outputs_tick[micro + 1])
            for micro in range(micro_count)
        ]
    )
    input_grads = jnp.stack(
        [
            jnp.where(first_section, grad_ticks[micro + 1], grad_ticks[micro])
            for micro in range(micro_count)
        ]
    )
    return (
        layer_outputs[None],
        input_grads[None],
        grad_attn_gain[None],
        grad_qkv[None],
        grad_bias_lead[None],
        grad_bias_value[None],
        grad_out[None],
        grad_mlp_gain[None],
        grad_gate[None],
        grad_up[None],
        grad_down[None],
    )


def solution(mesh):
    in_specs = (
        P(None, ("ctx", "fsdp"), None, None),
        P(None, ("ctx", "fsdp"), None, None),
        P("section", "fsdp"),
        P("section", "fsdp", None),
        P("section", "fsdp"),
        P("section", "fsdp", None),
        P("section", "fsdp"),
        P("section", "fsdp", None),
        P("section", "fsdp", None),
        P("section", "fsdp", None),
    )
    out_specs = (
        P("section", None, ("ctx", "fsdp"), None, None),
        P("section", None, ("ctx", "fsdp"), None, None),
        P("section", "fsdp"),
        P("section", "fsdp", None),
        P("section", "fsdp"),
        P("section", "fsdp"),
        P("section", "fsdp", None),
        P("section", "fsdp"),
        P("section", "fsdp", None),
        P("section", "fsdp", None),
        P("section", "fsdp", None),
    )
    return jax.shard_map(body, mesh=mesh, in_specs=in_specs, out_specs=out_specs, check_vma=False)
```

profile of v0, /device:TPU:0, one launch (start us, length us, event | category | flops | bytes accessed | tf_op | source)
XLA Modules:
  0.0 3582.7 jit_solution(8043961430327624668)
XLA Ops:
  33.0 25.8 all-gather.14.cloned.1.call-done
  64.3 22.3 all_gather.87
  88.0 19.1 all_gather.88
  117.0 158.7 %all-gather.18.cloned.1.call-done = bf16[1,8960,1536]{2,1,0:T(8,128)(2,1)} async-done(((bf16[1,2240,1536]{2,1,0:T(8,128)(2,1)}), bf16[1,8960,1536]{2,1,0:T(8,128)(2,1)}) %all-gather.18.cloned.1.call-update) | async-done | bytes 27525136 | tf_op jit(solution)/shard_map/all_gather | solution.py:352
  289.9 155.1 %all-gather.20.cloned.1.call-done = bf16[1,8960,1536]{2,1,0:T(8,128)(2,1)} async-done(((bf16[1,2240,1536]{2,1,0:T(8,128)(2,1)}), bf16[1,8960,1536]{2,1,0:T(8,128)(2,1)}) %all-gather.20.cloned.1.call-update) | async-done | bytes 27525136 | tf_op jit(solution)/shard_map/all_gather | solution.py:353
  445.0 15.6 fusion.38
  460.6 153.8 %all-gather.22.cloned.1.call-done = bf16[1,8960,1536]{2,1,0:T(8,128)(2,1)} async-done(((bf16[1,2240,1536]{2,1,0:T(8,128)(2,1)}), bf16[1,8960,1536]{2,1,0:T(8,128)(2,1)}) %all-gather.22.cloned.1.call-update) | async-done | bytes 27525136 | tf_op jit(solution)/shard_map/all_gather | solution.py:354
  632.4 14.9 fusion.8
  653.5 21.9 all_gather.94
  681.5 19.3 all_gather.95
  723.2 19.7 constant_dynamic-update-slice_fusion.26
  781.6 20.4 all_gather.96
  806.7 19.1 all_gather.97
  848.2 15.7 fusion.34
  863.9 15.1 fusion.201
  893.8 20.2 all_gather.98
  920.1 18.9 all_gather.99
  961.4 15.3 fusion.32
  976.8 15.4 broadcast_select_fusion.45
  1012.8 20.1 all_gather.100
  1038.6 18.9 all_gather.101
  1058.2 20.5 all_gather.103
  1107.4 18.9 all_gather.102
  1137.3 22.0 all_gather.104
  1162.3 19.3 all_gather.105
  1183.1 20.2 all_gather.106
  1206.3 21.0 all_gather.107
  1228.8 19.6 all_gather.108
  1253.2 21.2 all_gather.109
  1286.4 19.4 all_gather.110
  1308.7 19.8 all_gather.111
  1382.3 16.0 constant_dynamic-update-slice_fusion.25
  1442.5 91.2 %all-reduce.21.cloned.1.call-done = f32[512,2,512]{2,1,0:T(2,128)} async-done(((f32[512,2,512]{2,1,0:T(2,128)}), f32[512,2,512]{2,1,0:T(2,128)}) %all-reduce.21.cloned.1.call-update) | async-done | bytes 2097168
  1555.5 16.0 constant_dynamic-update-slice_fusion.24
  1615.4 93.1 %all-reduce.23.cloned.1.call-done = f32[512,2,512]{2,1,0:T(2,128)} async-done(((f32[512,2,512]{2,1,0:T(2,128)}), f32[512,2,512]{2,1,0:T(2,128)}) %all-reduce.23.cloned.1.call-update) | async-done | bytes 2097168
  1730.5 17.5 constant_dynamic-update-slice_fusion.23
  1791.9 93.1 %all-reduce.25.cloned.1.call-done = f32[512,2,512]{2,1,0:T(2,128)} async-done(((f32[512,2,512]{2,1,0:T(2,128)}), f32[512,2,512]{2,1,0:T(2,128)}) %all-reduce.25.cloned.1.call-update) | async-done | bytes 2097168
  1906.3 16.0 constant_dynamic-update-slice_fusion.22
  1976.1 82.0 %all-reduce.27.cloned.1.call-done = f32[512,2,512]{2,1,0:T(2,128)} async-done(((f32[512,2,512]{2,1,0:T(2,128)}), f32[512,2,512]{2,1,0:T(2,128)}) %all-reduce.27.cloned.1.call-update) | async-done | bytes 2097168
  2076.5 21.2 convolution_convert_fusion
  2099.5 23.3 convolution_convert_fusion.1
  2124.1 21.3 convolution_convert_fusion.2
  2145.4 23.9 reduce-scatter.6.cloned.1.call-done
  2169.3 198.8 %reduce-scatter.14.cloned.1.call-done = bf16[2240,1536]{1,0:T(8,128)(2,1)} async-done(((bf16[8960,1536]{1,0:T(8,128)(2,1)}), bf16[2240,1536]{1,0:T(8,128)(2,1)}) %reduce-scatter.14.cloned.1.call-update) | async-done | bytes 6881296 | tf_op jit(solution)/shard_map/reduce_scatter | solution.py:418
  2368.0 198.4 %reduce-scatter.12.cloned.1.call-done = bf16[2240,1536]{1,0:T(8,128)(2,1)} async-done(((bf16[8960,1536]{1,0:T(8,128)(2,1)}), bf16[2240,1536]{1,0:T(8,128)(2,1)}) %reduce-scatter.12.cloned.1.call-update) | async-done | bytes 6881296 | tf_op jit(solution)/shard_map/reduce_scatter | solution.py:425
  2566.4 198.6 %reduce-scatter.10.cloned.1.call-done = bf16[2240,1536]{1,0:T(8,128)(2,1)} async-done(((bf16[8960,1536]{1,0:T(8,128)(2,1)}), bf16[2240,1536]{1,0:T(8,128)(2,1)}) %reduce-scatter.10.cloned.1.call-update) | async-done | bytes 6881296 | tf_op jit(solution)/shard_map/reduce_scatter | solution.py:422
  2771.4 16.6 fusion.230
  2823.4 724.3 %all-reduce.29.cloned.1.call-done = (bf16[1,384,2048]{2,1,0:T(8,128)(2,1)}, bf16[1,384,1536]{2,1,0:T(8,128)(2,1)}, bf16[1,2240,1536]{2,1,0:T(8,128)(2,1)}, bf16[...) async-done(((bf16[1,384,2048]{2,1,0:T(8,128)(2,1)}, bf16[1,384,1536]{2,1,0:T(8,128)(2,1)}, bf16[1,2240,1536]{2,1,0:T(8,128)(2,1)}, bf16[1,2240,1536]{2,1,0:T(8,128)(2,1)}, ...) | async-done | bytes 23396368 | tf_op jit(solution)/shard_map/psum | solution.py:461
  (895 shorter events, 704.3 us)
Async XLA Ops:
  7.2 51.6 %all-gather.14.cloned.1.call-start = ((), (), s32[]{:S(2)}) async-start(), calls=%async_computation.10 | async-start | bytes 7864320 | tf_op jit(solution)/shard_map/all_gather | solution.py:346
  7.9 104.7 %all-gather.16.cloned.1.call-start = ((), (), s32[]{:S(2)}) async-start(), calls=%async_computation.11 | async-start | bytes 5898240 | tf_op jit(solution)/shard_map/all_gather | solution.py:348
  8.7 267.0 %all-gather.18.cloned.1.call-start = ((), (), s32[]{:S(2)}) async-start(), calls=%async_computation.12 | async-start | bytes 34406400 | tf_op jit(solution)/shard_map/all_gather | solution.py:352
  9.4 435.6 %all-gather.20.cloned.1.call-start = ((), (), s32[]{:S(2)}) async-start(), calls=%async_computation.13 | async-start | bytes 34406400 | tf_op jit(solution)/shard_map/all_gather | solution.py:353
  10.0 604.3 %all-gather.22.cloned.1.call-start = ((), (), s32[]{:S(2)}) async-start(), calls=%async_computation.14 | async-start | bytes 34406400 | tf_op jit(solution)/shard_map/all_gather | solution.py:354
  10.6 1348.4 %all-reduce.19.cloned.1.call-start = ((), (), s32[]{:S(2)}) async-start(), calls=%async_computation.15 | async-start | bytes 4194304
  19.7 612.6 %copy-start.26 = (f32[64,1536]{1,0:T(8,128)}, f32[64,1536]{1,0:T(8,128)S(1)}, u32[]{:S(2)}) copy-start(f32[64,1536]{1,0:T(8,128)S(1)} %select_n.672) | copy-start | bytes 1179652
  289.9 324.4 %copy-start.2 = (f32[64,8960]{1,0:T(8,128)}, f32[64,8960]{1,0:T(8,128)S(1)}, u32[]{:S(2)}) copy-start(f32[64,8960]{1,0:T(8,128)S(1)} %fusion.58) | copy-start | bytes 6881284
  628.9 18.4 collective-permute-start
  708.8 34.1 copy-start.16
  755.7 19.1 collective-permute-start.1
  804.0 26.2 copy-start.131
  880.0 6.2 collective-permute-start.2
  916.1 27.2 copy-start.133
  993.2 9.0 collective-permute-start.3
  1034.3 272.2 %copy-start.11 = (bf16[32,2,2,6,128]{4,0,3,2,1:T(8,128)(2,1)}, bf16[32,2,2,6,128]{4,0,3,2,1:T(8,128)(2,1)S(1)}, u32[]{:S(2)}) copy-start(bf16[32,2,2,6,128]{4,0,3,2,1:T(8,128)(2,1)S(1)} %pad_maximum_fusion.14) | copy-start | bytes 589828
  1134.5 399.2 %all-reduce.21.cloned.1.call-start = ((), (), s32[]{:S(2)}) async-start(), calls=%async_computation.16 | async-start | bytes 4194304
  1136.5 25.8 copy-start.146
  1181.7 24.6 copy-start.145
  1204.1 45.8 %copy-start.79 = (bf16[512,2,256]{0,2,1:T(8,128)(2,1)}, bf16[512,2,256]{0,2,1:T(8,128)(2,1)S(1)}, u32[]{:S(2)}) copy-start(bf16[512,2,256]{0,2,1:T(8,128)(2,1)S(1)} %copy.267) | copy-start | bytes 1572868
  1227.3 25.9 copy-start.144
  1249.8 28.6 copy-start.150
  1249.8 29.3 copy-start.43
  1249.8 29.3 copy-start.44
  1249.8 29.3 copy-start.47
  1249.8 29.3 copy-start.49
  1249.9 29.3 copy-start.50
  1368.3 30.0 copy-start.93
  1369.1 9.2 collective-permute-start.4
  1398.3 25.3 slice-start.2
  1439.2 97.9 %copy-start.171 = (f32[64]{0:T(128)S(1)}, f32[64]{0:T(128)}, u32[]{:S(2)}) copy-start(f32[64]{0:T(128)} %copy-done.170) | copy-start | bytes 772
  1439.2 269.3 %all-reduce.23.cloned.1.call-start = ((), (), s32[]{:S(2)}) async-start(), calls=%async_computation.17 | async-start | bytes 4194304
  1543.9 7.7 collective-permute-start.5
  1571.5 25.3 slice-start.4
  1612.4 99.6 %copy-start.51 = (f32[64,1536]{1,0:T(8,128)S(1)}, f32[64,1536]{1,0:T(8,128)}, u32[]{:S(2)}) copy-start(f32[64,1536]{1,0:T(8,128)} %reshape.1372) | copy-start | bytes 1179652
  1612.4 272.6 %all-reduce.25.cloned.1.call-start = ((), (), s32[]{:S(2)}) async-start(), calls=%async_computation.18 | async-start | bytes 4194304
  1719.6 7.7 collective-permute-start.6
  1748.0 25.3 slice-start.6
  1788.8 269.3 %all-reduce.27.cloned.1.call-start = ((), (), s32[]{:S(2)}) async-start(), calls=%async_computation.19 | async-start | bytes 4194304
  1894.7 7.7 collective-permute-start.7
  1922.3 24.8 slice-start.8
  1961.9 183.5 %reduce-scatter.8.cloned.1.call-start = ((), (), s32[]{:S(2)}) async-start(), calls=%async_computation.6 | async-start | bytes 5898240 | tf_op jit(solution)/shard_map/reduce_scatter | solution.py:442
  1970.9 198.4 %reduce-scatter.6.cloned.1.call-start = ((), (), s32[]{:S(2)}) async-start(), calls=%async_computation.5 | async-start | bytes 7864320 | tf_op jit(solution)/shard_map/reduce_scatter | solution.py:433
  2075.3 292.7 %reduce-scatter.14.cloned.1.call-start = ((), (), s32[]{:S(2)}) async-start(), calls=%async_computation.9 | async-start | bytes 34406400 | tf_op jit(solution)/shard_map/reduce_scatter | solution.py:418
  2097.7 468.7 %reduce-scatter.12.cloned.1.call-start = ((), (), s32[]{:S(2)}) async-start(), calls=%async_computation.8 | async-start | bytes 34406400 | tf_op jit(solution)/shard_map/reduce_scatter | solution.py:425
  2122.8 642.2 %reduce-scatter.10.cloned.1.call-start = ((), (), s32[]{:S(2)}) async-start(), calls=%async_computation.7 | async-start | bytes 34406400 | tf_op jit(solution)/shard_map/reduce_scatter | solution.py:422
  2145.3 1402.4 %all-reduce.29.cloned.1.call-start = ((), (), s32[]{:S(2)}) async-start(), calls=%async_computation.20 | async-start | bytes 46792704 | tf_op jit(solution)/shard_map/psum | solution.py:461
  2788.1 33.0 copy-start.111
  (172 other events, 1337.2 us)
Sparse Core Ops, SparseCore 0:
  9.6 49.1 all-gather.13
  60.3 45.9 all-gather.15
  107.8 167.8 all-gather.17
  277.1 167.8 all-gather.19
  446.4 167.8 all-gather.21
  1134.6 99.6 all-reduce.18
  1439.3 94.3 all-reduce.20
  1612.5 95.9 all-reduce.22
  1788.9 95.9 all-reduce.24
  1962.0 95.9 all-reduce.26
  2060.8 47.0 reduce-scatter.7
  2110.9 58.3 reduce-scatter.5
  2172.1 195.9 reduce-scatter.13
  2370.5 195.8 reduce-scatter.11
  2569.1 195.9 reduce-scatter.9
  2768.1 779.5 all-reduce.28
where the time goes:
time: 3590 us; the launch traced here: 3580 us
  waiting for transfers between devices  2230 us (62%)
  matrix products  635 us (18%)
  blocking collectives  442 us (12%)
  local copies, waits for them, and re-layouts  134 us (4%)
  other arithmetic  103 us (3%)
    psum x1, waiting for transfers between devices, body(): lax.psum(grad_qkv.astype(jnp.bfloat16), 'ctx').astype(jnp.float32)  724 us
    unnamed x21, waiting for transfers between devices  363 us
    dot_general x25, matrix products, matmul_trans(): lax.dot_general(former, latter, (((1,), (1,)), ((), ())), preferred_eleme...  264 us
    dot_general x25, matrix products, matmul(): return jnp.dot(former, latter, preferred_element_type=jnp.float32)  234 us
    reduce_scatter x1, waiting for transfers between devices, body(): lax.psum_scatter(grad_down.astype(jnp.bfloat16), 'fsdp', scatter_dimensio...  199 us
    reduce_scatter x1, waiting for transfers between devices, body(): lax.psum_scatter(grad_gate.astype(jnp.bfloat16), 'fsdp', scatter_dimensio...  199 us
    reduce_scatter x1, waiting for transfers between devices, body(): lax.psum_scatter(grad_up.astype(jnp.bfloat16), 'fsdp', scatter_dimension=...  198 us
    all_gather x1, waiting for transfers between devices, body(): lax.all_gather(gate_weight[0], 'fsdp', axis=0, tiled=True)  159 us
  transfers between devices with their start and end apart: 24, of which 19 were waited for; matrix products, arithmetic and copies ran while one was open for 8% of the time, Pallas kernels for 0%

commit v1 on v0

v1 whole, which is shorter than its diff:
```python
import functools
import math

import jax
import jax.numpy as jnp
from jax import lax
from jax.experimental import pallas as pl
from jax.experimental.pallas import tpu as pltpu
from jax.sharding import PartitionSpec as P

HEADS = 12
KV_HEADS = 2
HEAD_DIM = 128
GROUP = HEADS // KV_HEADS
EPS = 1e-06
ROPE_BASE = 1000000.0
NEGATIVE = -1e30
QCOLS = HEADS * HEAD_DIM
KCOLS = KV_HEADS * HEAD_DIM
SCALE = HEAD_DIM ** (-0.5)

MICROS = 1
LAG = 2

f32 = jnp.float32
bf16 = jnp.bfloat16
MIB = 1 << 20


def dot_nn(a, b):
    return lax.dot_general(a, b, (((1,), (0,)), ((), ())), preferred_element_type=f32)


def dot_nt(a, b):
    return lax.dot_general(a, b, (((1,), (1,)), ((), ())), preferred_element_type=f32)


def dot_tn(a, b):
    return lax.dot_general(a, b, (((0,), (0,)), ((), ())), preferred_element_type=f32)


def inverse_rms(values):
    return lax.rsqrt(jnp.mean(values * values, axis=-1, keepdims=True) + EPS)


def norm_backward(grad_normed, values, gain):
    inverse = inverse_rms(values)
    scaled = grad_normed * gain
    grad_values = inverse * scaled - values * (
        inverse**3 * jnp.mean(scaled * values, axis=-1, keepdims=True)
    )
    grad_gain = jnp.sum(grad_normed * values * inverse, axis=0, keepdims=True)
    return grad_values, grad_gain


def storage_place(indices, span_rows, half_rows):
    second = 2 * half_rows - span_rows * (indices // span_rows + 1) + indices % span_rows
    return jnp.stack([indices, second], axis=-1)


def exchange(block, axis, mask):
    size = lax.axis_size(axis)
    return lax.ppermute(block, axis, [(i, i ^ mask) for i in range(size)])


def passed_along(block, axis, distance):
    devices = range(lax.axis_size(axis))
    route = [(i - distance, i) for i in devices if i - distance in devices]
    return lax.ppermute(block, axis, route)


def bits_of(size):
    return [1 << b for b in reversed(range(size.bit_length() - 1))]


def relative_order(size):
    order = [0]
    for bit in bits_of(size):
        order = order + [r ^ bit for r in order]
    return order


def gather_pieces(block, axis):
    pieces = [block]
    for bit in bits_of(lax.axis_size(axis)):
        pieces = pieces + [exchange(p, axis, bit) for p in pieces]
    return pieces


def add_low(terms):
    total = terms[0].astype(f32)
    for term in terms[1:]:
        total = total + term.astype(f32)
    return total.astype(bf16)


def reduce_pieces(parts, axis):
    terms = [[p] for p in parts]
    for bit in reversed(bits_of(lax.axis_size(axis))):
        half = len(terms) // 2
        sent = [t[0] if len(t) == 1 else add_low(t) for t in terms[half:]]
        terms = [t + [exchange(s, axis, bit)] for t, s in zip(terms[:half], sent)]
    return terms[0]


def call(kernel, out_shape, args, flops, moved, name, limit=40, **kwargs):
    return pl.pallas_call(
        kernel,
        out_shape=out_shape,
        compiler_params=pltpu.CompilerParams(vmem_limit_bytes=limit * MIB),
        cost_estimate=pl.CostEstimate(flops=flops, bytes_accessed=moved, transcendentals=0),
        name=name,
        **kwargs,
    )(*args)


def turn(value, cos, sin):
    return value * cos + pltpu.roll(value, HEAD_DIM // 2, 1) * sin


def repeat_rows(table, count):
    return table if count == 1 else jnp.concatenate([table] * count, axis=0)


def project_kernel(reps, x_ref, gain_ref, w_ref, b_ref, cos_ref, sin_ref, q_ref, kv_ref, n_ref):
    step = pl.program_id(0)

    @pl.when(step == 0)
    def _():
        x = x_ref[...].astype(f32)
        n_ref[...] = (x * inverse_rms(x) * gain_ref[...].astype(f32)).astype(bf16)

    cos = repeat_rows(cos_ref[...], reps)
    sin = repeat_rows(sin_ref[...], reps)
    heads_here = w_ref.shape[1] // HEAD_DIM
    projected = dot_nn(n_ref[...], w_ref[...]) + b_ref[...].astype(f32)
    turned = []
    for j in range(heads_here):
        part = projected[:, j * HEAD_DIM : (j + 1) * HEAD_DIM]
        is_value = step * heads_here + j >= HEADS + KV_HEADS
        turned.append(jnp.where(is_value, part, turn(part, cos, sin)))
    low = jnp.concatenate(turned, axis=1).astype(bf16)

    @pl.when(step < pl.num_programs(0) - 1)
    def _():
        q_ref[...] = low

    @pl.when(step == pl.num_programs(0) - 1)
    def _():
        kv_ref[...] = low


def project(x, gain, w, b, cos, sin, reps):
    tokens, width = x.shape
    columns = w.shape[1]
    tile = 2 * KCOLS
    steps = columns // tile
    last_q = QCOLS // tile - 1
    return call(
        functools.partial(project_kernel, reps),
        (
            jax.ShapeDtypeStruct((tokens, QCOLS), bf16),
            jax.ShapeDtypeStruct((tokens, 2 * KCOLS), bf16),
        ),
        (x, gain, w, b, cos, sin),
        2 * tokens * width * columns,
        2 * width * columns,
        "project",
        grid=(steps,),
        in_specs=[
            pl.BlockSpec((tokens, width), lambda i: (0, 0)),
            pl.BlockSpec((1, width), lambda i: (0, 0)),
            pl.BlockSpec((width, tile), lambda i: (0, i)),
            pl.BlockSpec((1, tile), lambda i: (0, i)),
            pl.BlockSpec(cos.shape, lambda i: (0, 0)),
            pl.BlockSpec(sin.shape, lambda i: (0, 0)),
        ],
        out_specs=(
            pl.BlockSpec((tokens, tile), lambda i: (0, jnp.minimum(i, last_q))),
            pl.BlockSpec((tokens, tile), lambda i: (0, 0)),
        ),
        scratch_shapes=[pltpu.VMEM((tokens, width), bf16)],
    )


def head_rows(block, g):
    return jnp.concatenate(
        [
            block[:, (g * GROUP + j) * HEAD_DIM : (g * GROUP + j + 1) * HEAD_DIM]
            for j in range(GROUP)
        ],
        axis=0,
    )


def head_columns(rows, tokens):
    return [rows[j * tokens : (j + 1) * tokens] for j in range(GROUP)]


def key_rows(ref, seq, reps, tokens, column):
    columns = slice(column * HEAD_DIM, (column + 1) * HEAD_DIM)
    if reps == 1:
        return ref[:, columns]
    stride = reps * tokens
    return jnp.concatenate(
        [
            ref[a * stride + seq * tokens : a * stride + (seq + 1) * tokens, columns]
            for a in range(ref.shape[0] // stride)
        ],
        axis=0,
    )


def masked_scores(q, key_block, mask, tokens):
    scores = dot_nt(q, key_block) * SCALE
    keys = scores.shape[1]
    return (scores.reshape(GROUP, tokens, keys) + mask[None]).reshape(GROUP * tokens, keys)


def attend_kernel(pieces, reps, *refs):
    q_ref, x_ref, mask_ref, ow_ref, gain_ref = refs[:5]
    kv_refs = refs[5 : 5 + pieces]
    att_ref, hid_ref, n2_ref = refs[5 + pieces :]
    tokens = q_ref.shape[0] // reps
    for seq in range(reps):
        rows = slice(seq * tokens, (seq + 1) * tokens)
        q_all = q_ref[rows, :]
        for g in range(KV_HEADS):
            q = head_rows(q_all, g)
            scores = [
                masked_scores(q, key_rows(kv, seq, reps, tokens, g), mask_ref[p], tokens)
                for p, kv in enumerate(kv_refs)
            ]
            top = functools.reduce(
                jnp.maximum, [jnp.max(s, axis=-1, keepdims=True) for s in scores]
            )
            total = jnp.zeros_like(top)
            acc = jnp.zeros((GROUP * tokens, HEAD_DIM), f32)
            for s, kv in zip(scores, kv_refs):
                weights = jnp.exp(s - top)
                total = total + jnp.sum(weights, axis=-1, keepdims=True)
                acc = acc + dot_nn(
                    weights.astype(bf16), key_rows(kv, seq, reps, tokens, KV_HEADS + g)
                )
            low = (acc / total).astype(bf16)
            for j, block in enumerate(head_columns(low, tokens)):
                head = g * GROUP + j
                att_ref[rows, head * HEAD_DIM : (head + 1) * HEAD_DIM] = block
    hidden = x_ref[...].astype(f32) + dot_nn(att_ref[...], ow_ref[...])
    hid_ref[...] = hidden
    n2_ref[...] = (hidden * inverse_rms(hidden) * gain_ref[...].astype(f32)).astype(bf16)


def attend(q, x, mask, ow, gain, kv_pieces, reps):
    tokens, width = x.shape
    keys = sum(p.shape[0] for p in kv_pieces)
    return call(
        functools.partial(attend_kernel, len(kv_pieces), reps),
        (
            jax.ShapeDtypeStruct((tokens, QCOLS), bf16),
            jax.ShapeDtypeStruct((tokens, width), f32),
            jax.ShapeDtypeStruct((tokens, width), bf16),
        ),
        (q, x, mask, ow, gain, *kv_pieces),
        2 * tokens * QCOLS * width + 12 * tokens * QCOLS * keys // reps,
        2 * QCOLS * width + 4 * keys * KCOLS,
        "attend",
    )


def fill(scratch, refs):
    size = refs[0].shape[0]
    for p, ref in enumerate(refs):
        scratch[p * size : (p + 1) * size, :] = ref[...]


def mlp_kernel(pieces, *refs):
    n_refs = refs[:pieces]
    gate_ref, up_ref, down_ref = refs[pieces : pieces + 3]
    out_refs = refs[pieces + 3 : 2 * pieces + 3]
    cat_ref, acc_ref = refs[2 * pieces + 3 :]
    step = pl.program_id(0)

    @pl.when(step == 0)
    def _():
        fill(cat_ref, n_refs)
        acc_ref[...] = jnp.zeros_like(acc_ref)

    rows = cat_ref[...]
    gate_pre = dot_nt(rows, gate_ref[...])
    up_pre = dot_nt(rows, up_ref[...])
    activated = (jax.nn.sigmoid(gate_pre) * gate_pre * up_pre).astype(bf16)
    acc_ref[...] += dot_nn(activated, down_ref[...])

    @pl.when(step == pl.num_programs(0) - 1)
    def _():
        size = out_refs[0].shape[0]
        for p, ref in enumerate(out_refs):
            ref[...] = acc_ref[p * size : (p + 1) * size, :].astype(bf16)


def unit_tile(units, most):
    best = max(t for t in range(16, most + 1, 16) if units % t == 0)
    return best


def mlp(n_pieces, gate, up, down):
    units, width = gate.shape
    tokens = n_pieces[0].shape[0]
    count = len(n_pieces)
    tile = unit_tile(units, 512)
    whole = pl.BlockSpec((tokens, width), lambda i: (0, 0))
    part = pl.BlockSpec((tile, width), lambda i: (i, 0))
    return call(
        functools.partial(mlp_kernel, count),
        tuple(jax.ShapeDtypeStruct((tokens, width), bf16) for _ in n_pieces),
        (*n_pieces, gate, up, down),
        6 * count * tokens * width * units,
        6 * width * units,
        "mlp",
        grid=(units // tile,),
        in_specs=[whole] * count + [part] * 3,
        out_specs=tuple(whole for _ in n_pieces),
        scratch_shapes=[
            pltpu.VMEM((count * tokens, width), bf16),
            pltpu.VMEM((count * tokens, width), f32),
        ],
    )


def swiglu_backward(gate_pre, up_pre, grad_act):
    sigmoid = jax.nn.sigmoid(gate_pre)
    silu = gate_pre * sigmoid
    grad_gate = (grad_act * up_pre * (sigmoid + silu * (1.0 - sigmoid))).astype(bf16)
    grad_up = (grad_act * silu).astype(bf16)
    return silu, grad_gate, grad_up


def mlp_back_kernel(pieces, *refs):
    n_refs = refs[:pieces]
    g_refs = refs[pieces : 2 * pieces]
    gate_ref, up_ref, down_ref = refs[2 * pieces : 2 * pieces + 3]
    out_refs = refs[2 * pieces + 3 : 3 * pieces + 3]
    cat_ref, gcat_ref, acc_ref = refs[3 * pieces + 3 :]
    step = pl.program_id(0)

    @pl.when(step == 0)
    def _():
        fill(cat_ref, n_refs)
        fill(gcat_ref, g_refs)
        acc_ref[...] = jnp.zeros_like(acc_ref)

    rows = cat_ref[...]
    gate_pre = dot_nt(rows, gate_ref[...])
    up_pre = dot_nt(rows, up_ref[...])
    grad_act = dot_nt(gcat_ref[...], down_ref[...])
    _, grad_gate, grad_up = swiglu_backward(gate_pre, up_pre, grad_act)
    acc_ref[...] += dot_nn(grad_gate, gate_ref[...]) + dot_nn(grad_up, up_ref[...])

    @pl.when(step == pl.num_programs(0) - 1)
    def _():
        size = out_refs[0].shape[0]
        for p, ref in enumerate(out_refs):
            ref[...] = acc_ref[p * size : (p + 1) * size, :].astype(bf16)


def mlp_back(n_pieces, g_pieces, gate, up, down):
    units, width = gate.shape
    tokens = n_pieces[0].shape[0]
    count = len(n_pieces)
    tile = unit_tile(units, 512)
    whole = pl.BlockSpec((tokens, width), lambda i: (0, 0))
    part = pl.BlockSpec((tile, width), lambda i: (i, 0))
    return call(
        functools.partial(mlp_back_kernel, count),
        tuple(jax.ShapeDtypeStruct((tokens, width), bf16) for _ in n_pieces),
        (*n_pieces, *g_pieces, gate, up, down),
        10 * count * tokens * width * units,
        6 * width * units,
        "mlp_back",
        grid=(units // tile,),
        in_specs=[whole] * (2 * count) + [part] * 3,
        out_specs=tuple(whole for _ in n_pieces),
        scratch_shapes=[
            pltpu.VMEM((count * tokens, width), bf16),
            pltpu.VMEM((count * tokens, width), bf16),
            pltpu.VMEM((count * tokens, width), f32),
        ],
    )


def sum_refs(refs):
    total = refs[0][...].astype(f32)
    for ref in refs[1:]:
        total = total + ref[...].astype(f32)
    return total


def attend_back_kernel(pieces, terms, reps, *refs):
    gy_ref, hid_ref, gain_ref, ow_ref, q_ref, mask_ref, cos_ref, sin_ref = refs[:8]
    kv_refs = refs[8 : 8 + pieces]
    t_refs = refs[8 + pieces : 8 + pieces + terms]
    gh_ref, ghl_ref, dq_ref, mg_ref = refs[8 + pieces + terms : 12 + pieces + terms]
    dkv_refs = refs[12 + pieces + terms :]
    tokens = q_ref.shape[0] // reps
    grad_from_two, grad_gain = norm_backward(
        sum_refs(t_refs), hid_ref[...], gain_ref[...].astype(f32)
    )
    mg_ref[...] = grad_gain
    grad_hidden = gy_ref[...].astype(f32) + grad_from_two
    gh_ref[...] = grad_hidden
    grad_low = grad_hidden.astype(bf16)
    ghl_ref[...] = grad_low
    grad_att = dot_nt(grad_low, ow_ref[...]).astype(bf16)
    cos = cos_ref[...]
    sin = sin_ref[...]
    for seq in range(reps):
        rows = slice(seq * tokens, (seq + 1) * tokens)
        q_all = q_ref[rows, :]
        grad_all = grad_att[rows, :]
        for g in range(KV_HEADS):
            q = head_rows(q_all, g)
            go = head_rows(grad_all, g)
            key_blocks = [key_rows(kv, seq, reps, tokens, g) for kv in kv_refs]
            scores = [
                masked_scores(q, k, mask_ref[p], tokens) for p, k in enumerate(key_blocks)
            ]
            top = functools.reduce(
                jnp.maximum, [jnp.max(s, axis=-1, keepdims=True) for s in scores]
            )
            weights = [jnp.exp(s - top) for s in scores]
            total = functools.reduce(
                jnp.add, [jnp.sum(w, axis=-1, keepdims=True) for w in weights]
            )
            scale = 1.0 / total
            probs = [w * scale for w in weights]
            grad_probs = [
                dot_nt(go, key_rows(kv, seq, reps, tokens, KV_HEADS + g)) for kv in kv_refs
            ]
            delta = functools.reduce(
                jnp.add,
                [jnp.sum(p * d, axis=-1, keepdims=True) for p, d in zip(probs, grad_probs)],
            )
            dq = jnp.zeros((GROUP * tokens, HEAD_DIM), f32)
            for p in range(pieces):
                grad_z = (probs[p] * (grad_probs[p] - delta) * SCALE).astype(bf16)
                dq = dq + dot_nn(grad_z, key_blocks[p])
                dk = dot_tn(grad_z, q).astype(bf16)
                dv = dot_tn(probs[p].astype(bf16), go).astype(bf16)
                stride = reps * tokens
                for a in range(dk.shape[0] // tokens):
                    here = slice(a * stride + seq * tokens, a * stride + (seq + 1) * tokens)
                    part = slice(a * tokens, (a + 1) * tokens)
                    dkv_refs[p][here, g * HEAD_DIM : (g + 1) * HEAD_DIM] = dk[part]
                    v_at = (KV_HEADS + g) * HEAD_DIM
                    dkv_refs[p][here, v_at : v_at + HEAD_DIM] = dv[part]
            for j, block in enumerate(head_columns(dq, tokens)):
                head = g * GROUP + j
                dq_ref[rows, head * HEAD_DIM : (head + 1) * HEAD_DIM] = turn(
                    block, cos, -sin
                ).astype(bf16)


def attend_back(gy, hidden, gain, ow, q, mask, cos, sin, kv_pieces, terms, reps):
    tokens, width = gy.shape
    keys = sum(p.shape[0] for p in kv_pieces)
    return call(
        functools.partial(attend_back_kernel, len(kv_pieces), len(terms), reps),
        (
            jax.ShapeDtypeStruct((tokens, width), f32),
            jax.ShapeDtypeStruct((tokens, width), bf16),
            jax.ShapeDtypeStruct((tokens, QCOLS), bf16),
            jax.ShapeDtypeStruct((1, width), f32),
            *(jax.ShapeDtypeStruct(p.shape, bf16) for p in kv_pieces),
        ),
        (gy, hidden, gain, ow, q, mask, cos, sin, *kv_pieces, *terms),
        2 * tokens * QCOLS * width + 30 * tokens * QCOLS * keys // reps,
        2 * QCOLS * width + 8 * keys * KCOLS,
        "attend_back",
        limit=56,
    )


def project_back_kernel(terms, reps, *refs):
    dq_ref, x_ref, gh_ref, gain_ref, w_ref, cos_ref, sin_ref = refs[:7]
    t_refs = refs[7 : 7 + terms]
    gin_ref, gp_ref, n_ref, b_ref, ag_ref = refs[7 + terms :]
    dkv = sum_refs(t_refs)
    cos = repeat_rows(cos_ref[...], reps)
    sin = repeat_rows(sin_ref[...], reps)
    parts = [
        turn(dkv[:, j * HEAD_DIM : (j + 1) * HEAD_DIM], cos, -sin) for j in range(KV_HEADS)
    ]
    parts.append(dkv[:, KCOLS:])
    gp_ref[:, :QCOLS] = dq_ref[...]
    gp_ref[:, QCOLS:] = jnp.concatenate(parts, axis=1).astype(bf16)
    grad_projected = gp_ref[...]
    b_ref[...] = jnp.sum(grad_projected.astype(f32), axis=0, keepdims=True)
    x = x_ref[...].astype(f32)
    gain = gain_ref[...].astype(f32)
    n_ref[...] = (x * inverse_rms(x) * gain).astype(bf16)
    grad_normed = dot_nt(grad_projected, w_ref[...])
    grad_source, grad_gain = norm_backward(grad_normed, x, gain)
    ag_ref[...] = grad_gain
    gin_ref[...] = (gh_ref[...] + grad_source).astype(bf16)


def project_back(dq, x, gh, gain, w, cos, sin, terms, reps):
    tokens, width = x.shape
    columns = w.shape[1]
    return call(
        functools.partial(project_back_kernel, len(terms), reps),
        (
            jax.ShapeDtypeStruct((tokens, width), bf16),
            jax.ShapeDtypeStruct((tokens, columns), bf16),
            jax.ShapeDtypeStruct((tokens, width), bf16),
            jax.ShapeDtypeStruct((1, columns), f32),
            jax.ShapeDtypeStruct((1, width), f32),
        ),
        (dq, x, gh, gain, w, cos, sin, *terms),
        2 * tokens * width * columns,
        2 * width * columns,
        "project_back",
    )


def weight_grad_kernel(aliased, *refs):
    n_ref, g_ref, gate_ref, up_ref, down_ref = refs[:5]
    dg_ref, du_ref, dd_ref = refs[5 + aliased :]
    step = pl.program_id(1)

    @pl.when(step == 0)
    def _():
        dg_ref[...] = jnp.zeros_like(dg_ref)
        du_ref[...] = jnp.zeros_like(du_ref)
        dd_ref[...] = jnp.zeros_like(dd_ref)

    rows = n_ref[...]
    grads = g_ref[...]
    gate_pre = dot_nt(gate_ref[...], rows)
    up_pre = dot_nt(up_ref[...], rows)
    grad_act = dot_nt(down_ref[...], grads)
    silu, grad_gate, grad_up = swiglu_backward(gate_pre, up_pre, grad_act)
    activated = (silu * up_pre).astype(bf16)
    dg_ref[...] += dot_nn(grad_gate, rows)
    du_ref[...] += dot_nn(grad_up, rows)
    dd_ref[...] += dot_nn(activated, grads)


def weight_grads(n_all, g_all, gate, up, down, calls):
    units, width = gate.shape
    tokens = n_all.shape[0]
    tile = unit_tile(units, 320)
    chunk = math.gcd(tokens, 1024)
    tiles = units // tile
    shape = jax.ShapeDtypeStruct((units, width), f32)
    outs = ()
    first = 0
    for index in range(calls):
        here = tiles // calls + (1 if index < tiles % calls else 0)
        part = pl.BlockSpec((tile, width), lambda i, j, first=first: (i + first, 0))
        rows = pl.BlockSpec((chunk, width), lambda i, j: (j, 0))
        outs = call(
            functools.partial(weight_grad_kernel, len(outs)),
            (shape,) * 3,
            (n_all, g_all, gate, up, down, *outs),
            12 * tokens * width * tile * here,
            18 * width * tile * here,
            "weight_grads",
            limit=56,
            grid=(here, tokens // chunk),
            in_specs=[rows] * 2 + [part] * 3 + [pl.BlockSpec(memory_space=pl.ANY)] * len(outs),
            out_specs=(part,) * 3,
            input_output_aliases={5 + k: k for k in range(len(outs))},
        )
        first += here
    return outs


def body(
    inputs,
    cotangent,
    attn_gain,
    qkv_weight,
    qkv_bias,
    out_weight,
    mlp_gain,
    gate_weight,
    up_weight,
    down_weight,
):
    first = lax.axis_index("section") == 0
    micro, rows_here, _, width = inputs.shape
    fsdp = lax.axis_size("fsdp")
    ctx = lax.axis_size("ctx")
    fsdp_at = lax.axis_index("fsdp")
    ctx_at = lax.axis_index("ctx")
    tokens = 2 * rows_here
    reps = MICROS
    chunks = micro // reps
    steps = chunks + LAG
    span_rows = rows_here * fsdp
    half_rows = span_rows * ctx

    def places_of(c, f):
        index = (c * fsdp + f) * rows_here + jnp.arange(rows_here, dtype=jnp.int32)
        return storage_place(index, span_rows, half_rows).reshape(tokens)

    own = places_of(ctx_at, fsdp_at)
    key_places = jnp.stack(
        [
            jnp.concatenate([places_of(ctx_at ^ a, fsdp_at ^ r) for a in range(ctx)])
            for r in relative_order(fsdp)
        ]
    )
    mask = jnp.where(key_places[:, None, :] <= own[None, :, None], 0.0, NEGATIVE).astype(f32)
    half = HEAD_DIM // 2
    frequency = ROPE_BASE ** (-(jnp.arange(half, dtype=f32) * 2.0) / HEAD_DIM)
    angles = own.astype(f32)[:, None] * frequency
    cos = jnp.concatenate([jnp.cos(angles)] * 2, axis=1)
    sin = jnp.concatenate([-jnp.sin(angles), jnp.sin(angles)], axis=1)

    def gathered(shard):
        return lax.all_gather(shard, "fsdp", axis=0, tiled=True)

    qkv_full = gathered(qkv_weight[0])
    attn_full = gathered(attn_gain[0])[None]
    bias_full = gathered(qkv_bias[0])[None]
    mlp_full = gathered(mlp_gain[0])[None]
    out_full = gathered(out_weight[0])
    gate, up, down = gate_weight[0], up_weight[0], down_weight[0]

    def chunked(array):
        return array.reshape(chunks, reps * tokens, width)

    in_chunks = chunked(inputs)
    cot_chunks = chunked(cotangent)

    outputs, saved, moved = [], [], []
    for t in range(steps):
        if t < LAG:
            x = in_chunks[t]
        else:
            x = jnp.where(first, in_chunks[min(t, chunks - 1)], moved[t - LAG])
        q, kv = project(x, attn_full, qkv_full, bias_full, cos, sin, reps)
        kv_ctx = jnp.concatenate([kv] + [exchange(kv, "ctx", a) for a in range(1, ctx)], axis=0)
        kv_pieces = gather_pieces(kv_ctx, "fsdp")
        attended, hidden, n2 = attend(q, x, mask, out_full, mlp_full, kv_pieces, reps)
        n2_pieces = gather_pieces(n2, "fsdp")
        parts = mlp(n2_pieces, gate, up, down)
        terms = reduce_pieces(list(parts), "fsdp")
        y = add_low([hidden] + terms)
        outputs.append(y)
        if t < chunks:
            moved.append(passed_along(y, "section", 1))
        saved.append((x, q, attended, hidden, *kv_pieces, *n2_pieces))

    def pick(early, late):
        return jnp.where(first, early, late)

    n2_own = jnp.concatenate(
        [pick(saved[m][4 + fsdp], saved[m + LAG][4 + fsdp]) for m in range(chunks)], axis=0
    )
    n2_all = lax.all_gather(n2_own, ("ctx", "fsdp"), axis=0, tiled=True)

    grads_in, grads_moved, gys, smalls, factors = [], [], [], [], []
    for u in range(steps):
        if u < LAG:
            gy = jnp.where(first, jnp.zeros_like(cot_chunks[u]), cot_chunks[u])
        elif u < chunks:
            gy = pick(grads_moved[u - LAG], cot_chunks[u])
        else:
            gy = pick(grads_moved[u - LAG], jnp.zeros_like(cot_chunks[0]))
        gys.append(gy)
        both = zip(saved[max(u - LAG, 0)], saved[min(u + LAG, steps - 1)])
        x, q, attended, hidden, *rest = [pick(early, late) for early, late in both]
        kv_pieces, n2_pieces = rest[:fsdp], rest[fsdp:]
        g_pieces = gather_pieces(gy, "fsdp")
        parts = mlp_back(n2_pieces, g_pieces, gate, up, down)
        terms = reduce_pieces(list(parts), "fsdp")
        gh, gh_low, dq, grad_mlp_gain, *dkv = attend_back(
            gy, hidden, mlp_full, out_full, q, mask, cos, sin, kv_pieces, terms, reps
        )
        dkv_ctx = add_low(reduce_pieces(dkv, "fsdp"))
        size = reps * tokens
        dkv_terms = [
            dkv_ctx[a * size : (a + 1) * size]
            if a == 0
            else exchange(dkv_ctx[a * size : (a + 1) * size], "ctx", a)
            for a in range(ctx)
        ]
        g_in, g_proj, normed, grad_bias, grad_attn_gain = project_back(
            dq, x, gh, attn_full, qkv_full, cos, sin, dkv_terms, reps
        )
        grads_in.append(g_in)
        if u < chunks:
            grads_moved.append(passed_along(g_in, "section", -1))
        smalls.append(jnp.concatenate([grad_attn_gain, grad_bias, grad_mlp_gain], axis=1))
        factors.append((normed, g_proj, attended, gh_low))

    g_own = jnp.concatenate([pick(gys[m + LAG], gys[m]) for m in range(chunks)], axis=0)
    g_all = lax.all_gather(g_own, ("ctx", "fsdp"), axis=0, tiled=True)
    grad_gate, grad_up, grad_down = weight_grads(n2_all, g_all, gate, up, down, 4)

    normed_all, proj_all, attended_all, gh_all = (
        jnp.concatenate([pick(factors[m + LAG][k], factors[m][k]) for m in range(chunks)], axis=0)
        for k in range(4)
    )

    def own_shard(whole):
        shard = lax.psum_scatter(whole.astype(bf16), "fsdp", scatter_dimension=0, tiled=True)
        return lax.psum(shard, "ctx").astype(f32)

    grad_qkv = own_shard(dot_tn(normed_all, proj_all))
    grad_out = own_shard(dot_tn(attended_all, gh_all))

    small = lax.psum(functools.reduce(jnp.add, smalls)[0], ("ctx", "fsdp"))

    def cut(start, length):
        part = length // fsdp
        return lax.dynamic_slice(small, (start + fsdp_at * part,), (part,))

    lead = QCOLS + KCOLS
    columns = QCOLS + 2 * KCOLS
    grad_attn_gain = cut(0, width)
    grad_bias_lead = cut(width, lead)
    grad_bias_value = cut(width + lead, columns - lead)
    grad_mlp_gain = cut(width + columns, width)

    def restore(parts):
        return jnp.stack(parts).reshape(inputs.shape)

    layer_outputs = restore([pick(outputs[m], outputs[m + LAG]) for m in range(chunks)])
    input_grads = restore([pick(grads_in[m + LAG], grads_in[m]) for m in range(chunks)])
    return (
        layer_outputs[None],
        input_grads[None],
        grad_attn_gain[None],
        grad_qkv[None],
        grad_bias_lead[None],
        grad_bias_value[None],
        grad_out[None],
        grad_mlp_gain[None],
        grad_gate[None],
        grad_up[None],
        grad_down[None],
    )


def solution(mesh):
    rows = P(None, ("ctx", "fsdp"), None, None)
    vector = P("section", "fsdp")
    matrix = P("section", "fsdp", None)
    stacked = P("section", None, ("ctx", "fsdp"), None, None)
    in_specs = (rows, rows, vector, matrix, vector, matrix, vector, matrix, matrix, matrix)
    out_specs = (
        stacked,
        stacked,
        vector,
        matrix,
        vector,
        vector,
        matrix,
        vector,
        matrix,
        matrix,
        matrix,
    )
    return jax.shard_map(body, mesh=mesh, in_specs=in_specs, out_specs=out_specs, check_vma=False)
```

time: 3590 us -> 1290 us (0.36)
  waiting for transfers between devices: 2230 us -> 481 us
  matrix products: 635 us -> 8.15 us
  Pallas kernels: 0 us -> 454 us
  blocking collectives: 442 us -> 79.9 us
  starting transfers between devices: 18.8 us -> 130 us
  local copies, waits for them, and re-layouts: 134 us -> 60.3 us
  other arithmetic: 103 us -> 51 us
    psum x1, waiting for transfers between devices: 724 us -> 1.4 us  [own_shard(): return lax.psum(shard, 'ctx').astype(f32)]
    dot_general x90 -> x2, matrix products: 635 us -> 8.15 us  [dot_tn(): lax.dot_general(a, b, (((0,), (0,)), ((), ())), preferred_element_type=f32)]
    reduce_scatter x5 -> x2, waiting for transfers between devices: 620 us -> 73.8 us  [own_shard(): lax.psum_scatter(whole.astype(bf16), 'fsdp', scatter_dimension=0, tiled=T...]
    pallas_call x0 -> x40, Pallas kernels: none -> 454 us  [call(): pl.pallas_call(kernel, out_shape=out_shape, compiler_params=pltpu.Compile...]
    all_gather x23 -> x3, blocking collectives: 419 us -> 16.7 us  [gathered(): return lax.all_gather(shard, 'fsdp', axis=0, tiled=True)]
    unnamed x21 -> x7, waiting for transfers between devices: 363 us -> 1.46 us
    all_gather x5 -> x4, waiting for transfers between devices: 493 us -> 244 us  [the longest x1 102 us: body(): g_all = lax.all_gather(g_own, ('ctx', 'fsdp'), axis=0, tiled=True)]
    ppermute x0 -> x144, waiting for transfers between devices: none -> 145 us  [exchange(): return lax.ppermute(block, axis, [(i, i ^ mask) for i in range(size)])]
  transfers between devices with their start and end apart: 24 -> 159, of which waited for: 19 -> 57; matrix products, arithmetic and copies ran while one was open for 8% -> 5% of each run, Pallas kernels for 0% -> 17%
where the time goes in v1:
time: 1290 us; the launch traced here: 1280 us
  waiting for transfers between devices  481 us (37%)
  Pallas kernels  454 us (35%)
  starting transfers between devices  130 us (10%)
  blocking collectives  79.9 us (6%)
  local copies, waits for them, and re-layouts  60.3 us (5%)
  other arithmetic  51 us (4%)
  between operations  18.3 us (1%)
    pallas_call x40, Pallas kernels, call(): pl.pallas_call(kernel, out_shape=out_shape, compiler_params=pltpu.Compile...  454 us
    ppermute x144, waiting for transfers between devices, exchange(): return lax.ppermute(block, axis, [(i, i ^ mask) for i in range(size)])  145 us
    ppermute x144, starting transfers between devices, exchange(): return lax.ppermute(block, axis, [(i, i ^ mask) for i in range(size)])  108 us
    all_gather x1, waiting for transfers between devices, body(): g_all = lax.all_gather(g_own, ('ctx', 'fsdp'), axis=0, tiled=True)  102 us
    all_gather x1, waiting for transfers between devices, body(): n2_all = lax.all_gather(n2_own, ('ctx', 'fsdp'), axis=0, tiled=True)  97.4 us
    reduce_scatter x2, waiting for transfers between devices, own_shard(): lax.psum_scatter(whole.astype(bf16), 'fsdp', scatter_dimension=0, tiled=T...  73.8 us
    psum x1, blocking collectives, body(): small = lax.psum(functools.reduce(jnp.add, smalls)[0], ('ctx', 'fsdp'))  63.2 us
    unnamed x546, local copies, waits for them, and re-layouts  45.8 us
  transfers between devices with their start and end apart: 159, of which 57 were waited for; matrix products, arithmetic and copies ran while one was open for 5% of the time, Pallas kernels for 17%

profile of v1, /device:TPU:0, one launch (start us, length us, event | category | flops | bytes accessed | tf_op | source)
XLA Modules:
  0.0 1282.4 jit_solution(7790885546345280095)
XLA Ops:
  12.0 6.1 all-gather.gain_ref.refs_3_
  18.1 5.4 all-gather.2.b_ref
  24.2 34.5 %all-gather.14.cloned.1.call-done = bf16[1,1536,2048]{2,1,0:T(8,128)(2,1)} async-done(((bf16[1,384,2048]{2,1,0:T(8,128)(2,1)}), bf16[1,1536,2048]{2,1,0:T(8,128)(2,1)}) %all-gather.14.cloned.1.call-update) | async-done | bytes 6291472 | tf_op jit(solution)/shard_map/all_gather | solution.py:624
  76.2 11.9 collective-permute-done.28.refs_6_
  88.1 5.2 all-gather.4.refs_4_.refs_2_
  93.4 10.1 all-gather.16.cloned.1.call-done
  108.8 6.7 collective-permute-done.31.refs_1_
  120.0 10.0 mlp.8
  168.9 5.8 collective-permute-done.41.refs_6_
  189.4 10.1 mlp.6
  200.2 10.1 mlp.9
  213.1 5.6 collective-permute-done.11
  219.5 5.1 collective-permute-start.12
  247.5 6.0 collective-permute-done.16.refs_6_
  271.2 10.1 mlp.7
  285.1 7.0 collective-permute-done.67.refs_6_
  312.0 4.4 attend.11
  366.8 13.9 %mlp_back.6 = (bf16[64,1536]{1,0:T(8,128)(2,1)S(1)}, bf16[64,1536]{1,0:T(8,128)(2,1)S(1)}, bf16[64,1536]{1,0:T(8,128)(2,1)S(1)}, bf16[64,1536]{1,0:T(8,128)(2,1)S(1)}) custom-call(bf16[64,1536]{1,0:T(8,128)(2,1)S(1)} %get-tuple-element.446.refs_0_, bf16[64,1536]{1,0:T(8,128)(2,1)S(1)} %get-tuple-element.475.refs_1_, ...), custom_call_target="tpu_custom_call" | custom-call | flops 8808038400 | bytes 20643840 | tf_op jit(solution)/shard_map/mlp_back/pallas_call | solution.py:107
  381.0 14.4 %mlp_back.8 = (bf16[64,1536]{1,0:T(8,128)(2,1)S(1)}, bf16[64,1536]{1,0:T(8,128)(2,1)S(1)}, bf16[64,1536]{1,0:T(8,128)(2,1)S(1)}, bf16[64,1536]{1,0:T(8,128)(2,1)S(1)}) custom-call(bf16[64,1536]{1,0:T(8,128)(2,1)S(1)} %get-tuple-element.447.refs_0_, bf16[64,1536]{1,0:T(8,128)(2,1)S(1)} %get-tuple-element.474.refs_1_, ...), custom_call_target="tpu_custom_call" | custom-call | flops 8808038400 | bytes 20643840 | tf_op jit(solution)/shard_map/mlp_back/pallas_call | solution.py:107
  398.7 5.4 collective-permute-done.81.refs_14_
  404.9 8.8 attend_back.6
  413.8 8.9 attend_back.8
  427.8 5.7 collective-permute-done.84
  480.5 13.9 %mlp_back.7 = (bf16[64,1536]{1,0:T(8,128)(2,1)S(1)}, bf16[64,1536]{1,0:T(8,128)(2,1)S(1)}, bf16[64,1536]{1,0:T(8,128)(2,1)S(1)}, bf16[64,1536]{1,0:T(8,128)(2,1)S(1)}) custom-call(bf16[64,1536]{1,0:T(8,128)(2,1)S(1)} %copy-done.174, bf16[64,1536]{1,0:T(8,128)(2,1)S(1)} %copy-done.181, bf16[64,1536]{1,0:T(8,128)(2,1)S(1)} %copy-done.182, ...), custom_call_target="tpu_custom_call" | custom-call | flops 8808038400 | bytes 20643840 | tf_op jit(solution)/shard_map/mlp_back/pallas_call | solution.py:107
  495.1 13.8 %mlp_back.9 = (bf16[64,1536]{1,0:T(8,128)(2,1)S(1)}, bf16[64,1536]{1,0:T(8,128)(2,1)S(1)}, bf16[64,1536]{1,0:T(8,128)(2,1)S(1)}, bf16[64,1536]{1,0:T(8,128)(2,1)S(1)}) custom-call(bf16[64,1536]{1,0:T(8,128)(2,1)S(1)} %copy-done.173, bf16[64,1536]{1,0:T(8,128)(2,1)S(1)} %copy-done.177, bf16[64,1536]{1,0:T(8,128)(2,1)S(1)} %copy-done.180, ...), custom_call_target="tpu_custom_call" | custom-call | flops 8808038400 | bytes 20643840 | tf_op jit(solution)/shard_map/mlp_back/pallas_call | solution.py:107
  512.4 5.0 collective-permute-done.94.refs_14_
  518.1 8.8 attend_back.7
  527.8 9.0 attend_back.9
  541.8 5.8 collective-permute-done.97
  579.5 13.9 %mlp_back.10 = (bf16[64,1536]{1,0:T(8,128)(2,1)S(1)}, bf16[64,1536]{1,0:T(8,128)(2,1)S(1)}, bf16[64,1536]{1,0:T(8,128)(2,1)S(1)}, bf16[64,1536]{1,0:T(8,128)(2,1)S(1)}) custom-call(bf16[64,1536]{1,0:T(8,128)(2,1)S(1)} %copy-done.156, bf16[64,1536]{1,0:T(8,128)(2,1)S(1)} %copy-done.163, bf16[64,1536]{1,0:T(8,128)(2,1)S(1)} %copy-done.166, ...), custom_call_target="tpu_custom_call" | custom-call | flops 8808038400 | bytes 20643840 | tf_op jit(solution)/shard_map/mlp_back/pallas_call | solution.py:107
  594.1 14.0 %mlp_back.11 = (bf16[64,1536]{1,0:T(8,128)(2,1)S(1)}, bf16[64,1536]{1,0:T(8,128)(2,1)S(1)}, bf16[64,1536]{1,0:T(8,128)(2,1)S(1)}, bf16[64,1536]{1,0:T(8,128)(2,1)S(1)}) custom-call(bf16[64,1536]{1,0:T(8,128)(2,1)S(1)} %copy-done.113, bf16[64,1536]{1,0:T(8,128)(2,1)S(1)} %copy-done.161, bf16[64,1536]{1,0:T(8,128)(2,1)S(1)} %copy-done.162, ...), custom_call_target="tpu_custom_call" | custom-call | flops 8808038400 | bytes 20643840 | tf_op jit(solution)/shard_map/mlp_back/pallas_call | solution.py:107
  611.6 5.0 collective-permute-done.132.refs_14_
  617.3 8.9 attend_back.10
  627.9 8.8 attend_back.11
  646.2 7.0 collective-permute-done.135
  671.1 4.5 convolution_convert_fusion
  675.8 12.2 reduce-scatter.5.cloned.1.call-done
  688.0 61.5 %reduce-scatter.3.cloned.1.call-done = bf16[384,2048]{1,0:T(8,128)(2,1)} async-done(((bf16[1536,2048]{1,0:T(8,128)(2,1)}), bf16[384,2048]{1,0:T(8,128)(2,1)}) %reduce-scatter.3.cloned.1.call-update) | async-done | bytes 1572880 | tf_op jit(solution)/shard_map/reduce_scatter | solution.py:711
  754.8 10.1 mlp.11
  765.5 10.1 mlp.10
  778.7 4.9 collective-permute-done.75
  791.6 63.2 %psum.21 = f32[5120]{0:T(1024)S(1)} all-reduce(f32[5120]{0:T(1024)S(1)} %fusion.33), channel_id=1, replica_groups=mesh['section'=2,'ctx'=4,'fsdp'=4] {'ctx','fsdp'}, use_global_device_ids=true, to_apply=%region_0.1 | all-reduce | flops 5120 | bytes 40960 | tf_op jit(solution)/shard_map/psum | solution.py:717
  866.1 97.4 %all-gather.10.cloned.1.call-done.refs_0_ = bf16[4096,1536]{1,0:T(8,128)(2,1)} async-done(((bf16[256,1536]{1,0:T(8,128)(2,1)}), bf16[4096,1536]{1,0:T(8,128)(2,1)}) %all-gather.10.cloned.1.call-update) | async-done | bytes 12582928 | tf_op jit(solution)/shard_map/all_gather | solution.py:664
  963.5 101.8 %all-gather.12.cloned.1.call-done.refs_1_ = bf16[4096,1536]{1,0:T(8,128)(2,1)} async-done(((bf16[256,1536]{1,0:T(8,128)(2,1)}), bf16[4096,1536]{1,0:T(8,128)(2,1)}) %all-gather.12.cloned.1.call-update) | async-done | bytes 12582928 | tf_op jit(solution)/shard_map/all_gather | solution.py:702
  1065.4 59.5 %weight_grads.4 = (f32[2240,1536]{1,0:T(8,128)}, f32[2240,1536]{1,0:T(8,128)}, f32[2240,1536]{1,0:T(8,128)}) custom-call(bf16[4096,1536]{1,0:T(8,128)(2,1)} %all-gather.10.cloned.1.call-done.refs_0_, bf16[4096,1536]{1,0:T(8,128)(2,1)} %all-gather.12.cloned.1.call-done.refs_1_, bf16[2240,1536]{1,0:T(8,128)(2,1)} %bitcast.41, bf16[2240,1536]{1,0:T(8,128)(2,1)} %bitcast.97, ...), custom_call_target="tpu_custom_call" | custom-call | flops 48318382080 | bytes 17694720 | tf_op jit(solution)/shard_map/weight_grads/pallas_call | solution.py:107
  1124.8 59.4 %weight_grads.5 = (f32[2240,1536]{1,0:T(8,128)}, f32[2240,1536]{1,0:T(8,128)}, f32[2240,1536]{1,0:T(8,128)}) custom-call(bf16[4096,1536]{1,0:T(8,128)(2,1)} %all-gather.10.cloned.1.call-done.refs_0_, bf16[4096,1536]{1,0:T(8,128)(2,1)} %all-gather.12.cloned.1.call-done.refs_1_, ...), custom_call_target="tpu_custom_call", output_to_operand_aliasing={{0}: (5, {}), {1}: (6, {}), {2}: (7, {})} | custom-call | flops 48318382080 | bytes 17694720 | tf_op jit(solution)/shard_map/weight_grads/pallas_call | solution.py:107
  1184.3 59.6 %weight_grads.6 = (f32[2240,1536]{1,0:T(8,128)}, f32[2240,1536]{1,0:T(8,128)}, f32[2240,1536]{1,0:T(8,128)}) custom-call(bf16[4096,1536]{1,0:T(8,128)(2,1)} %all-gather.10.cloned.1.call-done.refs_0_, bf16[4096,1536]{1,0:T(8,128)(2,1)} %all-gather.12.cloned.1.call-done.refs_1_, ...), custom_call_target="tpu_custom_call", output_to_operand_aliasing={{0}: (5, {}), {1}: (6, {}), {2}: (7, {})} | custom-call | flops 48318382080 | bytes 17694720 | tf_op jit(solution)/shard_map/weight_grads/pallas_call | solution.py:107
  1243.9 31.5 %weight_grads.7 = (f32[2240,1536]{1,0:T(8,128)}, f32[2240,1536]{1,0:T(8,128)}, f32[2240,1536]{1,0:T(8,128)}) custom-call(bf16[4096,1536]{1,0:T(8,128)(2,1)} %all-gather.10.cloned.1.call-done.refs_0_, bf16[4096,1536]{1,0:T(8,128)(2,1)} %all-gather.12.cloned.1.call-done.refs_1_, ...), custom_call_target="tpu_custom_call", output_to_operand_aliasing={{0}: (5, {}), {1}: (6, {}), {2}: (7, {})} | custom-call | flops 24159191040 | bytes 8847360 | tf_op jit(solution)/shard_map/weight_grads/pallas_call | solution.py:107
  (1063 shorter events, 363.2 us)
Async XLA Ops:
  7.2 51.5 %all-gather.14.cloned.1.call-start = ((), (), s32[]{:S(2)}) async-start(), calls=%async_computation.6 | async-start | bytes 7864320 | tf_op jit(solution)/shard_map/all_gather | solution.py:624
  7.9 95.5 %all-gather.16.cloned.1.call-start = ((), (), s32[]{:S(2)}) async-start(), calls=%async_computation.7 | async-start | bytes 5898240 | tf_op jit(solution)/shard_map/all_gather | solution.py:624
  8.7 679.3 %reduce-scatter.5.cloned.1.call-start = ((), (), s32[]{:S(2)}) async-start(), calls=%async_computation.3 | async-start | bytes 5898240 | tf_op jit(solution)/shard_map/reduce_scatter | solution.py:711
  73.7 14.4 %collective-permute-start.28 = (bf16[256,512]{1,0:T(8,128)(2,1)S(1)}, bf16[256,512]{1,0:T(8,128)(2,1)S(1)}, u32[]{:S(2)}, u32[]{:S(2)}) collective-permute-start(bf16[256,512]{1,0:T(8,128)(2,1)S(1)} %constant_dynamic-update-slice_fusion.8.refs_5_), channel_id=1, source_target_pairs={{0,2},{1,3},{2,0},{3,1},{4,6},{5,7},{6,4},{7,5},{8,10},{9,11},{10,... | collective-permute-start | bytes 786440 | tf_op jit(solution)/shard_map/ppermute | solution.py:63
  76.1 27.3 %collective-permute-start.29 = (bf16[256,512]{1,0:T(8,128)(2,1)S(1)}, bf16[256,512]{1,0:T(8,128)(2,1)S(1)}, u32[]{:S(2)}, u32[]{:S(2)}) collective-permute-start(bf16[256,512]{1,0:T(8,128)(2,1)S(1)} %constant_dynamic-update-slice_fusion.8.refs_5_), channel_id=1, source_target_pairs={{0,1},{1,0},{2,3},{3,2},{4,5},{5,4},{6,7},{7,6},{8,9},{9,8},{10,11... | collective-permute-start | bytes 786440 | tf_op jit(solution)/shard_map/ppermute | solution.py:63
  88.1 15.4 %collective-permute-start.30 = (bf16[256,512]{1,0:T(8,128)(2,1)S(1)}, bf16[256,512]{1,0:T(8,128)(2,1)S(1)}, u32[]{:S(2)}, u32[]{:S(2)}) collective-permute-start(bf16[256,512]{1,0:T(8,128)(2,1)S(1)} %collective-permute-done.28.refs_6_), channel_id=1, source_target_pairs={{0,1},{1,0},{2,3},{3,2},{4,5},{5,4},{6,7},{7,6},{8,9},{9,8},{10,11... | collective-permute-start | bytes 786440 | tf_op jit(solution)/shard_map/ppermute | solution.py:63
  136.0 16.0 %collective-permute-start.2 = (bf16[64,512]{1,0:T(8,128)(2,1)S(1)}, bf16[64,512]{1,0:T(8,128)(2,1)S(1)}, u32[]{:S(2)}, u32[]{:S(2)}) collective-permute-start(bf16[64,512]{1,0:T(8,128)(2,1)S(1)} %get-tuple-element.180), channel_id=1, source_target_pairs={{0,12},{4,8},{8,4},{12,0},{1,13},{5,9},{9,5},{13,1},{2,14},{6,10},... | collective-permute-start | bytes 196616 | tf_op jit(solution)/shard_map/ppermute | solution.py:63
  139.4 12.6 collective-permute-start.1
  152.1 16.2 %collective-permute-start.3 = (bf16[256,512]{1,0:T(8,128)(2,1)S(1)}, bf16[256,512]{1,0:T(8,128)(2,1)S(1)}, u32[]{:S(2)}, u32[]{:S(2)}) collective-permute-start(bf16[256,512]{1,0:T(8,128)(2,1)S(1)} %constant_dynamic-update-slice_fusion.refs_5_), channel_id=1, source_target_pairs={{0,2},{1,3},{2,0},{3,1},{4,6},{5,7},{6,4},{7,5},{8,10},{9,11},{10,... | collective-permute-start | bytes 786440 | tf_op jit(solution)/shard_map/ppermute | solution.py:63
  185.5 14.7 %collective-permute-start.45 = (bf16[64,1536]{1,0:T(8,128)(2,1)S(1)}, bf16[64,1536]{1,0:T(8,128)(2,1)S(1)}, u32[]{:S(2)}, u32[]{:S(2)}) collective-permute-start(bf16[64,1536]{1,0:T(8,128)(2,1)S(1)} %get-tuple-element.206.refs_0_), channel_id=1, source_target_pairs={{0,1},{1,0},{2,3},{3,2},{4,5},{5,4},{6,7},{7,6},{8,9},{9,8},{10,11... | collective-permute-start | bytes 589832 | tf_op jit(solution)/shard_map/ppermute | solution.py:63
  199.6 13.6 %collective-permute-start.9 = (bf16[64,1536]{1,0:T(8,128)(2,1)S(1)}, bf16[64,1536]{1,0:T(8,128)(2,1)S(1)}, u32[]{:S(2)}, u32[]{:S(2)}) collective-permute-start(bf16[64,1536]{1,0:T(8,128)(2,1)S(1)} %get-tuple-element.184), channel_id=1, source_target_pairs={{0,1},{1,0},{2,3},{3,2},{4,5},{5,4},{6,7},{7,6},{8,9},{9,8},{10,11... | collective-permute-start | bytes 589832 | tf_op jit(solution)/shard_map/ppermute | solution.py:63
  211.6 12.9 %collective-permute-start.47 = (bf16[64,1536]{1,0:T(8,128)(2,1)S(1)}, bf16[64,1536]{1,0:T(8,128)(2,1)S(1)}, u32[]{:S(2)}, u32[]{:S(2)}) collective-permute-start(bf16[64,1536]{1,0:T(8,128)(2,1)S(1)} %get-tuple-element.208), channel_id=1, source_target_pairs={{0,1},{1,0},{2,3},{3,2},{4,5},{5,4},{6,7},{7,6},{8,9},{9,8},{10,11... | collective-permute-start | bytes 589832 | tf_op jit(solution)/shard_map/ppermute | solution.py:63
  212.0 12.6 collective-permute-start.49
  263.3 18.8 %collective-permute-start.66 = (bf16[64,512]{1,0:T(8,128)(2,1)S(1)}, bf16[64,512]{1,0:T(8,128)(2,1)S(1)}, u32[]{:S(2)}, u32[]{:S(2)}) collective-permute-start(bf16[64,512]{1,0:T(8,128)(2,1)S(1)} %get-tuple-element.220), channel_id=1, source_target_pairs={{0,12},{4,8},{8,4},{12,0},{1,13},{5,9},{9,5},{13,1},{2,14},{6,10},... | collective-permute-start | bytes 196616 | tf_op jit(solution)/shard_map/ppermute | solution.py:63
  266.1 15.3 %collective-permute-start.65 = (bf16[64,512]{1,0:T(8,128)(2,1)S(1)}, bf16[64,512]{1,0:T(8,128)(2,1)S(1)}, u32[]{:S(2)}, u32[]{:S(2)}) collective-permute-start(bf16[64,512]{1,0:T(8,128)(2,1)S(1)} %get-tuple-element.220), channel_id=1, source_target_pairs={{0,8},{4,12},{8,0},{12,4},{1,9},{5,13},{9,1},{13,5},{2,10},{6,14},... | collective-permute-start | bytes 196616 | tf_op jit(solution)/shard_map/ppermute | solution.py:63
  285.1 23.0 %collective-permute-start.68 = (bf16[256,512]{1,0:T(8,128)(2,1)}, bf16[256,512]{1,0:T(8,128)(2,1)}, u32[]{:S(2)}, u32[]{:S(2)}) collective-permute-start(bf16[256,512]{1,0:T(8,128)(2,1)} %constant_dynamic-update-slice_fusion.20.refs_5_), channel_id=1, source_target_pairs={{0,1},{1,0},{2,3},{3,2},{4,5},{5,4},{6,7},{7,6},{8,9},{9,8},{10,11... | collective-permute-start | bytes 786440 | tf_op jit(solution)/shard_map/ppermute | solution.py:63
  292.2 16.6 %collective-permute-start.69 = (bf16[256,512]{1,0:T(8,128)(2,1)}, bf16[256,512]{1,0:T(8,128)(2,1)}, u32[]{:S(2)}, u32[]{:S(2)}) collective-permute-start(bf16[256,512]{1,0:T(8,128)(2,1)} %collective-permute-done.67.refs_6_), channel_id=1, source_target_pairs={{0,1},{1,0},{2,3},{3,2},{4,5},{5,4},{6,7},{7,6},{8,9},{9,8},{10,11... | collective-permute-start | bytes 786440 | tf_op jit(solution)/shard_map/ppermute | solution.py:63
  297.7 20.1 %collective-permute-start.50 = (bf16[64,1536]{1,0:T(8,128)(2,1)}, bf16[64,1536]{1,0:T(8,128)(2,1)}, u32[]{:S(2)}, u32[]{:S(2)}) collective-permute-start(bf16[64,1536]{1,0:T(8,128)(2,1)} %get-tuple-element.361), channel_id=1, source_target_pairs={{0,16},{1,17},{2,18},{3,19},{4,20},{5,21},{6,22},{7,23},{8,24},{9,... | collective-permute-start | bytes 589832 | tf_op jit(solution)/shard_map/ppermute | solution.py:69
  305.0 76.0 %collective-permute-start.102 = (bf16[64,1536]{1,0:T(8,128)(2,1)}, bf16[64,1536]{1,0:T(8,128)(2,1)}, u32[]{:S(2)}, u32[]{:S(2)}) collective-permute-start(bf16[64,1536]{1,0:T(8,128)(2,1)} %select_n.903.refs_4_.refs_0_), channel_id=1, source_target_pairs={{0,1},{1,0},{2,3},{3,2},{4,5},{5,4},{6,7},{7,6},{8,9},{9,8},{10,11... | collective-permute-start | bytes 589832 | tf_op jit(solution)/shard_map/ppermute | solution.py:63
  305.0 59.4 %collective-permute-start.101 = (bf16[64,1536]{1,0:T(8,128)(2,1)}, bf16[64,1536]{1,0:T(8,128)(2,1)}, u32[]{:S(2)}, u32[]{:S(2)}) collective-permute-start(bf16[64,1536]{1,0:T(8,128)(2,1)} %select_n.903.refs_4_.refs_0_), channel_id=1, source_target_pairs={{0,2},{1,3},{2,0},{3,1},{4,6},{5,7},{6,4},{7,5},{8,10},{9,11},{10,... | collective-permute-start | bytes 589832 | tf_op jit(solution)/shard_map/ppermute | solution.py:63
  308.1 56.6 %collective-permute-start.76 = (bf16[64,1536]{1,0:T(8,128)(2,1)}, bf16[64,1536]{1,0:T(8,128)(2,1)}, u32[]{:S(2)}, u32[]{:S(2)}) collective-permute-start(bf16[64,1536]{1,0:T(8,128)(2,1)} %select_n.876.refs_4_.refs_0_), channel_id=1, source_target_pairs={{0,2},{1,3},{2,0},{3,1},{4,6},{5,7},{6,4},{7,5},{8,10},{9,11},{10,... | collective-permute-start | bytes 589832 | tf_op jit(solution)/shard_map/ppermute | solution.py:63
  316.4 44.0 %collective-permute-start.70 = (bf16[64,1536]{1,0:T(8,128)(2,1)}, bf16[64,1536]{1,0:T(8,128)(2,1)}, u32[]{:S(2)}, u32[]{:S(2)}) collective-permute-start(bf16[64,1536]{1,0:T(8,128)(2,1)} %get-tuple-element.222.refs_0_), channel_id=1, source_target_pairs={{0,2},{1,3},{2,0},{3,1},{4,6},{5,7},{6,4},{7,5},{8,10},{9,11},{10,... | collective-permute-start | bytes 589832 | tf_op jit(solution)/shard_map/ppermute | solution.py:63
  364.6 16.4 %collective-permute-start.103 = (bf16[64,1536]{1,0:T(8,128)(2,1)}, bf16[64,1536]{1,0:T(8,128)(2,1)S(1)}, u32[]{:S(2)}, u32[]{:S(2)}) collective-permute-start(bf16[64,1536]{1,0:T(8,128)(2,1)} %collective-permute-done.101.refs_5_), channel_id=1, source_target_pairs={{0,1},{1,0},{2,3},{3,2},{4,5},{5,4},{6,7},{7,6},{8,9},{9,8},{10,11... | collective-permute-start | bytes 589832 | tf_op jit(solution)/shard_map/ppermute | solution.py:63
  380.7 15.6 %collective-permute-start.80 = (bf16[64,1536]{1,0:T(8,128)(2,1)S(1)}, bf16[64,1536]{1,0:T(8,128)(2,1)S(1)}, u32[]{:S(2)}, u32[]{:S(2)}) collective-permute-start(bf16[64,1536]{1,0:T(8,128)(2,1)S(1)} %get-tuple-element.230), channel_id=1, source_target_pairs={{0,1},{1,0},{2,3},{3,2},{4,5},{5,4},{6,7},{7,6},{8,9},{9,8},{10,11... | collective-permute-start | bytes 589832 | tf_op jit(solution)/shard_map/ppermute | solution.py:63
  395.5 18.3 %collective-permute-start.104 = (bf16[64,1536]{1,0:T(8,128)(2,1)S(1)}, bf16[64,1536]{1,0:T(8,128)(2,1)}, u32[]{:S(2)}, u32[]{:S(2)}) collective-permute-start(bf16[64,1536]{1,0:T(8,128)(2,1)S(1)} %get-tuple-element.250), channel_id=1, source_target_pairs={{0,1},{1,0},{2,3},{3,2},{4,5},{5,4},{6,7},{7,6},{8,9},{9,8},{10,11... | collective-permute-start | bytes 589832 | tf_op jit(solution)/shard_map/ppermute | solution.py:63
  397.8 15.9 %collective-permute-start.106 = (bf16[64,1536]{1,0:T(8,128)(2,1)S(1)}, bf16[64,1536]{1,0:T(8,128)(2,1)}, u32[]{:S(2)}, u32[]{:S(2)}) collective-permute-start(bf16[64,1536]{1,0:T(8,128)(2,1)S(1)} %add_convert_fusion.15), channel_id=1, source_target_pairs={{0,2},{1,3},{2,0},{3,1},{4,6},{5,7},{6,4},{7,5},{8,10},{9,11},{10,... | collective-permute-start | bytes 589832 | tf_op jit(solution)/shard_map/ppermute | solution.py:63
  425.8 12.4 collective-permute-start.107
  447.0 17.8 %collective-permute-start.88 = (bf16[64,1536]{1,0:T(8,128)(2,1)}, bf16[64,1536]{1,0:T(8,128)(2,1)S(1)}, u32[]{:S(2)}, u32[]{:S(2)}) collective-permute-start(bf16[64,1536]{1,0:T(8,128)(2,1)} %get-tuple-element.237), channel_id=1, source_target_pairs={{16,0},{17,1},{18,2},{19,3},{20,4},{21,5},{22,6},{23,7},{24,8},{25... | collective-permute-start | bytes 589832 | tf_op jit(solution)/shard_map/ppermute | solution.py:69
  473.6 21.4 %collective-permute-start.115 = (bf16[64,1536]{1,0:T(8,128)(2,1)S(1)}, bf16[64,1536]{1,0:T(8,128)(2,1)S(1)}, u32[]{:S(2)}, u32[]{:S(2)}) collective-permute-start(bf16[64,1536]{1,0:T(8,128)(2,1)S(1)} %get-tuple-element.352.refs_4_.refs_0_), channel_id=1, source_target_pairs={{0,1},{1,0},{2,3},{3,2},{4,5},{5,4},{6,7},{7,6},{8,9},{9,8},{10,11... | collective-permute-start | bytes 589832 | tf_op jit(solution)/shard_map/ppermute | solution.py:63
  477.5 17.6 %collective-permute-start.116 = (bf16[64,1536]{1,0:T(8,128)(2,1)S(1)}, bf16[64,1536]{1,0:T(8,128)(2,1)S(1)}, u32[]{:S(2)}, u32[]{:S(2)}) collective-permute-start(bf16[64,1536]{1,0:T(8,128)(2,1)S(1)} %collective-permute-done.114.refs_5_), channel_id=1, source_target_pairs={{0,1},{1,0},{2,3},{3,2},{4,5},{5,4},{6,7},{7,6},{8,9},{9,8},{10,11... | collective-permute-start | bytes 589832 | tf_op jit(solution)/shard_map/ppermute | solution.py:63
  494.4 18.0 %collective-permute-start.92 = (bf16[64,1536]{1,0:T(8,128)(2,1)S(1)}, bf16[64,1536]{1,0:T(8,128)(2,1)S(1)}, u32[]{:S(2)}, u32[]{:S(2)}) collective-permute-start(bf16[64,1536]{1,0:T(8,128)(2,1)S(1)} %get-tuple-element.239), channel_id=1, source_target_pairs={{0,1},{1,0},{2,3},{3,2},{4,5},{5,4},{6,7},{7,6},{8,9},{9,8},{10,11... | collective-permute-start | bytes 589832 | tf_op jit(solution)/shard_map/ppermute | solution.py:63
  495.0 14.6 %collective-permute-start.93 = (bf16[64,1536]{1,0:T(8,128)(2,1)S(1)}, bf16[64,1536]{1,0:T(8,128)(2,1)S(1)}, u32[]{:S(2)}, u32[]{:S(2)}) collective-permute-start(bf16[64,1536]{1,0:T(8,128)(2,1)S(1)} %get-tuple-element.241), channel_id=1, source_target_pairs={{0,1},{1,0},{2,3},{3,2},{4,5},{5,4},{6,7},{7,6},{8,9},{9,8},{10,11... | collective-permute-start | bytes 589832 | tf_op jit(solution)/shard_map/ppermute | solution.py:63
  509.0 18.0 %collective-permute-start.117 = (bf16[64,1536]{1,0:T(8,128)(2,1)S(1)}, bf16[64,1536]{1,0:T(8,128)(2,1)S(1)}, u32[]{:S(2)}, u32[]{:S(2)}) collective-permute-start(bf16[64,1536]{1,0:T(8,128)(2,1)S(1)} %get-tuple-element.261), channel_id=1, source_target_pairs={{0,1},{1,0},{2,3},{3,2},{4,5},{5,4},{6,7},{7,6},{8,9},{9,8},{10,11... | collective-permute-start | bytes 589832 | tf_op jit(solution)/shard_map/ppermute | solution.py:63
  511.1 15.9 %collective-permute-start.119 = (bf16[64,1536]{1,0:T(8,128)(2,1)S(1)}, bf16[64,1536]{1,0:T(8,128)(2,1)S(1)}, u32[]{:S(2)}, u32[]{:S(2)}) collective-permute-start(bf16[64,1536]{1,0:T(8,128)(2,1)S(1)} %add_convert_fusion.14), channel_id=1, source_target_pairs={{0,2},{1,3},{2,0},{3,1},{4,6},{5,7},{6,4},{7,5},{8,10},{9,11},{10,... | collective-permute-start | bytes 589832 | tf_op jit(solution)/shard_map/ppermute | solution.py:63
  539.9 12.4 collective-permute-start.120
  575.8 18.3 %collective-permute-start.141 = (bf16[64,1536]{1,0:T(8,128)(2,1)S(1)}, bf16[64,1536]{1,0:T(8,128)(2,1)S(1)}, u32[]{:S(2)}, u32[]{:S(2)}) collective-permute-start(bf16[64,1536]{1,0:T(8,128)(2,1)S(1)} %get-tuple-element.439.refs_4_.refs_0_), channel_id=1, source_target_pairs={{0,1},{1,0},{2,3},{3,2},{4,5},{5,4},{6,7},{7,6},{8,9},{9,8},{10,11... | collective-permute-start | bytes 589832 | tf_op jit(solution)/shard_map/ppermute | solution.py:63
  579.4 14.7 %collective-permute-start.142 = (bf16[64,1536]{1,0:T(8,128)(2,1)S(1)}, bf16[64,1536]{1,0:T(8,128)(2,1)S(1)}, u32[]{:S(2)}, u32[]{:S(2)}) collective-permute-start(bf16[64,1536]{1,0:T(8,128)(2,1)S(1)} %collective-permute-done.140.refs_5_), channel_id=1, source_target_pairs={{0,1},{1,0},{2,3},{3,2},{4,5},{5,4},{6,7},{7,6},{8,9},{9,8},{10,11... | collective-permute-start | bytes 589832 | tf_op jit(solution)/shard_map/ppermute | solution.py:63
  593.4 18.1 %collective-permute-start.130 = (bf16[64,1536]{1,0:T(8,128)(2,1)S(1)}, bf16[64,1536]{1,0:T(8,128)(2,1)S(1)}, u32[]{:S(2)}, u32[]{:S(2)}) collective-permute-start(bf16[64,1536]{1,0:T(8,128)(2,1)S(1)} %get-tuple-element.272), channel_id=1, source_target_pairs={{0,1},{1,0},{2,3},{3,2},{4,5},{5,4},{6,7},{7,6},{8,9},{9,8},{10,11... | collective-permute-start | bytes 589832 | tf_op jit(solution)/shard_map/ppermute | solution.py:63
  594.0 14.7 %collective-permute-start.131 = (bf16[64,1536]{1,0:T(8,128)(2,1)S(1)}, bf16[64,1536]{1,0:T(8,128)(2,1)S(1)}, u32[]{:S(2)}, u32[]{:S(2)}) collective-permute-start(bf16[64,1536]{1,0:T(8,128)(2,1)S(1)} %get-tuple-element.274), channel_id=1, source_target_pairs={{0,1},{1,0},{2,3},{3,2},{4,5},{5,4},{6,7},{7,6},{8,9},{9,8},{10,11... | collective-permute-start | bytes 589832 | tf_op jit(solution)/shard_map/ppermute | solution.py:63
  608.2 19.0 %collective-permute-start.143 = (bf16[64,1536]{1,0:T(8,128)(2,1)S(1)}, bf16[64,1536]{1,0:T(8,128)(2,1)S(1)}, u32[]{:S(2)}, u32[]{:S(2)}) collective-permute-start(bf16[64,1536]{1,0:T(8,128)(2,1)S(1)} %get-tuple-element.283), channel_id=1, source_target_pairs={{0,1},{1,0},{2,3},{3,2},{4,5},{5,4},{6,7},{7,6},{8,9},{9,8},{10,11... | collective-permute-start | bytes 589832 | tf_op jit(solution)/shard_map/ppermute | solution.py:63
  610.3 16.9 %collective-permute-start.145 = (bf16[64,1536]{1,0:T(8,128)(2,1)S(1)}, bf16[64,1536]{1,0:T(8,128)(2,1)S(1)}, u32[]{:S(2)}, u32[]{:S(2)}) collective-permute-start(bf16[64,1536]{1,0:T(8,128)(2,1)S(1)} %add_convert_fusion.12), channel_id=1, source_target_pairs={{0,2},{1,3},{2,0},{3,1},{4,6},{5,7},{6,4},{7,5},{8,10},{9,11},{10,... | collective-permute-start | bytes 589832 | tf_op jit(solution)/shard_map/ppermute | solution.py:63
  641.4 108.2 %reduce-scatter.3.cloned.1.call-start = ((), (), s32[]{:S(2)}) async-start(), calls=%async_computation.2 | async-start | bytes 7864320 | tf_op jit(solution)/shard_map/reduce_scatter | solution.py:711
  645.3 12.4 collective-permute-start.146
  645.4 12.5 collective-permute-start.148
  675.7 185.2 %all-reduce.3.cloned.1.call-start = ((), (), s32[]{:S(2)}) async-start(), calls=%async_computation.8 | async-start | bytes 5505024 | tf_op jit(solution)/shard_map/psum | solution.py:712
  749.6 213.9 %all-gather.10.cloned.1.call-start = ((), (), s32[]{:S(2)}) async-start(), calls=%async_computation.4 | async-start | bytes 13369344 | tf_op jit(solution)/shard_map/all_gather | solution.py:664
  750.7 314.7 %all-gather.12.cloned.1.call-start = ((), (), s32[]{:S(2)}) async-start(), calls=%async_computation.5 | async-start | bytes 13369344 | tf_op jit(solution)/shard_map/all_gather | solution.py:702
  764.9 13.9 %collective-permute-start.73 = (bf16[64,1536]{1,0:T(8,128)(2,1)S(1)}, bf16[64,1536]{1,0:T(8,128)(2,1)S(1)}, u32[]{:S(2)}, u32[]{:S(2)}) collective-permute-start(bf16[64,1536]{1,0:T(8,128)(2,1)S(1)} %get-tuple-element.224), channel_id=1, source_target_pairs={{0,1},{1,0},{2,3},{3,2},{4,5},{5,4},{6,7},{7,6},{8,9},{9,8},{10,11... | collective-permute-start | bytes 589832 | tf_op jit(solution)/shard_map/ppermute | solution.py:63
  (375 other events, 4364.6 us)
Sparse Core Ops, SparseCore 0:
  9.6 49.0 all-gather.13
  60.3 43.1 all-gather.15
  641.5 46.4 reduce-scatter.4
  691.2 58.3 reduce-scatter.2
  751.9 108.9 all-reduce.2
  863.6 99.8 all-gather.9
  966.4 98.9 all-gather.11

commit v2 on v1

v2 whole, which is shorter than its diff:
```python
import functools
import math

import jax
import jax.numpy as jnp
from jax import lax
from jax.experimental import pallas as pl
from jax.experimental.pallas import tpu as pltpu
from jax.sharding import PartitionSpec as P

HEADS = 12
KV_HEADS = 2
HEAD_DIM = 128
GROUP = HEADS // KV_HEADS
EPS = 1e-06
ROPE_BASE = 1000000.0
NEGATIVE = -1e30
QCOLS = HEADS * HEAD_DIM
KCOLS = KV_HEADS * HEAD_DIM
SCALE = HEAD_DIM ** (-0.5)

MICROS = 1
LAG = 2
UNITS = 512

f32 = jnp.float32
bf16 = jnp.bfloat16
MIB = 1 << 20


def dot_nn(a, b):
    return lax.dot_general(a, b, (((1,), (0,)), ((), ())), preferred_element_type=f32)


def dot_nt(a, b):
    return lax.dot_general(a, b, (((1,), (1,)), ((), ())), preferred_element_type=f32)


def dot_tn(a, b):
    return lax.dot_general(a, b, (((0,), (0,)), ((), ())), preferred_element_type=f32)


def inverse_rms(values):
    return lax.rsqrt(jnp.mean(values * values, axis=-1, keepdims=True) + EPS)


def norm_backward(grad_normed, values, gain):
    inverse = inverse_rms(values)
    scaled = grad_normed * gain
    grad_values = inverse * scaled - values * (
        inverse**3 * jnp.mean(scaled * values, axis=-1, keepdims=True)
    )
    grad_gain = jnp.sum(grad_normed * values * inverse, axis=0, keepdims=True)
    return grad_values, grad_gain


def storage_place(indices, span_rows, half_rows):
    second = 2 * half_rows - span_rows * (indices // span_rows + 1) + indices % span_rows
    return jnp.stack([indices, second], axis=-1)


def exchange(block, axis, mask):
    size = lax.axis_size(axis)
    return lax.ppermute(block, axis, [(i, i ^ mask) for i in range(size)])


def passed_along(block, axis, distance):
    devices = range(lax.axis_size(axis))
    route = [(i - distance, i) for i in devices if i - distance in devices]
    return lax.ppermute(block, axis, route)


def bits_of(size):
    return [1 << b for b in reversed(range(size.bit_length() - 1))]


def relative_order(size):
    order = [0]
    for bit in bits_of(size):
        order = order + [r ^ bit for r in order]
    return order


def gather_pieces(block, axis):
    pieces = [block]
    for bit in bits_of(lax.axis_size(axis)):
        pieces = pieces + [exchange(p, axis, bit) for p in pieces]
    return pieces


def add_low(terms):
    total = terms[0].astype(f32)
    for term in terms[1:]:
        total = total + term.astype(f32)
    return total.astype(bf16)


def reduce_pieces(parts, axis):
    terms = [[p] for p in parts]
    for bit in reversed(bits_of(lax.axis_size(axis))):
        half = len(terms) // 2
        sent = [t[0] if len(t) == 1 else add_low(t) for t in terms[half:]]
        terms = [t + [exchange(s, axis, bit)] for t, s in zip(terms[:half], sent)]
    return terms[0]


def call(kernel, out_shape, args, flops, moved, name, limit=24, **kwargs):
    return pl.pallas_call(
        kernel,
        out_shape=out_shape,
        compiler_params=pltpu.CompilerParams(vmem_limit_bytes=limit * MIB),
        cost_estimate=pl.CostEstimate(flops=flops, bytes_accessed=moved, transcendentals=0),
        name=name,
        **kwargs,
    )(*args)


ANY = pl.BlockSpec(memory_space=pl.ANY)
VMEM = pl.BlockSpec(memory_space=pltpu.VMEM)
SMEM = pl.BlockSpec(memory_space=pltpu.SMEM)


def hold_kernel(count, *refs):
    copies = [
        pltpu.make_async_copy(refs[k], refs[count + k], refs[-1].at[k]) for k in range(count)
    ]
    for copy in copies:
        copy.start()
    for copy in copies:
        copy.wait()


def hold(*arrays):
    return call(
        functools.partial(hold_kernel, len(arrays)),
        tuple(pltpu.VMEM(a.shape, a.dtype) for a in arrays),
        [far(a) for a in arrays],
        0,
        2 * sum(a.size for a in arrays),
        "hold",
        limit=4,
        in_specs=[ANY] * len(arrays),
        out_specs=tuple(VMEM for _ in arrays),
        scratch_shapes=[pltpu.SemaphoreType.DMA((len(arrays),))],
    )


def held(array):
    return pltpu.with_memory_space_constraint(array, pltpu.VMEM)


def far(array):
    return pltpu.with_memory_space_constraint(array, pltpu.HBM)


def bring(flag_ref, sources, targets, sem):
    copies = []
    for k, (source, target) in enumerate(zip(sources, targets)):
        if len(source) == 1:
            copy = pltpu.make_async_copy(source[0], target, sem.at[k])
            copy.start()
        else:
            for is_first, ref in zip((1, 0), source):
                copy = pltpu.make_async_copy(ref, target, sem.at[k])
                pl.when(flag_ref[0] == is_first)(copy.start)
        copies.append(copy)
    return copies


def taken(refs, counts):
    groups = []
    for count in counts:
        groups.append(refs[:count])
        refs = refs[count:]
    return groups, refs


def turn(value, cos, sin):
    return value * cos + pltpu.roll(value, HEAD_DIM // 2, 1) * sin


def repeat_rows(table, count):
    return table if count == 1 else jnp.concatenate([table] * count, axis=0)


def choose(flag_ref, refs):
    if len(refs) == 1:
        return refs[0][...]
    return jnp.where(flag_ref[0] == 1, refs[0][...], refs[1][...])


def column_copies(source, target, sem):
    tile = 2 * KCOLS
    copies = []
    for k in range(source.shape[1] // tile):
        here = (slice(None), pl.ds(k * tile, tile))
        copies.append(pltpu.make_async_copy(source.at[here], target.at[here], sem.at[k]))
        copies[-1].start()
    return copies


def project_kernel(reps, versions, *refs):
    flag_ref, gain_ref, w_hbm, b_ref, cos_ref, sin_ref = refs[:6]
    x_refs = refs[6 : 6 + versions]
    q_ref, kv_ref, n_ref, w_ref, sem = refs[-5:]
    copies = column_copies(w_hbm, w_ref, sem)
    x = choose(flag_ref, x_refs).astype(f32)
    n_ref[...] = (x * inverse_rms(x) * gain_ref[...].astype(f32)).astype(bf16)
    cos = repeat_rows(cos_ref[...], reps)
    sin = repeat_rows(sin_ref[...], reps)
    tile = 2 * KCOLS
    for start in range(0, w_ref.shape[1], tile):
        here = slice(start, start + tile)
        copies[start // tile].wait()
        projected = dot_nn(n_ref[...], w_ref[:, here]) + b_ref[:, here].astype(f32)
        turned = []
        for j in range(0, tile, HEAD_DIM):
            part = projected[:, j : j + HEAD_DIM]
            turned.append(part if start + j >= QCOLS + KCOLS else turn(part, cos, sin))
        low = jnp.concatenate(turned, axis=1).astype(bf16)
        if start < QCOLS:
            q_ref[:, here] = low
        else:
            kv_ref[...] = low


def project(flag, xs, gain, w, b, cos, sin, reps, after=()):
    tokens, width = xs[0].shape
    columns = w.shape[1]
    return call(
        functools.partial(project_kernel, reps, len(xs)),
        (
            jax.ShapeDtypeStruct((tokens, QCOLS), bf16),
            jax.ShapeDtypeStruct((tokens, 2 * KCOLS), bf16),
        ),
        (flag, gain, far(w), b, cos, sin, *xs, *after),
        2 * tokens * width * columns,
        2 * width * columns,
        "project",
        limit=16,
        in_specs=[SMEM, VMEM, ANY] + [VMEM] * (3 + len(xs)) + [ANY] * len(after),
        out_specs=(VMEM, VMEM),
        scratch_shapes=[
            pltpu.VMEM((tokens, width), bf16),
            pltpu.VMEM((width, columns), bf16),
            pltpu.SemaphoreType.DMA((columns // (2 * KCOLS),)),
        ],
    )


def head_rows(block, g):
    return jnp.concatenate(
        [
            block[:, (g * GROUP + j) * HEAD_DIM : (g * GROUP + j + 1) * HEAD_DIM]
            for j in range(GROUP)
        ],
        axis=0,
    )


def head_columns(rows, tokens):
    return [rows[j * tokens : (j + 1) * tokens] for j in range(GROUP)]


def key_rows(ref, seq, reps, tokens, column):
    columns = slice(column * HEAD_DIM, (column + 1) * HEAD_DIM)
    if reps == 1:
        return ref[:, columns]
    stride = reps * tokens
    return jnp.concatenate(
        [
            ref[a * stride + seq * tokens : a * stride + (seq + 1) * tokens, columns]
            for a in range(ref.shape[0] // stride)
        ],
        axis=0,
    )


def masked_scores(q, key_block, mask, tokens):
    scores = dot_nt(q, key_block) * SCALE
    keys = scores.shape[1]
    return (scores.reshape(GROUP, tokens, keys) + mask[None]).reshape(GROUP * tokens, keys)


def attend_kernel(pieces, reps, versions, *refs):
    flag_ref, q_ref, mask_ref, ow_hbm, gain_ref = refs[:5]
    kv_refs = refs[5 : 5 + pieces]
    x_refs = refs[5 + pieces : 5 + pieces + versions]
    att_ref, hid_ref, n2_ref, ow_ref, sem = refs[5 + pieces + versions :]
    weights_in = pltpu.make_async_copy(ow_hbm, ow_ref, sem)
    weights_in.start()
    tokens = q_ref.shape[0] // reps
    for seq in range(reps):
        rows = slice(seq * tokens, (seq + 1) * tokens)
        q_all = q_ref[rows, :]
        for g in range(KV_HEADS):
            q = head_rows(q_all, g)
            scores = [
                masked_scores(q, key_rows(kv, seq, reps, tokens, g), mask_ref[p], tokens)
                for p, kv in enumerate(kv_refs)
            ]
            top = functools.reduce(
                jnp.maximum, [jnp.max(s, axis=-1, keepdims=True) for s in scores]
            )
            total = jnp.zeros_like(top)
            acc = jnp.zeros((GROUP * tokens, HEAD_DIM), f32)
            for s, kv in zip(scores, kv_refs):
                weights = jnp.exp(s - top)
                total = total + jnp.sum(weights, axis=-1, keepdims=True)
                acc = acc + dot_nn(
                    weights.astype(bf16), key_rows(kv, seq, reps, tokens, KV_HEADS + g)
                )
            low = (acc / total).astype(bf16)
            for j, block in enumerate(head_columns(low, tokens)):
                head = g * GROUP + j
                att_ref[rows, head * HEAD_DIM : (head + 1) * HEAD_DIM] = block
    weights_in.wait()
    hidden = choose(flag_ref, x_refs).astype(f32) + dot_nn(att_ref[...], ow_ref[...])
    hid_ref[...] = hidden
    n2_ref[...] = (hidden * inverse_rms(hidden) * gain_ref[...].astype(f32)).astype(bf16)


def attend(flag, q, xs, mask, ow, gain, kv_pieces, reps):
    tokens, width = xs[0].shape
    keys = sum(p.shape[0] for p in kv_pieces)
    return call(
        functools.partial(attend_kernel, len(kv_pieces), reps, len(xs)),
        (
            jax.ShapeDtypeStruct((tokens, QCOLS), bf16),
            jax.ShapeDtypeStruct((tokens, width), f32),
            jax.ShapeDtypeStruct((tokens, width), bf16),
        ),
        (flag, q, mask, far(ow), gain, *kv_pieces, *xs),
        2 * tokens * QCOLS * width + 12 * tokens * QCOLS * keys // reps,
        4 * keys * KCOLS + 12 * tokens * width,
        "attend",
        limit=16 + 24 * keys // (reps * 4096),
        in_specs=[SMEM, VMEM, VMEM, ANY] + [VMEM] * (1 + len(kv_pieces) + len(xs)),
        out_specs=(VMEM,) * 3,
        scratch_shapes=[pltpu.VMEM(ow.shape, bf16), pltpu.SemaphoreType.DMA(())],
    )


def fill(scratch, refs):
    size = refs[0].shape[0]
    for p, ref in enumerate(refs):
        scratch[p * size : (p + 1) * size, :] = ref[...]


def spread(out_refs, acc_ref):
    size = out_refs[0].shape[0]
    for p, ref in enumerate(out_refs):
        ref[...] = acc_ref[p * size : (p + 1) * size, :].astype(bf16)


def unit_spans(units):
    return [slice(at, min(at + UNITS, units)) for at in range(0, units, UNITS)]


def mlp_kernel(pieces, *refs):
    n_refs = refs[:pieces]
    gate_ref, up_ref, down_ref = refs[pieces : pieces + 3]
    out_refs = refs[-pieces - 2 : -2]
    cat_ref, acc_ref = refs[-2:]
    fill(cat_ref, n_refs)
    for k, here in enumerate(unit_spans(gate_ref.shape[0])):
        rows = cat_ref[...]
        gate_pre = dot_nt(rows, gate_ref[here, :])
        up_pre = dot_nt(rows, up_ref[here, :])
        activated = (jax.nn.sigmoid(gate_pre) * gate_pre * up_pre).astype(bf16)
        term = dot_nn(activated, down_ref[here, :])
        if k == 0:
            acc_ref[...] = term
        else:
            acc_ref[...] += term
    spread(out_refs, acc_ref)


def mlp(n_pieces, gate, up, down, after=()):
    units, width = gate.shape
    tokens = n_pieces[0].shape[0]
    count = len(n_pieces)
    return call(
        functools.partial(mlp_kernel, count),
        tuple(jax.ShapeDtypeStruct((tokens, width), bf16) for _ in n_pieces),
        (*n_pieces, held(gate), held(up), held(down), *after),
        6 * count * tokens * width * units,
        4 * count * tokens * width,
        "mlp",
        limit=12,
        in_specs=[VMEM] * (count + 3) + [ANY] * len(after),
        out_specs=(VMEM,) * count,
        scratch_shapes=[
            pltpu.VMEM((count * tokens, width), bf16),
            pltpu.VMEM((count * tokens, width), f32),
        ],
    )


def swiglu_backward(gate_pre, up_pre, grad_act):
    sigmoid = jax.nn.sigmoid(gate_pre)
    silu = gate_pre * sigmoid
    grad_gate = (grad_act * up_pre * (sigmoid + silu * (1.0 - sigmoid))).astype(bf16)
    grad_up = (grad_act * silu).astype(bf16)
    return silu, grad_gate, grad_up


def mlp_back_kernel(pieces, versions, *refs):
    (flags, weights, n_refs, g_refs), rest = taken(
        refs, (1, 3, pieces * versions, pieces)
    )
    gate_ref, up_ref, down_ref = weights
    out_refs = rest[-pieces - 4 : -4]
    cat_ref, gcat_ref, acc_ref, sem = rest[-4:]
    size = cat_ref.shape[0] // pieces
    spans = [pl.ds(p * size, size) for p in range(pieces)]
    sources = [n_refs[p * versions : (p + 1) * versions] for p in range(pieces)]
    copies = bring(
        flags[0],
        sources + [(g,) for g in g_refs],
        [cat_ref.at[span] for span in spans] + [gcat_ref.at[span] for span in spans],
        sem,
    )
    for copy in copies:
        copy.wait()
    for k, here in enumerate(unit_spans(gate_ref.shape[0])):
        rows = cat_ref[...]
        gate_pre = dot_nt(rows, gate_ref[here, :])
        up_pre = dot_nt(rows, up_ref[here, :])
        grad_act = dot_nt(gcat_ref[...], down_ref[here, :])
        _, grad_gate, grad_up = swiglu_backward(gate_pre, up_pre, grad_act)
        term = dot_nn(grad_gate, gate_ref[here, :]) + dot_nn(grad_up, up_ref[here, :])
        if k == 0:
            acc_ref[...] = term
        else:
            acc_ref[...] += term
    spread(out_refs, acc_ref)


def mlp_back(flag, n_versions, g_pieces, gate, up, down, after):
    units, width = gate.shape
    tokens = g_pieces[0].shape[0]
    count = len(g_pieces)
    versions = len(n_versions[0])
    n_arrays = [far(array) for piece in n_versions for array in piece]
    return call(
        functools.partial(mlp_back_kernel, count, versions),
        tuple(jax.ShapeDtypeStruct((tokens, width), bf16) for _ in g_pieces),
        (flag, held(gate), held(up), held(down), *n_arrays, *g_pieces, *after),
        10 * count * tokens * width * units,
        6 * count * tokens * width,
        "mlp_back",
        limit=16,
        in_specs=[SMEM] + [VMEM] * 3 + [ANY] * (len(n_arrays) + count + len(after)),
        out_specs=(VMEM,) * count,
        scratch_shapes=[
            pltpu.VMEM((count * tokens, width), bf16),
            pltpu.VMEM((count * tokens, width), bf16),
            pltpu.VMEM((count * tokens, width), f32),
            pltpu.SemaphoreType.DMA((2 * count,)),
        ],
    )


def sum_refs(refs):
    total = refs[0][...].astype(f32)
    for ref in refs[1:]:
        total = total + ref[...].astype(f32)
    return total


def attend_back_kernel(pieces, terms, reps, versions, *refs):
    (fixed, t_refs, sources, outs, dkv_refs, scratch), _ = taken(
        refs, (7, terms, (2 + pieces) * versions, 4, pieces, 6)
    )
    flag_ref, gy_ref, gain_ref, ow_hbm, mask_ref, cos_ref, sin_ref = fixed
    gh_ref, ghl_ref, dq_ref, mg_ref = outs
    hid_ref, q_ref, kv_ref, sem, ow_ref, ow_sem = scratch
    weights_in = pltpu.make_async_copy(ow_hbm, ow_ref, ow_sem)
    kv_refs = [kv_ref.at[p] for p in range(pieces)]
    copies = bring(
        flag_ref,
        [sources[k * versions : (k + 1) * versions] for k in range(2 + pieces)],
        [hid_ref, q_ref, *kv_refs],
        sem,
    )
    weights_in.start()
    tokens = q_ref.shape[0] // reps
    grad_normed = sum_refs(t_refs)
    for copy in copies:
        copy.wait()
    grad_from_two, grad_gain = norm_backward(
        grad_normed, hid_ref[...], gain_ref[...].astype(f32)
    )
    mg_ref[...] = grad_gain
    grad_hidden = gy_ref[...].astype(f32) + grad_from_two
    gh_ref[...] = grad_hidden
    grad_low = grad_hidden.astype(bf16)
    ghl_ref[...] = grad_low
    weights_in.wait()
    grad_att = dot_nt(grad_low, ow_ref[...]).astype(bf16)
    cos = cos_ref[...]
    sin = sin_ref[...]
    for seq in range(reps):
        rows = slice(seq * tokens, (seq + 1) * tokens)
        q_all = q_ref[rows, :]
        grad_all = grad_att[rows, :]
        for g in range(KV_HEADS):
            q = head_rows(q_all, g)
            go = head_rows(grad_all, g)
            key_blocks = [key_rows(kv, seq, reps, tokens, g) for kv in kv_refs]
            scores = [
                masked_scores(q, k, mask_ref[p], tokens) for p, k in enumerate(key_blocks)
            ]
            top = functools.reduce(
                jnp.maximum, [jnp.max(s, axis=-1, keepdims=True) for s in scores]
            )
            weights = [jnp.exp(s - top) for s in scores]
            total = functools.reduce(
                jnp.add, [jnp.sum(w, axis=-1, keepdims=True) for w in weights]
            )
            scale = 1.0 / total
            probs = [w * scale for w in weights]
            grad_probs = [
                dot_nt(go, key_rows(kv, seq, reps, tokens, KV_HEADS + g)) for kv in kv_refs
            ]
            delta = functools.reduce(
                jnp.add,
                [jnp.sum(p * d, axis=-1, keepdims=True) for p, d in zip(probs, grad_probs)],
            )
            dq = jnp.zeros((GROUP * tokens, HEAD_DIM), f32)
            for p in range(pieces):
                grad_z = (probs[p] * (grad_probs[p] - delta) * SCALE).astype(bf16)
                dq = dq + dot_nn(grad_z, key_blocks[p])
                dk = dot_tn(grad_z, q).astype(bf16)
                dv = dot_tn(probs[p].astype(bf16), go).astype(bf16)
                stride = reps * tokens
                for a in range(dk.shape[0] // tokens):
                    here = slice(a * stride + seq * tokens, a * stride + (seq + 1) * tokens)
                    part = slice(a * tokens, (a + 1) * tokens)
                    dkv_refs[p][here, g * HEAD_DIM : (g + 1) * HEAD_DIM] = dk[part]
                    v_at = (KV_HEADS + g) * HEAD_DIM
                    dkv_refs[p][here, v_at : v_at + HEAD_DIM] = dv[part]
            for j, block in enumerate(head_columns(dq, tokens)):
                head = g * GROUP + j
                dq_ref[rows, head * HEAD_DIM : (head + 1) * HEAD_DIM] = turn(
                    block, cos, -sin
                ).astype(bf16)


def attend_back(flag, gy, gain, ow, mask, cos, sin, terms, kept, reps):
    tokens, width = gy.shape
    pieces = len(kept) - 2
    versions = len(kept[0])
    arrays = [far(array) for item in kept for array in item]
    piece = kept[2][0]
    keys = pieces * piece.shape[0]
    return call(
        functools.partial(attend_back_kernel, pieces, len(terms), reps, versions),
        (
            jax.ShapeDtypeStruct((tokens, width), f32),
            jax.ShapeDtypeStruct((tokens, width), bf16),
            jax.ShapeDtypeStruct((tokens, QCOLS), bf16),
            jax.ShapeDtypeStruct((1, width), f32),
            *(jax.ShapeDtypeStruct(piece.shape, bf16) for _ in range(pieces)),
        ),
        (flag, gy, gain, far(ow), mask, cos, sin, *terms, *arrays),
        2 * tokens * QCOLS * width + 30 * tokens * QCOLS * keys // reps,
        8 * keys * KCOLS + 20 * tokens * width,
        "attend_back",
        limit=20 + 24 * keys // (reps * 4096),
        in_specs=[SMEM, VMEM, VMEM, ANY] + [VMEM] * (3 + len(terms)) + [ANY] * len(arrays),
        out_specs=(VMEM,) * (4 + pieces),
        scratch_shapes=[
            pltpu.VMEM((tokens, width), f32),
            pltpu.VMEM((tokens, QCOLS), bf16),
            pltpu.VMEM((pieces, *piece.shape), bf16),
            pltpu.SemaphoreType.DMA((2 + pieces,)),
            pltpu.VMEM(ow.shape, bf16),
            pltpu.SemaphoreType.DMA(()),
        ],
    )


def project_back_kernel(terms, reps, versions, *refs):
    (fixed, t_refs, x_refs, outs, scratch), _ = taken(refs, (7, terms, versions, 5, 2))
    flag_ref, dq_ref, gh_ref, gain_ref, w_hbm, cos_ref, sin_ref = fixed
    w_ref, sem = scratch
    copies = column_copies(w_hbm, w_ref, sem)
    gin_ref, gp_ref, n_ref, b_ref, ag_ref = outs
    dkv = sum_refs(t_refs)
    cos = repeat_rows(cos_ref[...], reps)
    sin = repeat_rows(sin_ref[...], reps)
    parts = [
        turn(dkv[:, j * HEAD_DIM : (j + 1) * HEAD_DIM], cos, -sin) for j in range(KV_HEADS)
    ]
    parts.append(dkv[:, KCOLS:])
    gp_ref[:, :QCOLS] = dq_ref[...]
    gp_ref[:, QCOLS:] = jnp.concatenate(parts, axis=1).astype(bf16)
    grad_projected = gp_ref[...]
    b_ref[...] = jnp.sum(grad_projected.astype(f32), axis=0, keepdims=True)
    x = choose(flag_ref, x_refs).astype(f32)
    gain = gain_ref[...].astype(f32)
    n_ref[...] = (x * inverse_rms(x) * gain).astype(bf16)
    grad_normed = jnp.zeros(x.shape, f32)
    tile = 2 * KCOLS
    for k, copy in enumerate(copies):
        here = slice(k * tile, (k + 1) * tile)
        copy.wait()
        grad_normed = grad_normed + dot_nt(grad_projected[:, here], w_ref[:, here])
    grad_source, grad_gain = norm_backward(grad_normed, x, gain)
    ag_ref[...] = grad_gain
    gin_ref[...] = (gh_ref[...] + grad_source).astype(bf16)


def project_back(flag, dq, xs, gh, gain, w, cos, sin, terms, reps):
    tokens, width = gh.shape
    columns = w.shape[1]
    return call(
        functools.partial(project_back_kernel, len(terms), reps, len(xs)),
        (
            jax.ShapeDtypeStruct((tokens, width), bf16),
            jax.ShapeDtypeStruct((tokens, columns), bf16),
            jax.ShapeDtypeStruct((tokens, width), bf16),
            jax.ShapeDtypeStruct((1, columns), f32),
            jax.ShapeDtypeStruct((1, width), f32),
        ),
        (flag, dq, gh, gain, far(w), cos, sin, *terms, *xs),
        2 * tokens * width * columns,
        2 * width * columns,
        "project_back",
        limit=20,
        in_specs=[SMEM] + [VMEM] * 3 + [ANY] + [VMEM] * (2 + len(terms) + len(xs)),
        out_specs=(VMEM,) * 5,
        scratch_shapes=[
            pltpu.VMEM((width, columns), bf16),
            pltpu.SemaphoreType.DMA((columns // (2 * KCOLS),)),
        ],
    )


def attention_grads_kernel(steps, versions, parts, *refs):
    (flags, sources, outs, scratch), _ = taken(refs, (1, 3 * steps + sum(versions), parts, 5))
    at_ref = flags[0]
    n_ref, p_ref, a_ref, h_ref, sem = scratch
    size = n_ref.shape[0] // steps
    copies = []
    groups = []
    targets = []
    for k, target in enumerate((n_ref, p_ref, h_ref)):
        for t in range(steps):
            groups.append((sources[k * steps + t],))
            targets.append(target.at[pl.ds(t * size, size)])
    at = 3 * steps
    for t in range(steps):
        groups.append(sources[at : at + versions[t]])
        targets.append(a_ref.at[pl.ds(t * size, size)])
        at += versions[t]
    copies = bring(at_ref, groups, targets, sem)
    for copy in copies:
        copy.wait()
    columns = p_ref.shape[1]
    rows = outs[0].shape[0]
    for r, out in enumerate(outs):
        here = pl.ds(pl.multiple_of(at_ref[1 + r] * rows, HEAD_DIM), rows)
        out[:, :columns] = dot_tn(n_ref[:, here], p_ref[...]).astype(bf16)
        out[:, columns:] = dot_tn(a_ref[:, here], h_ref[...]).astype(bf16)


def attention_grads(marks, normed, projected, grad_hidden, attended, parts):
    steps = len(normed)
    tokens, width = normed[0].shape
    columns = projected[0].shape[1]
    rows = width // parts
    versions = [len(a) for a in attended]
    arrays = [*normed, *projected, *grad_hidden, *(a for item in attended for a in item)]
    total = steps * tokens
    return call(
        functools.partial(attention_grads_kernel, steps, versions, parts),
        (jax.ShapeDtypeStruct((rows, columns + width), bf16),) * parts,
        (marks, *arrays),
        2 * total * width * (columns + width),
        2 * total * (2 * width + columns) + 2 * width * (width + columns),
        "attention_grads",
        limit=40,
        in_specs=[SMEM] + [ANY] * len(arrays),
        out_specs=(VMEM,) * parts,
        scratch_shapes=[
            pltpu.VMEM((total, width), bf16),
            pltpu.VMEM((total, columns), bf16),
            pltpu.VMEM((total, width), bf16),
            pltpu.VMEM((total, width), bf16),
            pltpu.SemaphoreType.DMA((4 * steps,)),
        ],
    )


def assemble_kernel(pieces, *refs):
    at_ref = refs[0]
    piece_refs = refs[1 : 1 + pieces]
    left_ref, right_ref = refs[-2:]
    columns = left_ref.shape[1]
    rows = piece_refs[0].shape[0]
    for a, piece in enumerate(piece_refs):
        here = pl.ds(pl.multiple_of(at_ref[a] * rows, 8), rows)
        left_ref[here, :] = piece[:, :columns].astype(f32)
        right_ref[here, :] = piece[:, columns:].astype(f32)


def assemble(places, pieces, columns, after):
    rows, total = pieces[0].shape
    count = len(pieces)
    return call(
        functools.partial(assemble_kernel, count),
        (
            jax.ShapeDtypeStruct((rows * count, columns), f32),
            jax.ShapeDtypeStruct((rows * count, total - columns), f32),
        ),
        (places, *pieces, *after),
        0,
        6 * rows * count * total,
        "assemble",
        limit=24,
        in_specs=[SMEM] + [VMEM] * count + [ANY] * len(after),
        out_specs=(VMEM, VMEM),
    )


def unit_tile(units, most):
    return max(t for t in range(16, most + 1, 16) if units % t == 0)


def weight_grad_kernel(aliased, adds, *refs):
    n_ref, g_ref, gate_ref, up_ref, down_ref = refs[:5]
    olds = refs[5 : 5 + aliased]
    news = refs[-4:-1]
    refs[-1][...] = jnp.zeros_like(refs[-1])

    @pl.when(pl.program_id(1) == 0)
    def _():
        for k, new in enumerate(news):
            new[...] = olds[k][...] if adds else jnp.zeros_like(new)

    rows = n_ref[...]
    grads = g_ref[...]
    gate_pre = dot_nt(gate_ref[...], rows)
    up_pre = dot_nt(up_ref[...], rows)
    grad_act = dot_nt(down_ref[...], grads)
    silu, grad_gate, grad_up = swiglu_backward(gate_pre, up_pre, grad_act)
    activated = (silu * up_pre).astype(bf16)
    news[0][...] += dot_nn(grad_gate, rows)
    news[1][...] += dot_nn(grad_up, rows)
    news[2][...] += dot_nn(activated, grads)


def weight_grads(n_all, g_all, gate, up, down, outs, adds, first, count, after):
    units, width = gate.shape
    tokens = n_all.shape[0]
    tile = unit_tile(units, 320)
    chunk = math.gcd(tokens, 1024)
    shape = jax.ShapeDtypeStruct((units, width), f32)
    part = pl.BlockSpec((tile, width), lambda i, j: (i + first, 0))
    rows = pl.BlockSpec((chunk, width), lambda i, j: (j, 0))
    *outs, zeros = call(
        functools.partial(weight_grad_kernel, len(outs), adds),
        (*(shape,) * 3, jax.ShapeDtypeStruct((8, 128), f32)),
        (n_all, g_all, gate, up, down, *outs, *after),
        12 * tokens * width * tile * count,
        18 * width * tile * count,
        "weight_grads",
        limit=60,
        grid=(count, tokens // chunk),
        in_specs=[rows] * 2
        + [part] * 3
        + [part if adds else ANY] * len(outs)
        + [ANY] * len(after),
        out_specs=((*(part,) * 3, pl.BlockSpec((8, 128), lambda i, j: (0, 0)))),
        input_output_aliases={5 + k: k for k in range(len(outs))},
    )
    return outs, zeros


def body(
    inputs,
    cotangent,
    attn_gain,
    qkv_weight,
    qkv_bias,
    out_weight,
    mlp_gain,
    gate_weight,
    up_weight,
    down_weight,
):
    first = lax.axis_index("section") == 0
    micro, rows_here, _, width = inputs.shape
    fsdp = lax.axis_size("fsdp")
    ctx = lax.axis_size("ctx")
    fsdp_at = lax.axis_index("fsdp")
    ctx_at = lax.axis_index("ctx")
    tokens = 2 * rows_here
    reps = MICROS
    chunks = micro // reps
    steps = chunks + LAG
    span_rows = rows_here * fsdp
    half_rows = span_rows * ctx

    def places_of(c, f):
        index = (c * fsdp + f) * rows_here + jnp.arange(rows_here, dtype=jnp.int32)
        return storage_place(index, span_rows, half_rows).reshape(tokens)

    own = places_of(ctx_at, fsdp_at)
    key_places = jnp.stack(
        [
            jnp.concatenate([places_of(ctx_at ^ a, fsdp_at ^ r) for a in range(ctx)])
            for r in relative_order(fsdp)
        ]
    )
    mask = jnp.where(key_places[:, None, :] <= own[None, :, None], 0.0, NEGATIVE).astype(f32)
    half = HEAD_DIM // 2
    frequency = ROPE_BASE ** (-(jnp.arange(half, dtype=f32) * 2.0) / HEAD_DIM)
    angles = own.astype(f32)[:, None] * frequency
    cos = jnp.concatenate([jnp.cos(angles)] * 2, axis=1)
    sin = jnp.concatenate([-jnp.sin(angles), jnp.sin(angles)], axis=1)

    def gathered(shard):
        return lax.all_gather(shard, "fsdp", axis=0, tiled=True)

    qkv_full = gathered(qkv_weight[0])
    attn_full = gathered(attn_gain[0])[None]
    bias_full = gathered(qkv_bias[0])[None]
    mlp_full = gathered(mlp_gain[0])[None]
    out_full = gathered(out_weight[0])
    gate, up, down = gate_weight[0], up_weight[0], down_weight[0]

    def chunked(array):
        return array.reshape(chunks, reps * tokens, width)

    in_chunks = chunked(inputs)
    cot_chunks = chunked(cotangent)

    gate_held, up_held, down_held = hold(gate, up, down)
    flag = first.astype(jnp.int32).reshape(1)

    def pick(early, late):
        return jnp.where(first, early, late)

    def versions(u, early, late):
        if u < LAG:
            return (late[u + LAG],)
        if u < chunks:
            return (early[u - LAG], late[u + LAG])
        return (early[u - LAG],)

    gys = [jnp.where(first, jnp.zeros_like(cot), cot) for cot in cot_chunks[:LAG]]
    early_pieces = [gather_pieces(gy, "fsdp") for gy in gys]

    outputs, moved, xs, kept, attended, n2_pieces = [], [], [], [], [], []

    def finish(t, after=()):
        parts = mlp(n2_pieces[t], gate_held, up_held, down_held, after)
        hidden = kept[t][0]
        outputs.append(add_low([hidden] + reduce_pieces(list(parts), "fsdp")))
        if t < chunks:
            moved.append(passed_along(outputs[t], "section", 1))

    for t in range(steps):
        if t < LAG:
            x = (in_chunks[t],)
        elif t < chunks:
            x = (in_chunks[t], moved[t - LAG])
        else:
            x = (moved[t - LAG],)
        xs.append(x)
        after = [p for pieces in early_pieces for p in pieces[1:]] if t == 0 else []
        q, kv = project(flag, x, attn_full, qkv_full, bias_full, cos, sin, reps, after)
        kv_ctx = jnp.concatenate([kv] + [exchange(kv, "ctx", a) for a in range(1, ctx)], axis=0)
        kv_pieces = gather_pieces(kv_ctx, "fsdp")
        att, hidden, n2 = attend(flag, q, x, mask, out_full, mlp_full, kv_pieces, reps)
        attended.append(att)
        n2_pieces.append(gather_pieces(n2, "fsdp"))
        kept.append((hidden, q, *kv_pieces))
        if t < chunks:
            finish(t)

    batches = [b for b in (range(0, chunks // 2), range(chunks // 2, chunks)) if len(b)]

    def all_tokens(early, late, batch):
        own_rows = jnp.concatenate([pick(early[m], late[m]) for m in batch], axis=0)
        return lax.all_gather(own_rows, ("ctx", "fsdp"), axis=0, tiled=True)

    n2_own = [pieces[0] for pieces in n2_pieces]
    n2_all = [all_tokens(n2_own, n2_own[LAG:], batch) for batch in batches]

    grads_in, grads_moved, smalls, factors = [], [], [], []
    for u in range(steps):
        if u < LAG:
            gy, g_pieces = gys[u], early_pieces[u]
        else:
            gy = grads_moved[u - LAG]
            gy = pick(gy, cot_chunks[u]) if u < chunks else gy
            gys.append(gy)
            g_pieces = gather_pieces(gy, "fsdp")
        after = [outputs[u + LAG]] if u + LAG < chunks else []
        n2_now = list(zip(*versions(u, n2_pieces, n2_pieces)))
        parts = mlp_back(flag, n2_now, g_pieces, gate_held, up_held, down_held, after)
        terms = reduce_pieces(list(parts), "fsdp")
        kept_now = list(zip(*versions(u, kept, kept)))
        gh, gh_low, dq, grad_mlp_gain, *dkv = attend_back(
            flag, gy, mlp_full, out_full, mask, cos, sin, terms, kept_now, reps
        )
        dkv_ctx = add_low(reduce_pieces(dkv, "fsdp"))
        size = reps * tokens
        dkv_terms = [
            dkv_ctx[a * size : (a + 1) * size]
            if a == 0
            else exchange(dkv_ctx[a * size : (a + 1) * size], "ctx", a)
            for a in range(ctx)
        ]
        x_early = [x[0] for x in xs]
        x_late = [x[-1] for x in xs]
        x_now = versions(u, x_early, x_late)
        g_in, g_proj, normed, grad_bias, grad_attn_gain = project_back(
            flag, dq, x_now, gh, attn_full, qkv_full, cos, sin, dkv_terms, reps
        )
        grads_in.append(g_in)
        if u < chunks:
            grads_moved.append(passed_along(g_in, "section", -1))
        smalls.append(jnp.concatenate([grad_attn_gain, grad_bias, grad_mlp_gain], axis=1))
        factors.append((normed, g_proj, gh_low, versions(u, attended, attended)))
        if u >= LAG and len(outputs) < steps:
            finish(len(outputs), [g_in])

    g_all = [all_tokens(gys[LAG:], gys, batch) for batch in batches]
    tiles = gate.shape[0] // unit_tile(gate.shape[0], 320)
    cuts = [0, 4 * tiles // 7, tiles], [0, tiles // 7, 5 * tiles // 7, tiles]
    plan = [
        (b, i, j - i)
        for b in range(len(batches))
        for i, j in zip(cuts[b], cuts[b][1:])
        if j > i
    ]
    mlp_grads = []

    def some_weight_grads(after):
        nonlocal mlp_grads
        if not plan:
            return None
        b, start, count = plan.pop(0)
        mlp_grads, zeros = weight_grads(
            n2_all[b], g_all[b], gate, up, down, mlp_grads, b > 0, start, count, after
        )
        return zeros

    lead = QCOLS + KCOLS
    columns = QCOLS + 2 * KCOLS
    marks = jnp.stack(
        [flag[0]] + [(fsdp_at ^ r).astype(jnp.int32) for r in relative_order(fsdp)]
    )
    normed, projected, grad_hidden, att_now = zip(*factors)
    small = functools.reduce(jnp.add, smalls).reshape(-1, HEAD_DIM)
    rows = width // fsdp
    if rows % HEAD_DIM == 0:
        summed = attention_grads(marks, normed, projected, grad_hidden, att_now, fsdp)
    else:
        start = jnp.stack([flag[0], jnp.int32(0)])
        (large,) = attention_grads(start, normed, projected, grad_hidden, att_now, 1)
        summed = [
            lax.dynamic_slice_in_dim(large, (fsdp_at ^ r) * rows, rows)
            for r in relative_order(fsdp)
        ]
    for bit in reversed(bits_of(fsdp)):
        count = len(summed) // 2
        moves = [exchange(p, "fsdp", bit) for p in summed[count:]]
        zero = 0.0
        if count == 1:
            zero = some_weight_grads([*summed[:1], *outputs[chunks:]])[0, 0]
        summed = [
            (p.astype(f32) + m.astype(f32) + zero).astype(bf16) for p, m in zip(summed, moves)
        ]
        small = small + exchange(small, "fsdp", bit)
    rows = width // fsdp // ctx
    terms = [
        lax.dynamic_slice_in_dim(summed[0], (ctx_at ^ a) * rows, rows) for a in range(ctx)
    ]
    moves = [exchange(terms[a], "ctx", a) for a in range(1, ctx)]
    for bit in bits_of(ctx):
        small = small + exchange(small, "ctx", bit)
    zeros = some_weight_grads(terms[:1])
    zeros = some_weight_grads([]) if plan else zeros
    block = functools.reduce(jnp.add, [t.astype(f32) for t in (terms[0], *moves)])
    block = (block + zeros[0, 0]).astype(bf16)
    pieces = [block] + [exchange(block, "ctx", a) for a in range(1, ctx)]
    zeros = some_weight_grads([block])
    places = jnp.stack([(ctx_at ^ a).astype(jnp.int32) for a in range(ctx)])
    grad_qkv, grad_out = assemble(places, pieces, columns, [] if zeros is None else [zeros])
    while plan:
        some_weight_grads([])
    grad_gate, grad_up, grad_down = mlp_grads

    small = small.reshape(-1)

    def cut(start, length):
        part = length // fsdp
        return lax.dynamic_slice(small, (start + fsdp_at * part,), (part,))

    grad_attn_gain = cut(0, width)
    grad_bias_lead = cut(width, lead)
    grad_bias_value = cut(width + lead, columns - lead)
    grad_mlp_gain = cut(width + columns, width)

    def restore(parts):
        return jnp.stack(parts).reshape(inputs.shape)

    layer_outputs = restore([pick(outputs[m], outputs[m + LAG]) for m in range(chunks)])
    input_grads = restore([pick(grads_in[m + LAG], grads_in[m]) for m in range(chunks)])
    return (
        layer_outputs[None],
        input_grads[None],
        grad_attn_gain[None],
        grad_qkv[None],
        grad_bias_lead[None],
        grad_bias_value[None],
        grad_out[None],
        grad_mlp_gain[None],
        grad_gate[None],
        grad_up[None],
        grad_down[None],
    )


def solution(mesh):
    rows = P(None, ("ctx", "fsdp"), None, None)
    vector = P("section", "fsdp")
    matrix = P("section", "fsdp", None)
    stacked = P("section", None, ("ctx", "fsdp"), None, None)
    in_specs = (rows, rows, vector, matrix, vector, matrix, vector, matrix, matrix, matrix)
    out_specs = (
        stacked,
        stacked,
        vector,
        matrix,
        vector,
        vector,
        matrix,
        vector,
        matrix,
        matrix,
        matrix,
    )
    return jax.shard_map(body, mesh=mesh, in_specs=in_specs, out_specs=out_specs, check_vma=False)
```

time: 1290 us -> 975 us (0.76)
  waiting for transfers between devices: 481 us -> 174 us
  blocking collectives: 79.9 us -> 17.1 us
  Pallas kernels: 454 us -> 485 us
  local copies, waits for them, and re-layouts: 60.3 us -> 87.2 us
    all_gather x2 -> x4, waiting for transfers between devices: 199 us -> 0.02 us  [all_tokens(): return lax.all_gather(own_rows, ('ctx', 'fsdp'), axis=0, tiled=True)]
    reduce_scatter x2 -> x0, waiting for transfers between devices: 73.8 us -> none  [own_shard(): lax.psum_scatter(whole.astype(bf16), 'fsdp', scatter_dimension=0, tiled=T...]
    psum x1 -> x0, blocking collectives: 63.2 us -> none  [body(): small = lax.psum(functools.reduce(jnp.add, smalls)[0], ('ctx', 'fsdp'))]
    pallas_call x40 -> x44, Pallas kernels: 454 us -> 485 us  [call(): pl.pallas_call(kernel, out_shape=out_shape, compiler_params=pltpu.Compile...]
    ppermute x144 -> x157, starting transfers between devices: 108 us -> 125 us  [exchange(): return lax.ppermute(block, axis, [(i, i ^ mask) for i in range(size)])]
    select_n x31 -> x12, other arithmetic: 29.6 us -> 12.6 us  [pick(): return jnp.where(first, early, late)]
    unnamed x546 -> x452, local copies, waits for them, and re-layouts: 45.8 us -> 61.4 us
    all_gather x2, waiting for transfers between devices: 44.5 us -> 29.6 us  [gathered(): return lax.all_gather(shard, 'fsdp', axis=0, tiled=True)]
  transfers between devices with their start and end apart: 159 -> 171, of which waited for: 57 -> 43; matrix products, arithmetic and copies ran while one was open for 5% -> 7% of each run, Pallas kernels for 17% -> 49%
where the time goes in v2:
time: 975 us; the launch traced here: 967 us
  Pallas kernels  485 us (50%)
  waiting for transfers between devices  174 us (18%)
  starting transfers between devices  140 us (14%)
  local copies, waits for them, and re-layouts  87.2 us (9%)
  other arithmetic  45.6 us (5%)
  between operations  18.1 us (2%)
  blocking collectives  17.1 us (2%)
    pallas_call x44, Pallas kernels, call(): pl.pallas_call(kernel, out_shape=out_shape, compiler_params=pltpu.Compile...  485 us
    ppermute x157, waiting for transfers between devices, exchange(): return lax.ppermute(block, axis, [(i, i ^ mask) for i in range(size)])  137 us
    ppermute x157, starting transfers between devices, exchange(): return lax.ppermute(block, axis, [(i, i ^ mask) for i in range(size)])  125 us
    unnamed x452, local copies, waits for them, and re-layouts  61.4 us
    all_gather x2, waiting for transfers between devices, gathered(): return lax.all_gather(shard, 'fsdp', axis=0, tiled=True)  29.6 us
  transfers between devices with their start and end apart: 171, of which 43 were waited for; matrix products, arithmetic and copies ran while one was open for 7% of the time, Pallas kernels for 49%

profile of v2, /device:TPU:0, one launch (start us, length us, event | category | flops | bytes accessed | tf_op | source)
XLA Modules:
  0.0 967.1 jit_solution(9684904158897200991)
XLA Ops:
  18.9 5.2 all-gather.refs_1_.refs_3_
  24.2 6.5 all-gather.2.refs_3_
  33.3 25.5 %all-gather.20.cloned.1.call-done = bf16[1,1536,2048]{2,1,0:T(8,128)(2,1)} async-done(((bf16[1,384,2048]{2,1,0:T(8,128)(2,1)}), bf16[1,1536,2048]{2,1,0:T(8,128)(2,1)}) %all-gather.20.cloned.1.call-update) | async-done | bytes 6291472 | tf_op jit(solution)/shard_map/all_gather | solution.py:827
  83.5 6.7 collective-permute-done.9.refs_6_.refs_16_
  90.8 9.8 %collective-permute-done.34.refs_6_.refs_16_ = bf16[256,512]{1,0:T(8,128)(2,1)S(1)} collective-permute-done((bf16[256,512]{1,0:T(8,128)(2,1)S(1)}, bf16[256,512]{1,0:T(8,128)(2,1)S(1)}, u32[]{:S(2)}, u32[]{:S(2)}) %collective-permute-start.34) | collective-permute-done | bytes 262176 | tf_op jit(solution)/shard_map/ppermute | solution.py:64
  100.7 5.3 all-gather.4.refs_4_.refs_2_
  123.6 7.0 hold.1
  131.4 6.1 mlp.6
  138.1 6.5 mlp.8
  147.4 5.6 collective-permute-done.17
  193.6 4.8 attend.7
  214.5 6.3 mlp.7
  221.5 6.1 mlp.9
  230.8 5.2 collective-permute-done.30
  295.4 11.6 %mlp_back.6 = (bf16[64,1536]{1,0:T(8,128)(2,1)S(1)}, bf16[64,1536]{1,0:T(8,128)(2,1)S(1)}, bf16[64,1536]{1,0:T(8,128)(2,1)S(1)}, bf16[64,1536]{1,0:T(8,128)(2,1)S(1)}) custom-call(s32[1]{0:T(128)} %bitcast.refs_0_, bf16[2240,1536]{1,0:T(8,128)(2,1)S(1)} %copy-done.1, bf16[2240,1536]{1,0:T(8,128)(2,1)S(1)} %copy-done.5, bf16[2240,1536]{1,0:T(8,128)(2,1)S(1)} %copy-done.10, ...), custom_call_target="tpu_custom_call" | custom-call | flops 8808038400 | bytes 2359296 | tf_op jit(solution)/shard_map/mlp_back/pallas_call | solution.py:108
  307.8 11.8 %mlp_back.8 = (bf16[64,1536]{1,0:T(8,128)(2,1)S(1)}, bf16[64,1536]{1,0:T(8,128)(2,1)S(1)}, bf16[64,1536]{1,0:T(8,128)(2,1)S(1)}, bf16[64,1536]{1,0:T(8,128)(2,1)S(1)}) custom-call(s32[1]{0:T(128)} %bitcast.refs_0_, bf16[2240,1536]{1,0:T(8,128)(2,1)S(1)} %copy-done.1, bf16[2240,1536]{1,0:T(8,128)(2,1)S(1)} %copy-done.5, bf16[2240,1536]{1,0:T(8,128)(2,1)S(1)} %copy-done.10, ...), custom_call_target="tpu_custom_call" | custom-call | flops 8808038400 | bytes 2359296 | tf_op jit(solution)/shard_map/mlp_back/pallas_call | solution.py:108
  322.7 9.5 collective-permute-done.68.refs_9_
  332.2 8.2 attend_back.6
  341.1 8.1 attend_back.8
  352.3 6.7 collective-permute-done.71
  368.0 5.1 project_back.6
  384.2 5.1 project_back.8
  391.7 5.9 collective-permute-done.110
  408.7 5.0 collective-permute-done.76.refs_13_
  413.7 5.6 collective-permute-done.98.refs_7_.refs_1_
  431.8 11.6 %mlp_back.7 = (bf16[64,1536]{1,0:T(8,128)(2,1)S(1)}, bf16[64,1536]{1,0:T(8,128)(2,1)S(1)}, bf16[64,1536]{1,0:T(8,128)(2,1)S(1)}, bf16[64,1536]{1,0:T(8,128)(2,1)S(1)}) custom-call(s32[1]{0:T(128)} %bitcast.refs_0_, bf16[2240,1536]{1,0:T(8,128)(2,1)S(1)} %copy-done.2, bf16[2240,1536]{1,0:T(8,128)(2,1)S(1)} %copy-done.6, bf16[2240,1536]{1,0:T(8,128)(2,1)S(1)} %copy-done.11, ...), custom_call_target="tpu_custom_call" | custom-call | flops 8808038400 | bytes 2359296 | tf_op jit(solution)/shard_map/mlp_back/pallas_call | solution.py:108
  444.7 11.7 %mlp_back.9 = (bf16[64,1536]{1,0:T(8,128)(2,1)S(1)}, bf16[64,1536]{1,0:T(8,128)(2,1)S(1)}, bf16[64,1536]{1,0:T(8,128)(2,1)S(1)}, bf16[64,1536]{1,0:T(8,128)(2,1)S(1)}) custom-call(s32[1]{0:T(128)} %bitcast.refs_0_, bf16[2240,1536]{1,0:T(8,128)(2,1)S(1)} %copy-done.2, bf16[2240,1536]{1,0:T(8,128)(2,1)S(1)} %copy-done.6, bf16[2240,1536]{1,0:T(8,128)(2,1)S(1)} %copy-done.11, ...), custom_call_target="tpu_custom_call" | custom-call | flops 8808038400 | bytes 2359296 | tf_op jit(solution)/shard_map/mlp_back/pallas_call | solution.py:108
  459.3 5.6 collective-permute-done.81.refs_9_
  464.8 8.0 attend_back.7
  473.6 7.9 attend_back.9
  484.7 6.8 collective-permute-done.84
  514.8 5.7 project_back.7
  526.3 5.3 project_back.9
  536.2 6.9 mlp.10
  545.0 6.8 mlp.11
  573.1 11.6 %mlp_back.10 = (bf16[64,1536]{1,0:T(8,128)(2,1)S(1)}, bf16[64,1536]{1,0:T(8,128)(2,1)S(1)}, bf16[64,1536]{1,0:T(8,128)(2,1)S(1)}, bf16[64,1536]{1,0:T(8,128)(2,1)S(1)}) custom-call(s32[1]{0:T(128)} %bitcast.refs_0_, bf16[2240,1536]{1,0:T(8,128)(2,1)S(1)} %copy-done.3, bf16[2240,1536]{1,0:T(8,128)(2,1)S(1)} %copy-done.7, bf16[2240,1536]{1,0:T(8,128)(2,1)S(1)} %copy-done.13, ...), custom_call_target="tpu_custom_call" | custom-call | flops 8808038400 | bytes 2359296 | tf_op jit(solution)/shard_map/mlp_back/pallas_call | solution.py:108
  585.4 11.6 %mlp_back.11 = (bf16[64,1536]{1,0:T(8,128)(2,1)S(1)}, bf16[64,1536]{1,0:T(8,128)(2,1)S(1)}, bf16[64,1536]{1,0:T(8,128)(2,1)S(1)}, bf16[64,1536]{1,0:T(8,128)(2,1)S(1)}) custom-call(s32[1]{0:T(128)} %bitcast.refs_0_, bf16[2240,1536]{1,0:T(8,128)(2,1)S(1)} %copy-done.3, bf16[2240,1536]{1,0:T(8,128)(2,1)S(1)} %copy-done.7, bf16[2240,1536]{1,0:T(8,128)(2,1)S(1)} %copy-done.13, ...), custom_call_target="tpu_custom_call" | custom-call | flops 8808038400 | bytes 2359296 | tf_op jit(solution)/shard_map/mlp_back/pallas_call | solution.py:108
  600.3 9.8 %collective-permute-done.132.refs_9_ = bf16[64,1536]{1,0:T(8,128)(2,1)S(1)} collective-permute-done((bf16[64,1536]{1,0:T(8,128)(2,1)S(1)}, bf16[64,1536]{1,0:T(8,128)(2,1)S(1)}, u32[]{:S(2)}, u32[]{:S(2)}) %collective-permute-start.132) | collective-permute-done | bytes 196640 | tf_op jit(solution)/shard_map/ppermute | solution.py:64
  611.3 8.9 attend_back.10
  620.8 8.2 attend_back.11
  631.8 6.5 collective-permute-done.135
  663.4 14.0 %attention_grads.1 = (bf16[384,3584]{1,0:T(8,128)(2,1)S(1)}, bf16[384,3584]{1,0:T(8,128)(2,1)S(1)}, bf16[384,3584]{1,0:T(8,128)(2,1)S(1)}, bf16[384,3584]{1,0:T(8,128)(2,1)}) custom-call(s32[5]{0:T(128)S(1)} %copy-done.160, bf16[64,1536]{1,0:T(8,128)(2,1)S(1)} %copy-done.183, bf16[64,1536]{1,0:T(8,128)(2,1)S(1)} %copy-done.185, ...), custom_call_target="tpu_custom_call" | custom-call | flops 4227858432 | bytes 14942208 | tf_op jit(solution)/shard_map/attention_grads/pallas_call | solution.py:108
  705.8 4.8 add_convert_fusion.1
  715.7 60.4 %weight_grads.5 = (f32[2240,1536]{1,0:T(8,128)}, f32[2240,1536]{1,0:T(8,128)}, f32[2240,1536]{1,0:T(8,128)}, f32[8,128]{1,0:T(8,128)}) custom-call(bf16[2048,1536]{1,0:T(8,128)(2,1)} %all-gather.12.cloned.1.call-done.refs_0_, bf16[2048,1536]{1,0:T(8,128)(2,1)} %all-gather.14.cloned.1.call-done.refs_1_, bf16[2240,1536]{1,0:T(8,128)(2,1)} %bitcast.64, ...), custom_call_target="tpu_custom_call" | custom-call | flops 48318382080 | bytes 35389440 | tf_op jit(solution)/shard_map/weight_grads/pallas_call | solution.py:108
  785.9 46.5 %weight_grads.6 = (f32[2240,1536]{1,0:T(8,128)}, f32[2240,1536]{1,0:T(8,128)}, f32[2240,1536]{1,0:T(8,128)}, f32[8,128]{1,0:T(8,128)}) custom-call(bf16[2048,1536]{1,0:T(8,128)(2,1)} %all-gather.12.cloned.1.call-done.refs_0_, bf16[2048,1536]{1,0:T(8,128)(2,1)} %all-gather.14.cloned.1.call-done.refs_1_, ...), custom_call_target="tpu_custom_call", output_to_operand_aliasing={{0}: (5, {}), {1}: (6, {}), {2}: (7, {})} | custom-call | flops 36238786560 | bytes 26542080 | tf_op jit(solution)/shard_map/weight_grads/pallas_call | solution.py:108
  832.5 20.4 %weight_grads.7 = (f32[2240,1536]{1,0:T(8,128)}, f32[2240,1536]{1,0:T(8,128)}, f32[2240,1536]{1,0:T(8,128)}, f32[8,128]{1,0:T(8,128)}) custom-call(bf16[2048,1536]{1,0:T(8,128)(2,1)} %all-gather.16.cloned.1.call-done.refs_0_, bf16[2048,1536]{1,0:T(8,128)(2,1)} %all-gather.18.cloned.1.call-done.refs_1_, ...), custom_call_target="tpu_custom_call", output_to_operand_aliasing={{0}: (5, {}), {1}: (6, {}), {2}: (7, {})} | custom-call | flops 12079595520 | bytes 8847360 | tf_op jit(solution)/shard_map/weight_grads/pallas_call | solution.py:108
  860.8 61.3 %weight_grads.8 = (f32[2240,1536]{1,0:T(8,128)}, f32[2240,1536]{1,0:T(8,128)}, f32[2240,1536]{1,0:T(8,128)}, f32[8,128]{1,0:T(8,128)}) custom-call(bf16[2048,1536]{1,0:T(8,128)(2,1)} %all-gather.16.cloned.1.call-done.refs_0_, bf16[2048,1536]{1,0:T(8,128)(2,1)} %all-gather.18.cloned.1.call-done.refs_1_, ...), custom_call_target="tpu_custom_call", output_to_operand_aliasing={{0}: (5, {}), {1}: (6, {}), {2}: (7, {})} | custom-call | flops 48318382080 | bytes 35389440 | tf_op jit(solution)/shard_map/weight_grads/pallas_call | solution.py:108
  922.2 34.4 %weight_grads.9 = (f32[2240,1536]{1,0:T(8,128)}, f32[2240,1536]{1,0:T(8,128)}, f32[2240,1536]{1,0:T(8,128)}, f32[8,128]{1,0:T(8,128)}) custom-call(bf16[2048,1536]{1,0:T(8,128)(2,1)} %all-gather.16.cloned.1.call-done.refs_0_, bf16[2048,1536]{1,0:T(8,128)(2,1)} %all-gather.18.cloned.1.call-done.refs_1_, ...), custom_call_target="tpu_custom_call", output_to_operand_aliasing={{0}: (5, {}), {1}: (6, {}), {2}: (7, {})} | custom-call | flops 24159191040 | bytes 17694720 | tf_op jit(solution)/shard_map/weight_grads/pallas_call | solution.py:108
  (979 shorter events, 385.2 us)
Async XLA Ops:
  7.2 51.6 %all-gather.20.cloned.1.call-start = ((), (), s32[]{:S(2)}) async-start(), calls=%async_computation.4 | async-start | bytes 7864320 | tf_op jit(solution)/shard_map/all_gather | solution.py:827
  7.9 102.2 %all-gather.22.cloned.1.call-start = ((), (), s32[]{:S(2)}) async-start(), calls=%async_computation.5 | async-start | bytes 5898240 | tf_op jit(solution)/shard_map/all_gather | solution.py:827
  10.7 20.5 %collective-permute-start = (bf16[64,1536]{1,0:T(8,128)(2,1)S(1)}, bf16[64,1536]{1,0:T(8,128)(2,1)S(1)}, u32[]{:S(2)}, u32[]{:S(2)}) collective-permute-start(bf16[64,1536]{1,0:T(8,128)(2,1)S(1)} %select_n.467.refs_8_.refs_1_), channel_id=1, source_target_pairs={{0,2},{1,3},{2,0},{3,1},{4,6},{5,7},{6,4},{7,5},{8,10},{9,11},{10,... | collective-permute-start | bytes 589832 | tf_op jit(solution)/shard_map/ppermute | solution.py:64
  13.7 18.2 %collective-permute-start.1 = (bf16[64,1536]{1,0:T(8,128)(2,1)S(1)}, bf16[64,1536]{1,0:T(8,128)(2,1)S(1)}, u32[]{:S(2)}, u32[]{:S(2)}) collective-permute-start(bf16[64,1536]{1,0:T(8,128)(2,1)S(1)} %select_n.467.refs_8_.refs_1_), channel_id=1, source_target_pairs={{0,1},{1,0},{2,3},{3,2},{4,5},{5,4},{6,7},{7,6},{8,9},{9,8},{10,11... | collective-permute-start | bytes 589832 | tf_op jit(solution)/shard_map/ppermute | solution.py:64
  13.8 17.8 %collective-permute-start.3 = (bf16[64,1536]{1,0:T(8,128)(2,1)S(1)}, bf16[64,1536]{1,0:T(8,128)(2,1)S(1)}, u32[]{:S(2)}, u32[]{:S(2)}) collective-permute-start(bf16[64,1536]{1,0:T(8,128)(2,1)S(1)} %select_n.469.refs_8_.refs_1_), channel_id=1, source_target_pairs={{0,2},{1,3},{2,0},{3,1},{4,6},{5,7},{6,4},{7,5},{8,10},{9,11},{10,... | collective-permute-start | bytes 589832 | tf_op jit(solution)/shard_map/ppermute | solution.py:64
  14.0 18.0 %collective-permute-start.4 = (bf16[64,1536]{1,0:T(8,128)(2,1)S(1)}, bf16[64,1536]{1,0:T(8,128)(2,1)S(1)}, u32[]{:S(2)}, u32[]{:S(2)}) collective-permute-start(bf16[64,1536]{1,0:T(8,128)(2,1)S(1)} %select_n.469.refs_8_.refs_1_), channel_id=1, source_target_pairs={{0,1},{1,0},{2,3},{3,2},{4,5},{5,4},{6,7},{7,6},{8,9},{9,8},{10,11... | collective-permute-start | bytes 589832 | tf_op jit(solution)/shard_map/ppermute | solution.py:64
  14.5 701.2 %all-gather.12.cloned.1.call-start = ((), (), s32[]{:S(2)}) async-start(), calls=%async_computation | async-start | bytes 6684672 | tf_op jit(solution)/shard_map/all_gather | solution.py:890
  81.0 19.6 %collective-permute-start.34 = (bf16[256,512]{1,0:T(8,128)(2,1)S(1)}, bf16[256,512]{1,0:T(8,128)(2,1)S(1)}, u32[]{:S(2)}, u32[]{:S(2)}) collective-permute-start(bf16[256,512]{1,0:T(8,128)(2,1)S(1)} %constant_dynamic-update-slice_fusion.8.refs_5_.refs_14_), channel_id=1, source_target_pairs={{0,2},{1,3},{2,0},{3,1},{4,6},{5,7},{6,4},{7,5},{8,10},{9,11},{10,... | collective-permute-start | bytes 786440 | tf_op jit(solution)/shard_map/ppermute | solution.py:64
  83.5 26.7 %collective-permute-start.10 = (bf16[256,512]{1,0:T(8,128)(2,1)S(1)}, bf16[256,512]{1,0:T(8,128)(2,1)S(1)}, u32[]{:S(2)}, u32[]{:S(2)}) collective-permute-start(bf16[256,512]{1,0:T(8,128)(2,1)S(1)} %constant_dynamic-update-slice_fusion.refs_5_.refs_14_), channel_id=1, source_target_pairs={{0,1},{1,0},{2,3},{3,2},{4,5},{5,4},{6,7},{7,6},{8,9},{9,8},{10,11... | collective-permute-start | bytes 786440 | tf_op jit(solution)/shard_map/ppermute | solution.py:64
  90.2 19.9 %collective-permute-start.11 = (bf16[256,512]{1,0:T(8,128)(2,1)S(1)}, bf16[256,512]{1,0:T(8,128)(2,1)S(1)}, u32[]{:S(2)}, u32[]{:S(2)}) collective-permute-start(bf16[256,512]{1,0:T(8,128)(2,1)S(1)} %collective-permute-done.9.refs_6_.refs_16_), channel_id=1, source_target_pairs={{0,1},{1,0},{2,3},{3,2},{4,5},{5,4},{6,7},{7,6},{8,9},{9,8},{10,11... | collective-permute-start | bytes 786440 | tf_op jit(solution)/shard_map/ppermute | solution.py:64
  90.2 25.9 %collective-permute-start.35 = (bf16[256,512]{1,0:T(8,128)(2,1)S(1)}, bf16[256,512]{1,0:T(8,128)(2,1)S(1)}, u32[]{:S(2)}, u32[]{:S(2)}) collective-permute-start(bf16[256,512]{1,0:T(8,128)(2,1)S(1)} %constant_dynamic-update-slice_fusion.8.refs_5_.refs_14_), channel_id=1, source_target_pairs={{0,1},{1,0},{2,3},{3,2},{4,5},{5,4},{6,7},{7,6},{8,9},{9,8},{10,11... | collective-permute-start | bytes 786440 | tf_op jit(solution)/shard_map/ppermute | solution.py:64
  100.6 15.5 %collective-permute-start.36 = (bf16[256,512]{1,0:T(8,128)(2,1)S(1)}, bf16[256,512]{1,0:T(8,128)(2,1)S(1)}, u32[]{:S(2)}, u32[]{:S(2)}) collective-permute-start(bf16[256,512]{1,0:T(8,128)(2,1)S(1)} %collective-permute-done.34.refs_6_.refs_16_), channel_id=1, source_target_pairs={{0,1},{1,0},{2,3},{3,2},{4,5},{5,4},{6,7},{7,6},{8,9},{9,8},{10,11... | collective-permute-start | bytes 786440 | tf_op jit(solution)/shard_map/ppermute | solution.py:64
  283.2 432.4 %all-gather.14.cloned.1.call-start = ((), (), s32[]{:S(2)}) async-start(), calls=%async_computation.1 | async-start | bytes 6684672 | tf_op jit(solution)/shard_map/all_gather | solution.py:890
  320.0 21.0 %collective-permute-start.101 = (bf16[64,1536]{1,0:T(8,128)(2,1)S(1)}, bf16[64,1536]{1,0:T(8,128)(2,1)S(1)}, u32[]{:S(2)}, u32[]{:S(2)}) collective-permute-start(bf16[64,1536]{1,0:T(8,128)(2,1)S(1)} %get-tuple-element.264), channel_id=1, source_target_pairs={{0,1},{1,0},{2,3},{3,2},{4,5},{5,4},{6,7},{7,6},{8,9},{9,8},{10,11... | collective-permute-start | bytes 589832 | tf_op jit(solution)/shard_map/ppermute | solution.py:64
  321.8 19.3 %collective-permute-start.103 = (bf16[64,1536]{1,0:T(8,128)(2,1)S(1)}, bf16[64,1536]{1,0:T(8,128)(2,1)S(1)}, u32[]{:S(2)}, u32[]{:S(2)}) collective-permute-start(bf16[64,1536]{1,0:T(8,128)(2,1)S(1)} %add_convert_fusion.21), channel_id=1, source_target_pairs={{0,2},{1,3},{2,0},{3,1},{4,6},{5,7},{6,4},{7,5},{8,10},{9,11},{10,... | collective-permute-start | bytes 589832 | tf_op jit(solution)/shard_map/ppermute | solution.py:64
  373.9 16.8 %collective-permute-start.75 = (bf16[64,1536]{1,0:T(8,128)(2,1)S(1)}, bf16[64,1536]{1,0:T(8,128)(2,1)}, u32[]{:S(2)}, u32[]{:S(2)}) collective-permute-start(bf16[64,1536]{1,0:T(8,128)(2,1)S(1)} %get-tuple-element.243), channel_id=1, source_target_pairs={{16,0},{17,1},{18,2},{19,3},{20,4},{21,5},{22,6},{23,7},{24,8},{25... | collective-permute-start | bytes 589832 | tf_op jit(solution)/shard_map/ppermute | solution.py:70
  398.6 433.9 %all-gather.16.cloned.1.call-start = ((), (), s32[]{:S(2)}) async-start(), calls=%async_computation.2 | async-start | bytes 6684672 | tf_op jit(solution)/shard_map/all_gather | solution.py:890
  399.4 433.0 %all-gather.18.cloned.1.call-start = ((), (), s32[]{:S(2)}) async-start(), calls=%async_computation.3 | async-start | bytes 6684672 | tf_op jit(solution)/shard_map/all_gather | solution.py:890
  401.6 17.7 %collective-permute-start.98 = (bf16[64,1536]{1,0:T(8,128)(2,1)S(1)}, bf16[64,1536]{1,0:T(8,128)(2,1)S(1)}, u32[]{:S(2)}, u32[]{:S(2)}) collective-permute-start(bf16[64,1536]{1,0:T(8,128)(2,1)S(1)} %get-tuple-element.262.refs_5_.refs_0_), channel_id=1, source_target_pairs={{0,2},{1,3},{2,0},{3,1},{4,6},{5,7},{6,4},{7,5},{8,10},{9,11},{10,... | collective-permute-start | bytes 589832 | tf_op jit(solution)/shard_map/ppermute | solution.py:64
  419.3 24.6 %collective-permute-start.99 = (bf16[64,1536]{1,0:T(8,128)(2,1)S(1)}, bf16[64,1536]{1,0:T(8,128)(2,1)S(1)}, u32[]{:S(2)}, u32[]{:S(2)}) collective-permute-start(bf16[64,1536]{1,0:T(8,128)(2,1)S(1)} %get-tuple-element.262.refs_5_.refs_0_), channel_id=1, source_target_pairs={{0,1},{1,0},{2,3},{3,2},{4,5},{5,4},{6,7},{7,6},{8,9},{9,8},{10,11... | collective-permute-start | bytes 589832 | tf_op jit(solution)/shard_map/ppermute | solution.py:64
  419.3 24.7 %collective-permute-start.100 = (bf16[64,1536]{1,0:T(8,128)(2,1)S(1)}, bf16[64,1536]{1,0:T(8,128)(2,1)S(1)}, u32[]{:S(2)}, u32[]{:S(2)}) collective-permute-start(bf16[64,1536]{1,0:T(8,128)(2,1)S(1)} %collective-permute-done.98.refs_7_.refs_1_), channel_id=1, source_target_pairs={{0,1},{1,0},{2,3},{3,2},{4,5},{5,4},{6,7},{7,6},{8,9},{9,8},{10,11... | collective-permute-start | bytes 589832 | tf_op jit(solution)/shard_map/ppermute | solution.py:64
  419.8 24.2 %collective-permute-start.112 = (bf16[64,1536]{1,0:T(8,128)(2,1)S(1)}, bf16[64,1536]{1,0:T(8,128)(2,1)S(1)}, u32[]{:S(2)}, u32[]{:S(2)}) collective-permute-start(bf16[64,1536]{1,0:T(8,128)(2,1)S(1)} %get-tuple-element.380.refs_12_.refs_1_), channel_id=1, source_target_pairs={{0,1},{1,0},{2,3},{3,2},{4,5},{5,4},{6,7},{7,6},{8,9},{9,8},{10,11... | collective-permute-start | bytes 589832 | tf_op jit(solution)/shard_map/ppermute | solution.py:64
  422.1 21.9 %collective-permute-start.113 = (bf16[64,1536]{1,0:T(8,128)(2,1)S(1)}, bf16[64,1536]{1,0:T(8,128)(2,1)S(1)}, u32[]{:S(2)}, u32[]{:S(2)}) collective-permute-start(bf16[64,1536]{1,0:T(8,128)(2,1)S(1)} %collective-permute-done.111.refs_13_), channel_id=1, source_target_pairs={{0,1},{1,0},{2,3},{3,2},{4,5},{5,4},{6,7},{7,6},{8,9},{9,8},{10,11... | collective-permute-start | bytes 589832 | tf_op jit(solution)/shard_map/ppermute | solution.py:64
  456.9 16.7 %collective-permute-start.114 = (bf16[64,1536]{1,0:T(8,128)(2,1)S(1)}, bf16[64,1536]{1,0:T(8,128)(2,1)S(1)}, u32[]{:S(2)}, u32[]{:S(2)}) collective-permute-start(bf16[64,1536]{1,0:T(8,128)(2,1)S(1)} %get-tuple-element.275), channel_id=1, source_target_pairs={{0,1},{1,0},{2,3},{3,2},{4,5},{5,4},{6,7},{7,6},{8,9},{9,8},{10,11... | collective-permute-start | bytes 589832 | tf_op jit(solution)/shard_map/ppermute | solution.py:64
  458.1 15.5 %collective-permute-start.116 = (bf16[64,1536]{1,0:T(8,128)(2,1)S(1)}, bf16[64,1536]{1,0:T(8,128)(2,1)S(1)}, u32[]{:S(2)}, u32[]{:S(2)}) collective-permute-start(bf16[64,1536]{1,0:T(8,128)(2,1)S(1)} %add_convert_fusion.20), channel_id=1, source_target_pairs={{0,2},{1,3},{2,0},{3,1},{4,6},{5,7},{6,4},{7,5},{8,10},{9,11},{10,... | collective-permute-start | bytes 589832 | tf_op jit(solution)/shard_map/ppermute | solution.py:64
  492.3 17.1 %collective-permute-start.86 = (bf16[64,512]{1,0:T(8,128)(2,1)}, bf16[64,512]{1,0:T(8,128)(2,1)}, u32[]{:S(2)}, u32[]{:S(2)}) collective-permute-start(bf16[64,512]{1,0:T(8,128)(2,1)} %get-tuple-element.410), channel_id=1, source_target_pairs={{0,8},{4,12},{8,0},{12,4},{1,9},{5,13},{9,1},{13,5},{2,10},{6,14},... | collective-permute-start | bytes 196616 | tf_op jit(solution)/shard_map/ppermute | solution.py:64
  499.7 23.5 %collective-permute-start.120 = (bf16[64,512]{1,0:T(8,128)(2,1)}, bf16[64,512]{1,0:T(8,128)(2,1)}, u32[]{:S(2)}, u32[]{:S(2)}) collective-permute-start(bf16[64,512]{1,0:T(8,128)(2,1)} %get-tuple-element.419), channel_id=1, source_target_pairs={{0,4},{4,0},{8,12},{12,8},{1,5},{5,1},{9,13},{13,9},{2,6},{6,2},{1... | collective-permute-start | bytes 196616 | tf_op jit(solution)/shard_map/ppermute | solution.py:64
  499.7 23.6 %collective-permute-start.121 = (bf16[64,512]{1,0:T(8,128)(2,1)}, bf16[64,512]{1,0:T(8,128)(2,1)}, u32[]{:S(2)}, u32[]{:S(2)}) collective-permute-start(bf16[64,512]{1,0:T(8,128)(2,1)} %get-tuple-element.418), channel_id=1, source_target_pairs={{0,8},{4,12},{8,0},{12,4},{1,9},{5,13},{9,1},{13,5},{2,10},{6,14},... | collective-permute-start | bytes 196616 | tf_op jit(solution)/shard_map/ppermute | solution.py:64
  500.7 22.6 %collective-permute-start.122 = (bf16[64,512]{1,0:T(8,128)(2,1)}, bf16[64,512]{1,0:T(8,128)(2,1)}, u32[]{:S(2)}, u32[]{:S(2)}) collective-permute-start(bf16[64,512]{1,0:T(8,128)(2,1)} %get-tuple-element.417), channel_id=1, source_target_pairs={{0,12},{4,8},{8,4},{12,0},{1,13},{5,9},{9,5},{13,1},{2,14},{6,10},... | collective-permute-start | bytes 196616 | tf_op jit(solution)/shard_map/ppermute | solution.py:64
  522.0 29.9 %collective-permute-start.126 = (bf16[64,1536]{1,0:T(8,128)(2,1)S(1)}, bf16[64,1536]{1,0:T(8,128)(2,1)}, u32[]{:S(2)}, u32[]{:S(2)}) collective-permute-start(bf16[64,1536]{1,0:T(8,128)(2,1)S(1)} %get-tuple-element.254.refs_7_), channel_id=1, source_target_pairs={{16,0},{17,1},{18,2},{19,3},{20,4},{21,5},{22,6},{23,7},{24,8},{25... | collective-permute-start | bytes 589832 | tf_op jit(solution)/shard_map/ppermute | solution.py:70
  531.7 22.8 %collective-permute-start.139 = (bf16[64,1536]{1,0:T(8,128)(2,1)S(1)}, bf16[64,1536]{1,0:T(8,128)(2,1)S(1)}, u32[]{:S(2)}, u32[]{:S(2)}) collective-permute-start(bf16[64,1536]{1,0:T(8,128)(2,1)S(1)} %get-tuple-element.284.refs_7_), channel_id=1, source_target_pairs={{16,0},{17,1},{18,2},{19,3},{20,4},{21,5},{22,6},{23,7},{24,8},{25... | collective-permute-start | bytes 589832 | tf_op jit(solution)/shard_map/ppermute | solution.py:70
  544.5 100.3 %collective-permute-start.88 = (bf16[64,1536]{1,0:T(8,128)(2,1)}, bf16[64,1536]{1,0:T(8,128)(2,1)}, u32[]{:S(2)}, u32[]{:S(2)}) collective-permute-start(bf16[64,1536]{1,0:T(8,128)(2,1)} %get-tuple-element.256), channel_id=1, source_target_pairs={{0,1},{1,0},{2,3},{3,2},{4,5},{5,4},{6,7},{7,6},{8,9},{9,8},{10,11... | collective-permute-start | bytes 589832 | tf_op jit(solution)/shard_map/ppermute | solution.py:64
  551.8 77.4 %collective-permute-start.124 = (bf16[64,1536]{1,0:T(8,128)(2,1)}, bf16[64,1536]{1,0:T(8,128)(2,1)S(1)}, u32[]{:S(2)}, u32[]{:S(2)}) collective-permute-start(bf16[64,1536]{1,0:T(8,128)(2,1)} %get-tuple-element.288), channel_id=1, source_target_pairs={{0,1},{1,0},{2,3},{3,2},{4,5},{5,4},{6,7},{7,6},{8,9},{9,8},{10,11... | collective-permute-start | bytes 589832 | tf_op jit(solution)/shard_map/ppermute | solution.py:64
  560.5 86.3 %collective-permute-start.90 = (bf16[64,1536]{1,0:T(8,128)(2,1)S(1)}, bf16[64,1536]{1,0:T(8,128)(2,1)S(1)}, u32[]{:S(2)}, u32[]{:S(2)}) collective-permute-start(bf16[64,1536]{1,0:T(8,128)(2,1)S(1)} %add_convert_fusion.23), channel_id=1, source_target_pairs={{0,2},{1,3},{2,0},{3,1},{4,6},{5,7},{6,4},{7,5},{8,10},{9,11},{10,... | collective-permute-start | bytes 589832 | tf_op jit(solution)/shard_map/ppermute | solution.py:64
  563.6 21.2 %collective-permute-start.141 = (bf16[64,1536]{1,0:T(8,128)(2,1)}, bf16[64,1536]{1,0:T(8,128)(2,1)S(1)}, u32[]{:S(2)}, u32[]{:S(2)}) collective-permute-start(bf16[64,1536]{1,0:T(8,128)(2,1)} %copy-done.124), channel_id=1, source_target_pairs={{0,1},{1,0},{2,3},{3,2},{4,5},{5,4},{6,7},{7,6},{8,9},{9,8},{10,11... | collective-permute-start | bytes 589832 | tf_op jit(solution)/shard_map/ppermute | solution.py:64
  563.6 21.3 %collective-permute-start.142 = (bf16[64,1536]{1,0:T(8,128)(2,1)S(1)}, bf16[64,1536]{1,0:T(8,128)(2,1)S(1)}, u32[]{:S(2)}, u32[]{:S(2)}) collective-permute-start(bf16[64,1536]{1,0:T(8,128)(2,1)S(1)} %collective-permute-done.140.refs_9_), channel_id=1, source_target_pairs={{0,1},{1,0},{2,3},{3,2},{4,5},{5,4},{6,7},{7,6},{8,9},{9,8},{10,11... | collective-permute-start | bytes 589832 | tf_op jit(solution)/shard_map/ppermute | solution.py:64
  600.2 20.0 %collective-permute-start.143 = (bf16[64,1536]{1,0:T(8,128)(2,1)S(1)}, bf16[64,1536]{1,0:T(8,128)(2,1)S(1)}, u32[]{:S(2)}, u32[]{:S(2)}) collective-permute-start(bf16[64,1536]{1,0:T(8,128)(2,1)S(1)} %get-tuple-element.301), channel_id=1, source_target_pairs={{0,1},{1,0},{2,3},{3,2},{4,5},{5,4},{6,7},{7,6},{8,9},{9,8},{10,11... | collective-permute-start | bytes 589832 | tf_op jit(solution)/shard_map/ppermute | solution.py:64
  651.1 29.5 %collective-permute-start.123 = (bf16[64,1536]{1,0:T(8,128)(2,1)S(1)}, bf16[64,1536]{1,0:T(8,128)(2,1)S(1)}, u32[]{:S(2)}, u32[]{:S(2)}) collective-permute-start(bf16[64,1536]{1,0:T(8,128)(2,1)S(1)} %copy-done.191), channel_id=1, source_target_pairs={{0,1},{1,0},{2,3},{3,2},{4,5},{5,4},{6,7},{7,6},{8,9},{9,8},{10,11... | collective-permute-start | bytes 589832 | tf_op jit(solution)/shard_map/ppermute | solution.py:64
  651.2 29.4 %collective-permute-start.125 = (bf16[64,1536]{1,0:T(8,128)(2,1)S(1)}, bf16[64,1536]{1,0:T(8,128)(2,1)S(1)}, u32[]{:S(2)}, u32[]{:S(2)}) collective-permute-start(bf16[64,1536]{1,0:T(8,128)(2,1)S(1)} %add_convert_fusion.19), channel_id=1, source_target_pairs={{0,2},{1,3},{2,0},{3,1},{4,6},{5,7},{6,4},{7,5},{8,10},{9,11},{10,... | collective-permute-start | bytes 589832 | tf_op jit(solution)/shard_map/ppermute | solution.py:64
  680.4 25.3 %collective-permute-start.157 = (bf16[384,3584]{1,0:T(8,128)(2,1)}, bf16[384,3584]{1,0:T(8,128)(2,1)}, u32[]{:S(2)}, u32[]{:S(2)}) collective-permute-start(bf16[384,3584]{1,0:T(8,128)(2,1)} %get-tuple-element.356), channel_id=1, source_target_pairs={{0,1},{1,0},{2,3},{3,2},{4,5},{5,4},{6,7},{7,6},{8,9},{9,8},{10,11... | collective-permute-start | bytes 8257544 | tf_op jit(solution)/shard_map/ppermute | solution.py:64
  687.9 23.8 %collective-permute-start.156 = (bf16[384,3584]{1,0:T(8,128)(2,1)}, bf16[384,3584]{1,0:T(8,128)(2,1)}, u32[]{:S(2)}, u32[]{:S(2)}) collective-permute-start(bf16[384,3584]{1,0:T(8,128)(2,1)} %copy-done.161), channel_id=1, source_target_pairs={{0,1},{1,0},{2,3},{3,2},{4,5},{5,4},{6,7},{7,6},{8,9},{9,8},{10,11... | collective-permute-start | bytes 8257544 | tf_op jit(solution)/shard_map/ppermute | solution.py:64
  710.5 66.7 %collective-permute-start.158 = (bf16[384,3584]{1,0:T(8,128)(2,1)}, bf16[384,3584]{1,0:T(8,128)(2,1)}, u32[]{:S(2)}, u32[]{:S(2)}) collective-permute-start(bf16[384,3584]{1,0:T(8,128)(2,1)} %add_convert_fusion.1), channel_id=1, source_target_pairs={{0,2},{1,3},{2,0},{3,1},{4,6},{5,7},{6,4},{7,5},{8,10},{9,11},{10,... | collective-permute-start | bytes 8257544 | tf_op jit(solution)/shard_map/ppermute | solution.py:64
  781.5 72.5 %collective-permute-start.159 = (bf16[96,3584]{1,0:T(8,128)(2,1)S(1)}, bf16[96,3584]{1,0:T(8,128)(2,1)S(1)}, u32[]{:S(2)}, u32[]{:S(2)}) collective-permute-start(bf16[96,3584]{1,0:T(8,128)(2,1)S(1)} %get-tuple-element.392), channel_id=1, source_target_pairs={{0,4},{4,0},{8,12},{12,8},{1,5},{5,1},{9,13},{13,9},{2,6},{6,2},{1... | collective-permute-start | bytes 2064392 | tf_op jit(solution)/shard_map/ppermute | solution.py:64
  782.2 71.8 %collective-permute-start.160 = (bf16[96,3584]{1,0:T(8,128)(2,1)S(1)}, bf16[96,3584]{1,0:T(8,128)(2,1)}, u32[]{:S(2)}, u32[]{:S(2)}) collective-permute-start(bf16[96,3584]{1,0:T(8,128)(2,1)S(1)} %get-tuple-element.391), channel_id=1, source_target_pairs={{0,8},{4,12},{8,0},{12,4},{1,9},{5,13},{9,1},{13,5},{2,10},{6,14},... | collective-permute-start | bytes 2064392 | tf_op jit(solution)/shard_map/ppermute | solution.py:64
  783.2 70.8 %collective-permute-start.161 = (bf16[96,3584]{1,0:T(8,128)(2,1)S(1)}, bf16[96,3584]{1,0:T(8,128)(2,1)}, u32[]{:S(2)}, u32[]{:S(2)}) collective-permute-start(bf16[96,3584]{1,0:T(8,128)(2,1)S(1)} %get-tuple-element.390), channel_id=1, source_target_pairs={{0,12},{4,8},{8,4},{12,0},{1,13},{5,9},{9,5},{13,1},{2,14},{6,10},... | collective-permute-start | bytes 2064392 | tf_op jit(solution)/shard_map/ppermute | solution.py:64
  856.4 100.2 %collective-permute-start.162 = (bf16[96,3584]{1,0:T(8,128)(2,1)S(1)}, bf16[96,3584]{1,0:T(8,128)(2,1)S(1)}, u32[]{:S(2)}, u32[]{:S(2)}) collective-permute-start(bf16[96,3584]{1,0:T(8,128)(2,1)S(1)} %add_convert_fusion.3.refs_8_.refs_1_), channel_id=1, source_target_pairs={{0,4},{4,0},{8,12},{12,8},{1,5},{5,1},{9,13},{13,9},{2,6},{6,2},{1... | collective-permute-start | bytes 2064392 | tf_op jit(solution)/shard_map/ppermute | solution.py:64
  856.4 100.2 %collective-permute-start.163 = (bf16[96,3584]{1,0:T(8,128)(2,1)S(1)}, bf16[96,3584]{1,0:T(8,128)(2,1)S(1)}, u32[]{:S(2)}, u32[]{:S(2)}) collective-permute-start(bf16[96,3584]{1,0:T(8,128)(2,1)S(1)} %add_convert_fusion.3.refs_8_.refs_1_), channel_id=1, source_target_pairs={{0,8},{4,12},{8,0},{12,4},{1,9},{5,13},{9,1},{13,5},{2,10},{6,14},... | collective-permute-start | bytes 2064392 | tf_op jit(solution)/shard_map/ppermute | solution.py:64
  858.1 98.5 %collective-permute-start.164 = (bf16[96,3584]{1,0:T(8,128)(2,1)S(1)}, bf16[96,3584]{1,0:T(8,128)(2,1)S(1)}, u32[]{:S(2)}, u32[]{:S(2)}) collective-permute-start(bf16[96,3584]{1,0:T(8,128)(2,1)S(1)} %add_convert_fusion.3.refs_8_.refs_1_), channel_id=1, source_target_pairs={{0,12},{4,8},{8,4},{12,0},{1,13},{5,9},{9,5},{13,1},{2,14},{6,10},... | collective-permute-start | bytes 2064392 | tf_op jit(solution)/shard_map/ppermute | solution.py:64
  (340 other events, 4704.5 us)
Sparse Core Ops, SparseCore 0:
  9.6 49.1 all-gather.19
  60.3 49.7 all-gather.21
  283.3 70.3 all-gather.11
  398.7 63.4 all-gather.13
  464.3 69.1 all-gather.15
  556.0 67.4 all-gather.17

commit v3 on v2

v3 whole, which is shorter than its diff:
```python
import functools
import math

import jax
import jax.numpy as jnp
from jax import lax
from jax.experimental import pallas as pl
from jax.experimental.pallas import tpu as pltpu
from jax.sharding import PartitionSpec as P

HEADS = 12
KV_HEADS = 2
HEAD_DIM = 128
GROUP = HEADS // KV_HEADS
EPS = 1e-06
ROPE_BASE = 1000000.0
NEGATIVE = -1e30
QCOLS = HEADS * HEAD_DIM
KCOLS = KV_HEADS * HEAD_DIM
SCALE = HEAD_DIM ** (-0.5)

MICROS = 2
LAG = 1
FORWARD = "KJQAMRY"
SEQUENCE = (
    "K0 J0 Q0 A0 H M0 R0 Y0 K1 Q1 J1 A1 H M1 R1 "
    "B0 Y1 S0 K2 T0 D0 J2 Q2 E0 P0 A2 G1 H "
    "B1 S1 T1 D1 E1 P1 G2 H B2 M2 S2 T2 D2 E2 P2 "
)
ROWS = 16
UNITS = 512

f32 = jnp.float32
bf16 = jnp.bfloat16
MIB = 1 << 20


def dot_nn(a, b):
    return lax.dot_general(a, b, (((1,), (0,)), ((), ())), preferred_element_type=f32)


def dot_nt(a, b):
    return lax.dot_general(a, b, (((1,), (1,)), ((), ())), preferred_element_type=f32)


def dot_tn(a, b):
    return lax.dot_general(a, b, (((0,), (0,)), ((), ())), preferred_element_type=f32)


def inverse_rms(values):
    return lax.rsqrt(jnp.mean(values * values, axis=-1, keepdims=True) + EPS)


def norm_backward(grad_normed, values, gain):
    inverse = inverse_rms(values)
    scaled = grad_normed * gain
    grad_values = inverse * scaled - values * (
        inverse**3 * jnp.mean(scaled * values, axis=-1, keepdims=True)
    )
    grad_gain = jnp.sum(grad_normed * values * inverse, axis=0, keepdims=True)
    return grad_values, grad_gain


def exchange(block, axis, mask):
    size = lax.axis_size(axis)
    return lax.ppermute(block, axis, [(i, i ^ mask) for i in range(size)])


def passed_along(block, axis, distance):
    devices = range(lax.axis_size(axis))
    route = [(i - distance, i) for i in devices if i - distance in devices]
    return lax.ppermute(block, axis, route)


def bits_of(size):
    return [1 << b for b in reversed(range(size.bit_length() - 1))]


def relative_order(size):
    order = [0]
    for bit in bits_of(size):
        order = order + [r ^ bit for r in order]
    return order


def gather_pieces(block, axis):
    pieces = [block]
    for bit in bits_of(lax.axis_size(axis)):
        pieces = pieces + [exchange(p, axis, bit) for p in pieces]
    return pieces


def reduction(near, far_half, axis, total):
    terms = [near]
    sent = far_half
    extent = near.shape[0]
    bits = bits_of(lax.axis_size(axis))[::-1]
    for k, bit in enumerate(bits):
        if k > 0:
            extent //= 2
            sent = total(terms, extent)
        terms.append(exchange(sent, axis, bit))
        yield
    return terms


ORDER = []


def call(
    kernel, out_shape, args, flops, moved, name, in_specs, limit=24, after=(), ordered=True, **kwargs
):
    waits = [*after, *(ORDER if ordered else ())]

    def body(*refs):
        kernel(*refs[len(waits) :])

    result = pl.pallas_call(
        body,
        out_shape=out_shape,
        in_specs=[*[ANY] * len(waits), *in_specs],
        compiler_params=pltpu.CompilerParams(vmem_limit_bytes=limit * MIB),
        cost_estimate=pl.CostEstimate(flops=flops, bytes_accessed=moved, transcendentals=0),
        name=name,
        **kwargs,
    )(*waits, *args)
    if ordered:
        ORDER[:] = [result[0] if isinstance(result, (tuple, list)) else result]
    return result


ANY = pl.BlockSpec(memory_space=pl.ANY)
VMEM = pl.BlockSpec(memory_space=pltpu.VMEM)
SMEM = pl.BlockSpec(memory_space=pltpu.SMEM)


def hold_kernel(count, *refs):
    copies = [
        pltpu.make_async_copy(refs[k], refs[count + k], refs[-1].at[k]) for k in range(count)
    ]
    for copy in copies:
        copy.start()
    wait_all(copies)


def hold(*arrays):
    return call(
        functools.partial(hold_kernel, len(arrays)),
        tuple(pltpu.VMEM(a.shape, a.dtype) for a in arrays),
        [far(a) for a in arrays],
        0,
        2 * sum(a.size for a in arrays),
        "hold",
        limit=4,
        in_specs=[ANY] * len(arrays),
        out_specs=tuple(VMEM for _ in arrays),
        scratch_shapes=[pltpu.SemaphoreType.DMA((len(arrays),))],
    )


def held(array):
    return pltpu.with_memory_space_constraint(array, pltpu.VMEM)


def far(array):
    return pltpu.with_memory_space_constraint(array, pltpu.HBM)


def bring(marks_ref, sources, targets, sem):
    copies = []
    for k, (source, target) in enumerate(zip(sources, targets)):
        if len(source) == 1:
            copy = pltpu.make_async_copy(source[0], target, sem.at[k])
            copy.start()
        else:
            for is_first, ref in zip((1, 0), source):
                copy = pltpu.make_async_copy(ref, target, sem.at[k])
                pl.when(marks_ref[0] == is_first)(copy.start)
        copies.append(copy)
    return copies


def taken(refs, counts):
    groups = []
    for count in counts:
        groups.append(refs[:count])
        refs = refs[count:]
    return groups, refs


def turn(value, cos, sin):
    return value * cos + pltpu.roll(value, HEAD_DIM // 2, 1) * sin


def repeat_rows(table, count):
    return table if count == 1 else jnp.concatenate([table] * count, axis=0)


def choose(marks_ref, refs):
    if len(refs) == 1:
        return refs[0][...]
    return jnp.where(marks_ref[0] == 1, refs[0][...], refs[1][...])


def weight_copies(starts_ref, pieces, target, sem, tile=None):
    columns = target.shape[1]
    tile = tile or columns
    tiles = []
    for k in range(columns // tile):
        copies = []
        for r, piece in enumerate(pieces):
            at = pl.multiple_of(starts_ref[r] * ROWS, ROWS)
            there = target.at[pl.ds(at, piece.shape[0]), pl.ds(k * tile, tile)]
            copy = pltpu.make_async_copy(piece.at[:, pl.ds(k * tile, tile)], there, sem.at[k, r])
            copy.start()
            copies.append(copy)
        tiles.append(copies)
    return tiles


def wait_all(copies):
    for copy in copies:
        copy.wait()


def project_kernel(reps, versions, pieces, turned_heads, tile, *refs):
    (fixed, w_refs, x_refs), rest = taken(refs, (6, pieces, versions))
    marks_ref, starts_ref, gain_ref, b_ref, cos_ref, sin_ref = fixed
    out_ref, n_ref, w_ref, sem = rest[-4:]
    tiles = weight_copies(starts_ref, w_refs, w_ref, sem, tile)
    x = choose(marks_ref, x_refs).astype(f32)
    n_ref[...] = (x * inverse_rms(x) * gain_ref[...].astype(f32)).astype(bf16)
    cos = repeat_rows(cos_ref[...], reps)
    sin = repeat_rows(sin_ref[...], reps)
    for k, copies in enumerate(tiles):
        here = slice(k * tile, (k + 1) * tile)
        wait_all(copies)
        projected = dot_nn(n_ref[...], w_ref[:, here]) + b_ref[:, here].astype(f32)
        turned = []
        for j in range(tile // HEAD_DIM):
            part = projected[:, j * HEAD_DIM : (j + 1) * HEAD_DIM]
            head = k * tile // HEAD_DIM + j
            turned.append(turn(part, cos, sin) if head < turned_heads else part)
        out_ref[:, here] = jnp.concatenate(turned, axis=1).astype(bf16)


def project(marks, xs, gain, weight, b, cos, sin, reps, turned_heads, after=()):
    w_pieces, starts = weight
    tokens, width = xs[0].shape
    columns = w_pieces[0].shape[1]
    tile = 2 * KCOLS
    count = len(w_pieces)
    return call(
        functools.partial(project_kernel, reps, len(xs), count, turned_heads, tile),
        jax.ShapeDtypeStruct((tokens, columns), bf16),
        (marks, starts, gain, b, cos, sin, *(far(w) for w in w_pieces), *xs),
        2 * tokens * width * columns,
        2 * width * columns,
        "project",
        limit=16,
        in_specs=[SMEM] * 2 + [VMEM] * 4 + [ANY] * count + [VMEM] * len(xs),
        after=after,
        out_specs=VMEM,
        scratch_shapes=[
            pltpu.VMEM((tokens, width), bf16),
            pltpu.VMEM((width, columns), bf16),
            pltpu.SemaphoreType.DMA((columns // tile, count)),
        ],
    )


def head_rows(block, g):
    return jnp.concatenate(
        [
            block[:, (g * GROUP + j) * HEAD_DIM : (g * GROUP + j + 1) * HEAD_DIM]
            for j in range(GROUP)
        ],
        axis=0,
    )


def head_columns(rows, tokens):
    return [rows[j * tokens : (j + 1) * tokens] for j in range(GROUP)]


def key_rows(ref, seq, reps, tokens, column):
    columns = slice(column * HEAD_DIM, (column + 1) * HEAD_DIM)
    if reps == 1:
        return ref[:, columns]
    stride = reps * tokens
    return jnp.concatenate(
        [
            ref[a * stride + seq * tokens : a * stride + (seq + 1) * tokens, columns]
            for a in range(ref.shape[0] // stride)
        ],
        axis=0,
    )


def masked_scores(q, key_block, mask, tokens):
    scores = dot_nt(q, key_block) * SCALE
    keys = scores.shape[1]
    return (scores.reshape(GROUP, tokens, keys) + mask[None]).reshape(GROUP * tokens, keys)


def attend_kernel(pieces, weights, reps, versions, *refs):
    (fixed, ow_refs, kv_refs, x_refs), rest = taken(refs, (5, weights, pieces, versions))
    marks_ref, starts_ref, q_ref, mask_ref, gain_ref = fixed
    att_ref, hid_ref, n2_ref, ow_ref, sem = rest[-5:]
    (weights_in,) = weight_copies(starts_ref, ow_refs, ow_ref, sem)
    tokens = q_ref.shape[0] // reps
    for seq in range(reps):
        rows = slice(seq * tokens, (seq + 1) * tokens)
        q_all = q_ref[rows, :]
        for g in range(KV_HEADS):
            q = head_rows(q_all, g)
            scores = [
                masked_scores(q, key_rows(kv, seq, reps, tokens, g), mask_ref[p], tokens)
                for p, kv in enumerate(kv_refs)
            ]
            top = functools.reduce(
                jnp.maximum, [jnp.max(s, axis=-1, keepdims=True) for s in scores]
            )
            total = jnp.zeros_like(top)
            acc = jnp.zeros((GROUP * tokens, HEAD_DIM), f32)
            for s, kv in zip(scores, kv_refs):
                weights = jnp.exp(s - top)
                total = total + jnp.sum(weights, axis=-1, keepdims=True)
                acc = acc + dot_nn(
                    weights.astype(bf16), key_rows(kv, seq, reps, tokens, KV_HEADS + g)
                )
            low = (acc / total).astype(bf16)
            for j, block in enumerate(head_columns(low, tokens)):
                head = g * GROUP + j
                att_ref[rows, head * HEAD_DIM : (head + 1) * HEAD_DIM] = block
    wait_all(weights_in)
    hidden = choose(marks_ref, x_refs).astype(f32) + dot_nn(att_ref[...], ow_ref[...])
    hid_ref[...] = hidden
    n2_ref[...] = (hidden * inverse_rms(hidden) * gain_ref[...].astype(f32)).astype(bf16)


def attend(marks, q, xs, mask, weight, gain, kv_pieces, reps, after=()):
    ow_pieces, starts = weight
    tokens, width = xs[0].shape
    keys = sum(p.shape[0] for p in kv_pieces)
    return call(
        functools.partial(attend_kernel, len(kv_pieces), len(ow_pieces), reps, len(xs)),
        (
            jax.ShapeDtypeStruct((tokens, QCOLS), bf16),
            jax.ShapeDtypeStruct((tokens, width), f32),
            jax.ShapeDtypeStruct((tokens, width), bf16),
        ),
        (marks, starts, q, mask, gain, *(far(w) for w in ow_pieces), *kv_pieces, *xs),
        2 * tokens * QCOLS * width + 12 * tokens * QCOLS * keys // reps,
        4 * keys * KCOLS + 12 * tokens * width,
        "attend",
        limit=16 + 24 * keys // (reps * 4096),
        in_specs=[SMEM] * 2
        + [VMEM] * 3
        + [ANY] * len(ow_pieces)
        + [VMEM] * (len(kv_pieces) + len(xs)),
        after=after,
        out_specs=(VMEM,) * 3,
        scratch_shapes=[
            pltpu.VMEM((QCOLS, width), bf16),
            pltpu.SemaphoreType.DMA((1, len(ow_pieces))),
        ],
    )


def fill(scratch, refs):
    size = refs[0].shape[0]
    for p, ref in enumerate(refs):
        scratch[p * size : (p + 1) * size, :] = ref[...]


def spread(out_refs, acc_ref):
    fill_from = 0
    for ref in out_refs:
        ref[...] = acc_ref[fill_from : fill_from + ref.shape[0], :].astype(bf16)
        fill_from += ref.shape[0]


def unit_spans(units):
    return [slice(at, min(at + UNITS, units)) for at in range(0, units, UNITS)]


def mlp_kernel(pieces, *refs):
    n_refs = refs[:pieces]
    gate_ref, up_ref, down_ref = refs[pieces : pieces + 3]
    out_refs = refs[-4:-2]
    cat_ref, acc_ref = refs[-2:]
    fill(cat_ref, n_refs)
    for k, here in enumerate(unit_spans(gate_ref.shape[0])):
        rows = cat_ref[...]
        gate_pre = dot_nt(rows, gate_ref[here, :])
        up_pre = dot_nt(rows, up_ref[here, :])
        activated = (jax.nn.sigmoid(gate_pre) * gate_pre * up_pre).astype(bf16)
        term = dot_nn(activated, down_ref[here, :])
        if k == 0:
            acc_ref[...] = term
        else:
            acc_ref[...] += term
    spread(out_refs, acc_ref)


def mlp(n_pieces, gate, up, down, after=()):
    units, width = gate.shape
    tokens = n_pieces[0].shape[0]
    count = len(n_pieces)
    return call(
        functools.partial(mlp_kernel, count),
        (jax.ShapeDtypeStruct((count // 2 * tokens, width), bf16),) * 2,
        (*n_pieces, held(gate), held(up), held(down)),
        6 * count * tokens * width * units,
        4 * count * tokens * width,
        "mlp",
        limit=12 * max(1, count * tokens // 512),
        in_specs=[VMEM] * (count + 3),
        after=after,
        out_specs=(VMEM,) * 2,
        scratch_shapes=[
            pltpu.VMEM((count * tokens, width), bf16),
            pltpu.VMEM((count * tokens, width), f32),
        ],
    )


def swiglu_backward(gate_pre, up_pre, grad_act):
    sigmoid = jax.nn.sigmoid(gate_pre)
    silu = gate_pre * sigmoid
    grad_gate = (grad_act * up_pre * (sigmoid + silu * (1.0 - sigmoid))).astype(bf16)
    grad_up = (grad_act * silu).astype(bf16)
    return silu, grad_gate, grad_up


def mlp_back_kernel(pieces, versions, *refs):
    (flags, weights, n_refs, g_refs), rest = taken(
        refs, (1, 3, pieces * versions, pieces)
    )
    gate_ref, up_ref, down_ref = weights
    out_refs = rest[-6:-4]
    cat_ref, gcat_ref, acc_ref, sem = rest[-4:]
    size = cat_ref.shape[0] // pieces
    spans = [pl.ds(p * size, size) for p in range(pieces)]
    sources = [n_refs[p * versions : (p + 1) * versions] for p in range(pieces)]
    copies = bring(
        flags[0],
        sources + [(g,) for g in g_refs],
        [cat_ref.at[span] for span in spans] + [gcat_ref.at[span] for span in spans],
        sem,
    )
    for copy in copies:
        copy.wait()
    for k, here in enumerate(unit_spans(gate_ref.shape[0])):
        rows = cat_ref[...]
        gate_pre = dot_nt(rows, gate_ref[here, :])
        up_pre = dot_nt(rows, up_ref[here, :])
        grad_act = dot_nt(gcat_ref[...], down_ref[here, :])
        _, grad_gate, grad_up = swiglu_backward(gate_pre, up_pre, grad_act)
        term = dot_nn(grad_gate, gate_ref[here, :]) + dot_nn(grad_up, up_ref[here, :])
        if k == 0:
            acc_ref[...] = term
        else:
            acc_ref[...] += term
    spread(out_refs, acc_ref)


def mlp_back(flag, n_versions, g_pieces, gate, up, down, after):
    units, width = gate.shape
    tokens = g_pieces[0].shape[0]
    count = len(g_pieces)
    versions = len(n_versions[0])
    n_arrays = [far(array) for piece in n_versions for array in piece]
    return call(
        functools.partial(mlp_back_kernel, count, versions),
        (jax.ShapeDtypeStruct((count // 2 * tokens, width), bf16),) * 2,
        (flag, held(gate), held(up), held(down), *n_arrays, *g_pieces),
        10 * count * tokens * width * units,
        6 * count * tokens * width,
        "mlp_back",
        limit=16 * max(1, count * tokens // 512),
        in_specs=[SMEM] + [VMEM] * 3 + [ANY] * (len(n_arrays) + count),
        after=after,
        out_specs=(VMEM,) * 2,
        scratch_shapes=[
            pltpu.VMEM((count * tokens, width), bf16),
            pltpu.VMEM((count * tokens, width), bf16),
            pltpu.VMEM((count * tokens, width), f32),
            pltpu.SemaphoreType.DMA((2 * count,)),
        ],
    )


def sum_refs(refs, rows=None):
    rows = rows or refs[0].shape[0]
    total = refs[0][:rows, :].astype(f32)
    for ref in refs[1:]:
        total = total + ref[:rows, :].astype(f32)
    return total


def attend_back_kernel(pieces, weights, terms, reps, versions, *refs):
    (fixed, ow_refs, t_refs, sources, outs, dkv_refs, scratch), _ = taken(
        refs, (7, weights, terms, (2 + pieces) * versions, 4, 2, 6)
    )
    marks_ref, starts_ref, gy_ref, gain_ref, mask_ref, cos_ref, sin_ref = fixed
    gh_ref, ghl_ref, dq_ref, mg_ref = outs
    hid_ref, q_ref, kv_ref, sem, ow_ref, ow_sem = scratch
    kv_refs = [kv_ref.at[p] for p in range(pieces)]
    *copies, hidden_in = bring(
        marks_ref,
        [sources[k * versions : (k + 1) * versions] for k in (*range(1, 2 + pieces), 0)],
        [q_ref, *kv_refs, hid_ref],
        sem,
    )
    (weights_in,) = weight_copies(starts_ref, ow_refs, ow_ref, ow_sem)
    tokens = q_ref.shape[0] // reps
    wait_all(copies)
    places = [(seq, g) for seq in range(reps) for g in range(KV_HEADS)]
    probs_at = {}
    for seq, g in places:
        q = head_rows(q_ref[seq * tokens : (seq + 1) * tokens, :], g)
        scores = [
            masked_scores(q, key_rows(kv, seq, reps, tokens, g), mask_ref[p], tokens)
            for p, kv in enumerate(kv_refs)
        ]
        top = functools.reduce(jnp.maximum, [jnp.max(s, axis=-1, keepdims=True) for s in scores])
        weights = [jnp.exp(s - top) for s in scores]
        total = functools.reduce(jnp.add, [jnp.sum(w, axis=-1, keepdims=True) for w in weights])
        scale = 1.0 / total
        probs_at[seq, g] = [w * scale for w in weights]
    hidden_in.wait()
    grad_from_two, grad_gain = norm_backward(
        sum_refs(t_refs, hid_ref.shape[0]), hid_ref[...], gain_ref[...].astype(f32)
    )
    mg_ref[...] = grad_gain
    grad_hidden = gy_ref[...].astype(f32) + grad_from_two
    gh_ref[...] = grad_hidden
    grad_low = grad_hidden.astype(bf16)
    ghl_ref[...] = grad_low
    wait_all(weights_in)
    grad_att = dot_nt(grad_low, ow_ref[...]).astype(bf16)
    cos = cos_ref[...]
    sin = sin_ref[...]
    for seq, g in places:
        rows = slice(seq * tokens, (seq + 1) * tokens)
        q = head_rows(q_ref[rows, :], g)
        go = head_rows(grad_att[rows, :], g)
        probs = probs_at[seq, g]
        grad_probs = [
            dot_nt(go, key_rows(kv, seq, reps, tokens, KV_HEADS + g)) for kv in kv_refs
        ]
        delta = functools.reduce(
            jnp.add,
            [jnp.sum(p * d, axis=-1, keepdims=True) for p, d in zip(probs, grad_probs)],
        )
        dq = jnp.zeros((GROUP * tokens, HEAD_DIM), f32)
        for p in range(pieces):
            grad_z = (probs[p] * (grad_probs[p] - delta) * SCALE).astype(bf16)
            dq = dq + dot_nn(grad_z, key_rows(kv_refs[p], seq, reps, tokens, g))
            dk = dot_tn(grad_z, q).astype(bf16)
            dv = dot_tn(probs[p].astype(bf16), go).astype(bf16)
            stride = reps * tokens
            dkv_ref = dkv_refs[p // (pieces // 2)]
            base = p % (pieces // 2) * kv_ref.shape[1] + seq * tokens
            for a in range(dk.shape[0] // tokens):
                here = slice(base + a * stride, base + a * stride + tokens)
                part = slice(a * tokens, (a + 1) * tokens)
                dkv_ref[here, g * HEAD_DIM : (g + 1) * HEAD_DIM] = dk[part]
                v_at = (KV_HEADS + g) * HEAD_DIM
                dkv_ref[here, v_at : v_at + HEAD_DIM] = dv[part]
        for j, block in enumerate(head_columns(dq, tokens)):
            head = g * GROUP + j
            dq_ref[rows, head * HEAD_DIM : (head + 1) * HEAD_DIM] = turn(
                block, cos, -sin
            ).astype(bf16)


def attend_back(marks, gy, gain, weight, mask, cos, sin, terms, kept, reps):
    ow_pieces, starts = weight
    tokens, width = gy.shape
    pieces = len(kept) - 2
    versions = len(kept[0])
    arrays = [far(array) for item in kept for array in item]
    piece = kept[2][0]
    keys = pieces * piece.shape[0]
    return call(
        functools.partial(
            attend_back_kernel, pieces, len(ow_pieces), len(terms), reps, versions
        ),
        (
            jax.ShapeDtypeStruct((tokens, width), f32),
            jax.ShapeDtypeStruct((tokens, width), bf16),
            jax.ShapeDtypeStruct((tokens, QCOLS), bf16),
            jax.ShapeDtypeStruct((1, width), f32),
            *(jax.ShapeDtypeStruct((pieces // 2 * piece.shape[0], piece.shape[1]), bf16),) * 2,
        ),
        (marks, starts, gy, gain, mask, cos, sin, *(far(w) for w in ow_pieces), *terms, *arrays),
        2 * tokens * QCOLS * width + 30 * tokens * QCOLS * keys // reps,
        8 * keys * KCOLS + 20 * tokens * width,
        "attend_back",
        limit=20 + 40 * keys // (reps * 4096),
        in_specs=[SMEM] * 2
        + [VMEM] * 5
        + [ANY] * len(ow_pieces)
        + [VMEM] * len(terms)
        + [ANY] * len(arrays),
        out_specs=(VMEM,) * 6,
        scratch_shapes=[
            pltpu.VMEM((tokens, width), f32),
            pltpu.VMEM((tokens, QCOLS), bf16),
            pltpu.VMEM((pieces, *piece.shape), bf16),
            pltpu.SemaphoreType.DMA((2 + pieces,)),
            pltpu.VMEM((QCOLS, width), bf16),
            pltpu.SemaphoreType.DMA((1, len(ow_pieces))),
        ],
    )


def project_back_kernel(terms, reps, versions, q_count, kv_count, tile, *refs):
    (fixed, q_refs, kv_refs, t_refs, x_refs, outs, scratch), _ = taken(
        refs, (9, q_count, kv_count, terms, versions, 4, 4)
    )
    marks_ref, q_starts, kv_starts, dq_ref, gh_ref, gain_ref, mg_ref, cos_ref, sin_ref = fixed
    gin_ref, gp_ref, n_ref, small_ref = outs
    wq_ref, wkv_ref, q_sem, kv_sem = scratch
    tiles = [
        (wq_ref, k, copies)
        for k, copies in enumerate(weight_copies(q_starts, q_refs, wq_ref, q_sem, tile))
    ]
    tiles += [
        (wkv_ref, k, copies)
        for k, copies in enumerate(weight_copies(kv_starts, kv_refs, wkv_ref, kv_sem, tile))
    ]
    dkv = sum_refs(t_refs)
    cos = repeat_rows(cos_ref[...], reps)
    sin = repeat_rows(sin_ref[...], reps)
    parts = [
        turn(dkv[:, j * HEAD_DIM : (j + 1) * HEAD_DIM], cos, -sin) for j in range(KV_HEADS)
    ]
    parts.append(dkv[:, KCOLS:])
    gp_ref[:, :QCOLS] = dq_ref[...]
    gp_ref[:, QCOLS:] = jnp.concatenate(parts, axis=1).astype(bf16)
    grad_projected = gp_ref[...]
    width = gh_ref.shape[1]
    columns = gp_ref.shape[1]
    small_ref[:, width : width + columns] = jnp.sum(
        grad_projected.astype(f32), axis=0, keepdims=True
    )
    small_ref[:, width + columns :] = mg_ref[...]
    x = choose(marks_ref, x_refs).astype(f32)
    gain = gain_ref[...].astype(f32)
    n_ref[...] = (x * inverse_rms(x) * gain).astype(bf16)
    grad_normed = jnp.zeros(x.shape, f32)
    for at, (w_ref, k, copies) in enumerate(tiles):
        wait_all(copies)
        grad_normed = grad_normed + dot_nt(
            grad_projected[:, at * tile : (at + 1) * tile], w_ref[:, k * tile : (k + 1) * tile]
        )
    grad_source, grad_gain = norm_backward(grad_normed, x, gain)
    small_ref[:, :width] = grad_gain
    gin_ref[...] = (gh_ref[...] + grad_source).astype(bf16)


def project_back(marks, dq, xs, gh, gain, grad_mlp_gain, q_weight, kv_weight, cos, sin, terms, reps):
    q_pieces, q_starts = q_weight
    kv_pieces, kv_starts = kv_weight
    tokens, width = gh.shape
    columns = QCOLS + 2 * KCOLS
    tile = 2 * KCOLS
    weights = [far(w) for w in (*q_pieces, *kv_pieces)]
    return call(
        functools.partial(
            project_back_kernel, len(terms), reps, len(xs), len(q_pieces), len(kv_pieces), tile
        ),
        (
            jax.ShapeDtypeStruct((tokens, width), bf16),
            jax.ShapeDtypeStruct((tokens, columns), bf16),
            jax.ShapeDtypeStruct((tokens, width), bf16),
            jax.ShapeDtypeStruct((1, columns + 2 * width), f32),
        ),
        (marks, q_starts, kv_starts, dq, gh, gain, grad_mlp_gain, cos, sin, *weights, *terms, *xs),
        2 * tokens * width * columns,
        2 * width * columns,
        "project_back",
        limit=20,
        in_specs=[SMEM] * 3 + [VMEM] * 6 + [ANY] * len(weights) + [VMEM] * (len(terms) + len(xs)),
        out_specs=(VMEM,) * 4,
        scratch_shapes=[
            pltpu.VMEM((width, QCOLS), bf16),
            pltpu.VMEM((width, 2 * KCOLS), bf16),
            pltpu.SemaphoreType.DMA((QCOLS // tile, len(q_pieces))),
            pltpu.SemaphoreType.DMA((2 * KCOLS // tile, len(kv_pieces))),
        ],
    )


def add_kernel(parts, first, rows, *refs):
    outs = refs[len(refs) - parts :]
    total = refs[0][first : first + rows, :].astype(f32)
    for ref in refs[1 : len(refs) - parts]:
        total = total + ref[first : first + rows, :].astype(f32)
    total = total.astype(bf16)
    rows = rows // parts
    for k, out in enumerate(outs):
        out[...] = total[k * rows : (k + 1) * rows]


def add_up(terms, first, rows, parts=1, after=()):
    width = terms[0].shape[1]
    out = jax.ShapeDtypeStruct((rows // parts, width), bf16)
    return call(
        functools.partial(add_kernel, parts, first, rows),
        (out,) * parts,
        terms,
        0,
        2 * (len(terms) + 1) * rows * width,
        "add_up",
        limit=8,
        in_specs=[VMEM] * len(terms),
        after=after,
        out_specs=(VMEM,) * parts,
    )


def join_kernel(*refs):
    fill(refs[-1], refs[:-1])


def join(blocks):
    rows, width = blocks[0].shape
    return call(
        join_kernel,
        jax.ShapeDtypeStruct((rows * len(blocks), width), bf16),
        blocks,
        0,
        4 * len(blocks) * rows * width,
        "join",
        limit=4,
        in_specs=[VMEM] * len(blocks),
        out_specs=VMEM,
    )


def select_kernel(marks_ref, early_ref, late_ref, out_ref):
    out_ref[...] = choose(marks_ref, (early_ref, late_ref))


def select(marks, early, late):
    return call(
        select_kernel,
        jax.ShapeDtypeStruct(early.shape, early.dtype),
        (marks, early, late),
        0,
        6 * early.size,
        "select",
        limit=4,
        in_specs=[SMEM, VMEM, VMEM],
        out_specs=VMEM,
    )


def rows_kernel(at_ref, source, out, sem):
    rows = out.shape[0]
    at = pl.multiple_of(at_ref[0] * rows, ROWS)
    copy = pltpu.make_async_copy(source.at[pl.ds(at, rows)], out, sem)
    copy.start()
    copy.wait()


def rows_of(array, block, rows, after):
    out = jax.ShapeDtypeStruct((rows, array.shape[1]), array.dtype)
    return call(
        rows_kernel,
        out,
        (block.astype(jnp.int32).reshape(1), far(array)),
        0,
        4 * out.size,
        "rows_of",
        limit=4,
        in_specs=[SMEM, ANY],
        after=after,
        ordered=False,
        out_specs=VMEM,
        scratch_shapes=[pltpu.SemaphoreType.DMA(())],
    )


def collect_kernel(versions, *refs):
    (marks, outs, scratch) = refs[0], refs[-2], refs[-1]
    sources = refs[1:-2]
    count = len(sources) // versions
    rows = sources[0].shape[0]
    wait_all(
        bring(
            marks,
            [sources[k * versions : (k + 1) * versions] for k in range(count)],
            [outs.at[pl.ds(k * rows, rows)] for k in range(count)],
            scratch,
        )
    )


def collect(marks, early, late, after=()):
    count = len(early)
    rows, width = early[0].shape
    arrays = [a for pair in zip(early, late) for a in pair]
    return call(
        functools.partial(collect_kernel, 2),
        jax.ShapeDtypeStruct((count * rows, width), early[0].dtype),
        (marks, *arrays),
        0,
        4 * count * rows * width,
        "collect",
        limit=4,
        ordered=False,
        after=after,
        in_specs=[SMEM] + [ANY] * len(arrays),
        out_specs=ANY,
        scratch_shapes=[pltpu.SemaphoreType.DMA((count,))],
    )


def attention_grads_kernel(steps, versions, parts, *refs):
    (flags, small_refs, sources, outs, scratch), _ = taken(
        refs, (1, steps, 3 * steps + sum(versions), parts + 1, 5)
    )
    at_ref = flags[0]
    *outs, small_ref = outs
    n_ref, p_ref, a_ref, h_ref, sem = scratch
    size = n_ref.shape[0] // steps
    copies = []
    groups = []
    targets = []
    for k, target in enumerate((n_ref, p_ref, h_ref)):
        for t in range(steps):
            groups.append((sources[k * steps + t],))
            targets.append(target.at[pl.ds(t * size, size)])
    at = 3 * steps
    for t in range(steps):
        groups.append(sources[at : at + versions[t]])
        targets.append(a_ref.at[pl.ds(t * size, size)])
        at += versions[t]
    copies = bring(at_ref, groups, targets, sem)
    small_ref[...] = sum_refs(small_refs)
    wait_all(copies)
    columns = p_ref.shape[1]
    rows = outs[0].shape[0]
    for r, out in enumerate(outs):
        here = pl.ds(pl.multiple_of(at_ref[1 + r] * rows, HEAD_DIM), rows)
        out[:, :columns] = dot_tn(n_ref[:, here], p_ref[...]).astype(bf16)
        out[:, columns:] = dot_tn(a_ref[:, here], h_ref[...]).astype(bf16)


def attention_grads(marks, smalls, normed, projected, grad_hidden, attended, parts):
    steps = len(normed)
    tokens, width = normed[0].shape
    columns = projected[0].shape[1]
    rows = width // parts
    versions = [len(a) for a in attended]
    arrays = [*normed, *projected, *grad_hidden, *(a for item in attended for a in item)]
    total = steps * tokens
    return call(
        functools.partial(attention_grads_kernel, steps, versions, parts),
        (
            *(jax.ShapeDtypeStruct((rows, columns + width), bf16),) * parts,
            jax.ShapeDtypeStruct(smalls[0].shape, f32),
        ),
        (marks, *smalls, *arrays),
        2 * total * width * (columns + width),
        2 * total * (2 * width + columns) + 2 * width * (width + columns),
        "attention_grads",
        limit=40,
        in_specs=[SMEM] + [VMEM] * steps + [ANY] * len(arrays),
        out_specs=(VMEM,) * (parts + 1),
        scratch_shapes=[
            pltpu.VMEM((total, width), bf16),
            pltpu.VMEM((total, columns), bf16),
            pltpu.VMEM((total, width), bf16),
            pltpu.VMEM((total, width), bf16),
            pltpu.SemaphoreType.DMA((4 * steps,)),
        ],
    )


def assemble_kernel(pieces, *refs):
    at_ref = refs[0]
    piece_refs = refs[1 : 1 + pieces]
    left_ref, right_ref = refs[-2:]
    columns = left_ref.shape[1]
    rows = piece_refs[0].shape[0]
    for a, piece in enumerate(piece_refs):
        here = pl.ds(pl.multiple_of(at_ref[a] * rows, 8), rows)
        left_ref[here, :] = piece[:, :columns].astype(f32)
        right_ref[here, :] = piece[:, columns:].astype(f32)


def assemble(places, pieces, columns, after):
    rows, total = pieces[0].shape
    count = len(pieces)
    return call(
        functools.partial(assemble_kernel, count),
        (
            jax.ShapeDtypeStruct((rows * count, columns), f32),
            jax.ShapeDtypeStruct((rows * count, total - columns), f32),
        ),
        (places, *pieces),
        0,
        6 * rows * count * total,
        "assemble",
        limit=24,
        in_specs=[SMEM] + [VMEM] * count,
        after=after,
        ordered=False,
        out_specs=(VMEM, VMEM),
    )


def unit_tile(units, most):
    return max(t for t in range(16, most + 1, 16) if units % t == 0)


def weight_grad_kernel(aliased, adds, *refs):
    n_ref, g_ref, gate_ref, up_ref, down_ref = refs[:5]
    olds = refs[5 : 5 + aliased]
    news = refs[-4:-1]
    refs[-1][...] = jnp.zeros_like(refs[-1])

    @pl.when(pl.program_id(1) == 0)
    def _():
        for k, new in enumerate(news):
            new[...] = olds[k][...] if adds else jnp.zeros_like(new)

    rows = n_ref[...]
    grads = g_ref[...]
    gate_pre = dot_nt(gate_ref[...], rows)
    up_pre = dot_nt(up_ref[...], rows)
    grad_act = dot_nt(down_ref[...], grads)
    silu, grad_gate, grad_up = swiglu_backward(gate_pre, up_pre, grad_act)
    activated = (silu * up_pre).astype(bf16)
    news[0][...] += dot_nn(grad_gate, rows)
    news[1][...] += dot_nn(grad_up, rows)
    news[2][...] += dot_nn(activated, grads)


def weight_grads(n_all, g_all, gate, up, down, outs, adds, first, count, after):
    units, width = gate.shape
    tokens = n_all.shape[0]
    tile = unit_tile(units, 320)
    chunk = math.gcd(tokens, 1024)
    shape = jax.ShapeDtypeStruct((units, width), f32)
    part = pl.BlockSpec((tile, width), lambda i, j: (i + first, 0))
    rows = pl.BlockSpec((chunk, width), lambda i, j: (j, 0))
    *outs, zeros = call(
        functools.partial(weight_grad_kernel, len(outs), adds),
        (*(shape,) * 3, jax.ShapeDtypeStruct((8, 128), f32)),
        (n_all, g_all, gate, up, down, *outs),
        12 * tokens * width * tile * count,
        18 * width * tile * count,
        "weight_grads",
        limit=60,
        ordered=False,
        grid=(count, tokens // chunk),
        in_specs=[rows] * 2
        + [part] * 3
        + [part if adds else ANY] * len(outs),
        after=after,
        out_specs=((*(part,) * 3, pl.BlockSpec((8, 128), lambda i, j: (0, 0)))),
        input_output_aliases={len(after) + 5 + k: k for k in range(len(outs))},
    )
    return outs, zeros


def body(
    inputs,
    cotangent,
    attn_gain,
    qkv_weight,
    qkv_bias,
    out_weight,
    mlp_gain,
    gate_weight,
    up_weight,
    down_weight,
):
    first = lax.axis_index("section") == 0
    micro, rows_here, _, width = inputs.shape
    fsdp = lax.axis_size("fsdp")
    ctx = lax.axis_size("ctx")
    fsdp_at = lax.axis_index("fsdp")
    ctx_at = lax.axis_index("ctx")
    tokens = 2 * rows_here
    reps = MICROS
    chunks = micro // reps
    steps = chunks + LAG
    span_rows = rows_here * fsdp
    half_rows = span_rows * ctx

    def places_of(c, f, token):
        index = (c * fsdp + f) * rows_here + token // 2
        second = 2 * half_rows - span_rows * (index // span_rows + 1) + index % span_rows
        return jnp.where(token % 2 == 0, index, second)

    own = places_of(ctx_at, fsdp_at, jnp.arange(tokens, dtype=jnp.int32))
    shape = (fsdp, tokens, ctx * tokens)
    number = lax.broadcasted_iota(jnp.int32, shape, 0)
    other = jnp.zeros(shape, jnp.int32)
    for k, r in enumerate(relative_order(fsdp)):
        other = jnp.where(number == k, fsdp_at ^ r, other)
    column = lax.broadcasted_iota(jnp.int32, shape, 2)
    key_places = places_of(ctx_at ^ (column // tokens), other, column % tokens)
    query_places = places_of(ctx_at, fsdp_at, lax.broadcasted_iota(jnp.int32, shape, 1))
    mask = jnp.where(key_places <= query_places, 0.0, NEGATIVE).astype(f32)
    half = HEAD_DIM // 2
    frequency = ROPE_BASE ** (-(jnp.arange(half, dtype=f32) * 2.0) / HEAD_DIM)
    angles = own.astype(f32)[:, None] * frequency
    cos = jnp.concatenate([jnp.cos(angles)] * 2, axis=1)
    sin = jnp.concatenate([-jnp.sin(angles), jnp.sin(angles)], axis=1)

    packed = jnp.concatenate([attn_gain, qkv_bias, mlp_gain], axis=1)
    packed_pieces = gather_pieces(packed, "fsdp")
    owners = jnp.arange(fsdp, dtype=jnp.int32)[:, None]
    packed = functools.reduce(
        jnp.add,
        [
            jnp.where(owners == fsdp_at ^ r, piece, jnp.zeros_like(piece))
            for r, piece in zip(relative_order(fsdp), packed_pieces)
        ],
    )
    gain_part, bias_part = attn_gain.shape[1], qkv_bias.shape[1]
    attn_full = packed[:, :gain_part].reshape(1, -1)
    bias_full = packed[:, gain_part : gain_part + bias_part].reshape(1, -1)
    mlp_full = packed[:, gain_part + bias_part :].reshape(1, -1)

    def gathered(shard, after=None):
        units = shard.shape[0] // ROWS
        pieces = [(shard, fsdp_at * units)]
        for bit in bits_of(fsdp):
            if len(pieces) == 1 and after is not None:
                half = units // 2
                odd = ctx_at & 1
                mine = exchange(rows_of(shard, odd, half * ROWS, after), "fsdp", bit)
                other = exchange(mine, "ctx", 1)
                base = (fsdp_at ^ bit) * units
                pieces += [(mine, base + odd * half), (other, base + (1 - odd) * half)]
            else:
                pieces += [
                    (exchange(piece, "fsdp", bit), (at // units ^ bit) * units + at % units)
                    for piece, at in pieces
                ]
        starts = jnp.stack([at.astype(jnp.int32) for _, at in pieces])
        return [piece for piece, _ in pieces], starts

    kv_weight = gathered(qkv_weight[0, :, QCOLS:])
    q_weight = gathered(qkv_weight[0, :, :QCOLS], kv_weight[0][1:2])
    gate, up, down = gate_weight[0], up_weight[0], down_weight[0]
    flag = first.astype(jnp.int32)
    marks = jnp.stack([flag] + [(fsdp_at ^ r).astype(jnp.int32) for r in relative_order(fsdp)])

    def chunked(array):
        return array.reshape(chunks, reps * tokens, width)

    in_chunks = chunked(inputs)
    cot_chunks = chunked(cotangent)

    def pick(early, late):
        return jnp.where(first, early, late)

    def versions(u, early, late):
        if u < LAG:
            return (late[u + LAG],)
        if u < chunks:
            return (early[u - LAG], late[u + LAG])
        return (early[u - LAG],)

    gys = [jnp.where(first, jnp.zeros_like(cot), cot) for cot in cot_chunks[:LAG]]
    early_pieces = [gather_pieces(gy, "fsdp") for gy in gys]
    gys = dict(enumerate(gys))

    ORDER.clear()

    def pick(early, late):
        return jnp.where(first, early, late)

    def versions(u, early, late):
        if u < LAG:
            return (late[u + LAG],)
        if u < chunks:
            return (early[u - LAG], late[u + LAG])
        return (early[u - LAG],)


    first_keys, out_weights = [], []
    near_weights = [gate, up, down]
    outputs, moved, xs, kept, attended, n2_pieces = {}, {}, {}, {}, {}, {}
    grads_in, grads_moved, smalls, factors = {}, {}, {}, {}

    def add_one(terms, rows):
        return add_up(terms, rows, rows)[0]

    def forward(t):
        if t < LAG:
            x = (in_chunks[t],)
        elif t < chunks:
            x = (in_chunks[t], moved[t])
        else:
            x = (moved[t],)
        xs[t] = x
        kv = project(
            marks, x, attn_full, kv_weight, bias_full[:, QCOLS:], cos, sin, reps, KV_HEADS
        )
        first_keys.append(kv)
        blocks = [kv] + [exchange(kv, "ctx", a) for a in range(1, ctx)]
        yield "K"
        for name in "QJ" if LAG <= t < chunks else "JQ":
            if name == "J":
                kv_pieces = gather_pieces(join(blocks), "fsdp")
            else:
                q = project(
                    marks, x, attn_full, q_weight, bias_full[:, :QCOLS], cos, sin, reps, HEADS
                )
            yield name
        if t == 0:
            out_weights.extend(gathered(out_weight[0], first_keys))
        after = [p for pieces in early_pieces for p in pieces[1:]] if t == LAG else []
        att, hidden, n2 = attend(
            marks, q, x, mask, out_weights, mlp_full, kv_pieces, reps, after
        )
        attended[t] = att
        n2_pieces[t] = gather_pieces(n2, "fsdp")
        kept[t] = (hidden, q, *kv_pieces)
        yield "A"
        parts = mlp(n2_pieces[t], *near_weights)
        terms = yield from stages(reduction(*parts, "fsdp", add_one), "M", "R")
        outputs[t] = add_up([hidden, *terms], 0, hidden.shape[0])[0]
        if t < chunks:
            moved[t + LAG] = passed_along(outputs[t], "section", 1)
        yield "Y"

    def stages(generator, first_name, name):
        while True:
            try:
                next(generator)
            except StopIteration as end:
                return end.value
            yield first_name
            first_name = name

    def backward(u):
        if u < LAG:
            gy, g_pieces = gys[u], early_pieces[u]
        else:
            gy = select(marks, grads_moved[u], cot_chunks[u]) if u < chunks else grads_moved[u]
            gys[u] = gy
            g_pieces = gather_pieces(gy, "fsdp")
            yield "G"
        n2_now = list(zip(*versions(u, n2_pieces, n2_pieces)))
        parts = mlp_back(marks, n2_now, g_pieces, *near_weights, [])
        terms = yield from stages(reduction(*parts, "fsdp", add_one), "B", "S")
        kept_now = list(zip(*versions(u, kept, kept)))
        gh, gh_low, dq, grad_mlp_gain, *dkv = attend_back(
            marks, gy, mlp_full, out_weights, mask, cos, sin, terms, kept_now, reps
        )
        terms = yield from stages(reduction(*dkv, "fsdp", add_one), "T", "D")
        own, *others = add_up(terms, 0, ctx * reps * tokens, ctx)
        dkv_terms = [own] + [exchange(other, "ctx", a + 1) for a, other in enumerate(others)]
        yield "E"
        x_now = versions(u, {t: x[0] for t, x in xs.items()}, {t: x[-1] for t, x in xs.items()})
        g_in, g_proj, normed, small = project_back(
            marks,
            dq,
            x_now,
            gh,
            attn_full,
            grad_mlp_gain,
            q_weight,
            kv_weight,
            cos,
            sin,
            dkv_terms,
            reps,
        )
        grads_in[u] = g_in
        if u < chunks:
            grads_moved[u + LAG] = passed_along(g_in, "section", -1)
        smalls[u] = small
        factors[u] = (normed, g_proj, gh_low, versions(u, attended, attended))
        yield "P"

    running = {}
    for name in SEQUENCE.split():
        if name == "H":
            near_weights[:] = hold(gate, up, down)
            continue
        kind, step = name[0], int(name[1:])
        key = (kind in FORWARD, step)
        if key not in running:
            running[key] = forward(step) if key[0] else backward(step)
        while next(running[key]) != kind:
            pass
    grads_in, gys, smalls, factors = (
        [found[t] for t in range(steps)] for found in (grads_in, gys, smalls, factors)
    )

    batches = [b for b in (range(0, chunks // 2), range(chunks // 2, chunks)) if len(b)]

    def all_tokens(early, late, batch):
        own_rows = collect(marks, [early[m] for m in batch], [late[m] for m in batch])
        return lax.all_gather(own_rows, ("ctx", "fsdp"), axis=0, tiled=True)

    n2_own = [n2_pieces[t][0] for t in range(steps)]
    n2_all = [all_tokens(n2_own, n2_own[LAG:], batch) for batch in batches]
    g_all = [all_tokens(gys[LAG:], gys, batch) for batch in batches]
    tiles = gate.shape[0] // unit_tile(gate.shape[0], 320)
    cuts = [0, tiles // 7, 6 * tiles // 7, tiles], [0, 3 * tiles // 7, tiles]
    plan = [
        (b, i, j - i)
        for b in range(len(batches))
        for i, j in zip(cuts[b], cuts[b][1:])
        if j > i
    ]
    mlp_grads = []

    def some_weight_grads(after):
        nonlocal mlp_grads
        if not plan:
            return None
        b, start, count = plan.pop(0)
        mlp_grads, zeros = weight_grads(
            n2_all[b], g_all[b], gate, up, down, mlp_grads, b > 0, start, count, after
        )
        return zeros

    lead = QCOLS + KCOLS
    columns = QCOLS + 2 * KCOLS
    normed, projected, grad_hidden, att_now = zip(*factors)
    rows = width // fsdp
    if rows % HEAD_DIM == 0:
        *summed, small = attention_grads(
            marks, smalls, normed, projected, grad_hidden, att_now, fsdp
        )
    else:
        start = jnp.stack([flag, jnp.int32(0)])
        large, small = attention_grads(
            start, smalls, normed, projected, grad_hidden, att_now, 1
        )
        summed = [
            lax.dynamic_slice_in_dim(large, (fsdp_at ^ r) * rows, rows)
            for r in relative_order(fsdp)
        ]
    small = small.reshape(-1, HEAD_DIM)
    for bit in reversed(bits_of(fsdp)):
        count = len(summed) // 2
        moves = [exchange(p, "fsdp", bit) for p in summed[count:]]
        zeros = some_weight_grads(summed[:1])
        zero = 0.0 if zeros is None else zeros[0, 0]
        small = small + zero
        summed = [
            (p.astype(f32) + m.astype(f32) + zero).astype(bf16) for p, m in zip(summed, moves)
        ]
        small = small + exchange(small, "fsdp", bit)
    rows = width // fsdp // ctx
    terms = [
        lax.dynamic_slice_in_dim(summed[0], (ctx_at ^ a) * rows, rows) for a in range(ctx)
    ]
    moves = [exchange(terms[a], "ctx", a) for a in range(1, ctx)]
    small = small + exchange(small, "ctx", bits_of(ctx)[0])
    zeros = some_weight_grads(terms[:1])
    zeros = some_weight_grads([]) if plan else zeros
    block = functools.reduce(jnp.add, [t.astype(f32) for t in (terms[0], *moves)])
    small = small + (0.0 if zeros is None else zeros[0, 0])
    block = (block + (0.0 if zeros is None else zeros[0, 0])).astype(bf16)
    pieces = [block] + [exchange(block, "ctx", a) for a in range(1, ctx)]
    for bit in bits_of(ctx)[1:]:
        small = small + exchange(small, "ctx", bit)
    zeros = some_weight_grads([block])
    places = jnp.stack([(ctx_at ^ a).astype(jnp.int32) for a in range(ctx)])
    ends = [] if zeros is None else [zeros]
    grad_qkv, grad_out = assemble(places, pieces, columns, [] if zeros is None else [zeros])
    while plan:
        some_weight_grads([])
    grad_gate, grad_up, grad_down = mlp_grads

    small = small.reshape(-1)

    def cut(start, length):
        part = length // fsdp
        return lax.dynamic_slice(small, (start + fsdp_at * part,), (part,))

    grad_attn_gain = cut(0, width)
    grad_bias_lead = cut(width, lead)
    grad_bias_value = cut(width + lead, columns - lead)
    grad_mlp_gain = cut(width + columns, width)

    for generator in running.values():
        for _ in generator:
            pass
    outputs = [outputs[t] for t in range(steps)]
    layer_outputs = collect(marks, outputs[:chunks], outputs[LAG:], ends).reshape(inputs.shape)
    input_grads = collect(marks, grads_in[LAG:], grads_in[:chunks], ends).reshape(inputs.shape)
    return (
        layer_outputs[None],
        input_grads[None],
        grad_attn_gain[None],
        grad_qkv[None],
        grad_bias_lead[None],
        grad_bias_value[None],
        grad_out[None],
        grad_mlp_gain[None],
        grad_gate[None],
        grad_up[None],
        grad_down[None],
    )


def solution(mesh):
    rows = P(None, ("ctx", "fsdp"), None, None)
    vector = P("section", "fsdp")
    matrix = P("section", "fsdp", None)
    stacked = P("section", None, ("ctx", "fsdp"), None, None)
    in_specs = (rows, rows, vector, matrix, vector, matrix, vector, matrix, matrix, matrix)
    out_specs = (
        stacked,
        stacked,
        vector,
        matrix,
        vector,
        vector,
        matrix,
        vector,
        matrix,
        matrix,
        matrix,
    )
    return jax.shard_map(body, mesh=mesh, in_specs=in_specs, out_specs=out_specs, check_vma=False)
```

time: 975 us -> 947 us (0.971)
  waiting for transfers between devices: 174 us -> 282 us
  local copies, waits for them, and re-layouts: 87.2 us -> 40.1 us
  starting transfers between devices: 140 us -> 103 us
  other arithmetic: 45.6 us -> 22 us
  blocking collectives: 17.1 us -> 0 us
  Pallas kernels: 485 us -> 474 us
    ppermute x157 -> x92, waiting for transfers between devices: 137 us -> 257 us  [exchange(): return lax.ppermute(block, axis, [(i, i ^ mask) for i in range(size)])]
    unnamed x452 -> x209, local copies, waits for them, and re-layouts: 61.4 us -> 23.2 us
    ppermute x157 -> x92, starting transfers between devices: 125 us -> 91.3 us  [exchange(): return lax.ppermute(block, axis, [(i, i ^ mask) for i in range(size)])]
    all_gather x2 -> x0, waiting for transfers between devices: 29.6 us -> none  [gathered(): return lax.all_gather(shard, 'fsdp', axis=0, tiled=True)]
    ppermute x8 -> x4, waiting for transfers between devices: 5.97 us -> 25.6 us  [passed_along(): return lax.ppermute(block, axis, route)]
    all_gather x3 -> x0, blocking collectives: 17.1 us -> none  [gathered(): return lax.all_gather(shard, 'fsdp', axis=0, tiled=True)]
    select_n x13 -> x2, other arithmetic: 12.7 us -> 0.18 us  [the longest x1 0.17 us: body(): mask = jnp.where(key_places <= query_places, 0.0, NEGATIVE).astype(f32)]
    pallas_call x44 -> x59, Pallas kernels: 485 us -> 474 us  [call(): pl.pallas_call(body, out_shape=out_shape, in_specs=[*[ANY] * len(waits),...]
  transfers between devices with their start and end apart: 171 -> 100, of which waited for: 43 -> 44; matrix products, arithmetic and copies ran while one was open for 7% -> 4% of each run, Pallas kernels for 49% -> 47%
where the time goes in v3:
time: 947 us; the launch traced here: 937 us
  Pallas kernels  474 us (50%)
  waiting for transfers between devices  282 us (30%)
  starting transfers between devices  103 us (11%)
  local copies, waits for them, and re-layouts  40.1 us (4%)
  other arithmetic  22 us (2%)
  between operations  15.9 us (2%)
    pallas_call x59, Pallas kernels, call(): pl.pallas_call(body, out_shape=out_shape, in_specs=[*[ANY] * len(waits),...  474 us
    ppermute x92, waiting for transfers between devices, exchange(): return lax.ppermute(block, axis, [(i, i ^ mask) for i in range(size)])  257 us
    ppermute x92, starting transfers between devices, exchange(): return lax.ppermute(block, axis, [(i, i ^ mask) for i in range(size)])  91.3 us
    ppermute x4, waiting for transfers between devices, passed_along(): return lax.ppermute(block, axis, route)  25.6 us
    unnamed x209, local copies, waits for them, and re-layouts  23.2 us
  transfers between devices with their start and end apart: 100, of which 44 were waited for; matrix products, arithmetic and copies ran while one was open for 4% of the time, Pallas kernels for 47%

profile of v3, /device:TPU:0, one launch (start us, length us, event | category | flops | bytes accessed | tf_op | source)
XLA Modules:
  0.0 937.4 jit_solution(17775724603572576547)
XLA Ops:
  34.4 8.0 collective-permute-done.12.refs_8_.refs_11_
  46.8 13.1 %collective-permute-done.10.refs_3_ = bf16[128,512]{1,0:T(8,128)(2,1)S(1)} collective-permute-done((bf16[128,512]{1,0:T(8,128)(2,1)S(1)}, bf16[128,512]{1,0:T(8,128)(2,1)S(1)}, u32[]{:S(2)}, u32[]{:S(2)}) %collective-permute-start.10) | collective-permute-done | bytes 131104 | tf_op jit(solution)/shard_map/ppermute | solution.py:66
  70.0 10.8 %collective-permute-done.22.refs_13_.refs_23_ = bf16[512,512]{1,0:T(8,128)(2,1)S(1)} collective-permute-done((bf16[512,512]{1,0:T(8,128)(2,1)S(1)}, bf16[512,512]{1,0:T(8,128)(2,1)S(1)}, u32[]{:S(2)}, u32[]{:S(2)}) %collective-permute-start.22) | collective-permute-done | bytes 524320 | tf_op jit(solution)/shard_map/ppermute | solution.py:66
  94.4 10.6 %collective-permute-done.25.refs_2_.refs_7_ = bf16[128,1536]{1,0:T(8,128)(2,1)S(1)} collective-permute-done((bf16[128,1536]{1,0:T(8,128)(2,1)S(1)}, bf16[128,1536]{1,0:T(8,128)(2,1)S(1)}, u32[]{:S(2)}, u32[]{:S(2)}) %collective-permute-start.25) | collective-permute-done | bytes 393248 | tf_op jit(solution)/shard_map/ppermute | solution.py:66
  105.0 7.0 hold.4
  112.1 11.4 %mlp.3 = (bf16[256,1536]{1,0:T(8,128)(2,1)S(1)}, bf16[256,1536]{1,0:T(8,128)(2,1)S(1)}) custom-call(bf16[2240,1536]{1,0:T(8,128)(2,1)S(1)} %get-tuple-element.113.refs_0_.refs_5_, bf16[128,1536]{1,0:T(8,128)(2,1)S(1)} %get-tuple-element.114.refs_1_.refs_5_, bf16[128,1536]{1,0:T(8,128)(2,1)S(1)} %collective-permute-done.25.refs_2_.refs_7_, ...), custom_call_target="tpu_custom_call" | custom-call | flops 10569646080 | bytes 3145728 | tf_op jit(solution)/shard_map/mlp/pallas_call | solution.py:118
  126.6 10.9 %collective-permute-done.29.refs_4_ = bf16[128,1536]{1,0:T(8,128)(2,1)S(1)} collective-permute-done((bf16[128,1536]{1,0:T(8,128)(2,1)S(1)}, bf16[128,1536]{1,0:T(8,128)(2,1)S(1)}, u32[]{:S(2)}, u32[]{:S(2)}) %collective-permute-start.29) | collective-permute-done | bytes 393248 | tf_op jit(solution)/shard_map/ppermute | solution.py:66
  141.3 7.9 collective-permute-done.30.refs_12_.refs_14_.refs_20_.refs_24_
  167.6 9.3 collective-permute-done.34.refs_16_.refs_20_
  185.0 7.0 attend.4
  196.5 10.6 %collective-permute-done.37.refs_2_.refs_6_ = bf16[128,1536]{1,0:T(8,128)(2,1)S(1)} collective-permute-done((bf16[128,1536]{1,0:T(8,128)(2,1)S(1)}, bf16[128,1536]{1,0:T(8,128)(2,1)S(1)}, u32[]{:S(2)}, u32[]{:S(2)}) %collective-permute-start.37) | collective-permute-done | bytes 393248 | tf_op jit(solution)/shard_map/ppermute | solution.py:66
  208.3 6.9 hold.5
  215.3 11.5 %mlp.4 = (bf16[256,1536]{1,0:T(8,128)(2,1)S(1)}, bf16[256,1536]{1,0:T(8,128)(2,1)S(1)}) custom-call(bf16[2240,1536]{1,0:T(8,128)(2,1)S(1)} %get-tuple-element.121.refs_0_.refs_5_.refs_2_, bf16[128,1536]{1,0:T(8,128)(2,1)S(1)} %get-tuple-element.122.refs_1_.refs_5_.refs_2_, bf16[128,1536]{1,0:T(8,128)(2,1)S(1)} %collective-permute-done.37.refs_2_.refs_6_, ...), custom_call_target="tpu_custom_call" | custom-call | flops 10569646080 | bytes 3145728 | tf_op jit(solution)/shard_map/mlp/pallas_call | solution.py:118
  229.3 22.2 %mlp_back.3 = (bf16[256,1536]{1,0:T(8,128)(2,1)S(1)}, bf16[256,1536]{1,0:T(8,128)(2,1)S(1)}) custom-call(bf16[128,1536]{1,0:T(8,128)(2,1)S(1)} %add_up.17.refs_0_, s32[5]{0:T(128)S(1)} %stack.81.refs_0_.refs_1_.refs_4_, bf16[2240,1536]{1,0:T(8,128)(2,1)S(1)} %get-tuple-element.121.refs_0_.refs_5_.refs_2_, ...), custom_call_target="tpu_custom_call" | custom-call | flops 17616076800 | bytes 4718592 | tf_op jit(solution)/shard_map/mlp_back/pallas_call | solution.py:118
  252.7 10.5 %collective-permute-done.41.refs_4_ = bf16[128,1536]{1,0:T(8,128)(2,1)S(1)} collective-permute-done((bf16[128,1536]{1,0:T(8,128)(2,1)S(1)}, bf16[128,1536]{1,0:T(8,128)(2,1)S(1)}, u32[]{:S(2)}, u32[]{:S(2)}) %collective-permute-start.41) | collective-permute-done | bytes 393248 | tf_op jit(solution)/shard_map/ppermute | solution.py:66
  268.7 7.3 collective-permute-done.43.refs_11_.refs_13_.refs_16_.refs_25_
  278.5 12.0 %attend_back.3 = (f32[128,1536]{1,0:T(8,128)S(1)}, bf16[128,1536]{1,0:T(8,128)(2,1)S(1)}, bf16[128,1536]{1,0:T(8,128)(2,1)S(1)}, f32[1,1536]{1,0:T(1,128)S(1)}, ...) custom-call(bf16[128,512]{1,0:T(8,128)(2,1)S(1)} %project.10.refs_0_.refs_1_, ...), custom_call_target="tpu_custom_call" | custom-call | flops 6643777536 | bytes 8126464 | tf_op jit(solution)/shard_map/attend_back/pallas_call | solution.py:118
  291.3 8.5 collective-permute-start.46
  304.7 7.7 collective-permute-done.47.refs_3_
  314.6 12.9 %collective-permute-done.53.refs_13_.refs_24_ = bf16[512,512]{1,0:T(8,128)(2,1)} collective-permute-done((bf16[512,512]{1,0:T(8,128)(2,1)S(1)}, bf16[512,512]{1,0:T(8,128)(2,1)}, u32[]{:S(2)}, u32[]{:S(2)}) %collective-permute-start.53) | collective-permute-done | bytes 524320 | tf_op jit(solution)/shard_map/ppermute | solution.py:66
  344.4 7.6 collective-permute-done.51.refs_22_
  363.3 6.9 attend.5
  375.9 10.2 %collective-permute-done.60.refs_14_ = bf16[128,1536]{1,0:T(8,128)(2,1)S(1)} collective-permute-done((bf16[128,1536]{1,0:T(8,128)(2,1)S(1)}, bf16[128,1536]{1,0:T(8,128)(2,1)S(1)}, u32[]{:S(2)}, u32[]{:S(2)}) %collective-permute-start.60) | collective-permute-done | bytes 393248 | tf_op jit(solution)/shard_map/ppermute | solution.py:66
  386.1 8.2 collective-permute-done.57.refs_8_.refs_2_
  394.3 7.1 hold.6
  402.4 22.7 %mlp_back.4 = (bf16[256,1536]{1,0:T(8,128)(2,1)S(1)}, bf16[256,1536]{1,0:T(8,128)(2,1)}) custom-call(bf16[2240,1536]{1,0:T(8,128)(2,1)S(1)} %get-tuple-element.141.refs_0_.refs_2_, s32[5]{0:T(128)S(1)} %stack.81.refs_0_.refs_1_.refs_4_, bf16[2240,1536]{1,0:T(8,128)(2,1)S(1)} %get-tuple-element.141.refs_0_.refs_2_, ...), custom_call_target="tpu_custom_call" | custom-call | flops 17616076800 | bytes 4718592 | tf_op jit(solution)/shard_map/mlp_back/pallas_call | solution.py:118
  429.8 11.1 %collective-permute-done.64.refs_16_ = bf16[128,1536]{1,0:T(8,128)(2,1)S(1)} collective-permute-done((bf16[128,1536]{1,0:T(8,128)(2,1)S(1)}, bf16[128,1536]{1,0:T(8,128)(2,1)S(1)}, u32[]{:S(2)}, u32[]{:S(2)}) %collective-permute-start.64) | collective-permute-done | bytes 393248 | tf_op jit(solution)/shard_map/ppermute | solution.py:66
  440.9 12.7 %attend_back.4 = (f32[128,1536]{1,0:T(8,128)S(1)}, bf16[128,1536]{1,0:T(8,128)(2,1)S(1)}, bf16[128,1536]{1,0:T(8,128)(2,1)S(1)}, f32[1,1536]{1,0:T(1,128)S(1)}, ...) custom-call(bf16[128,1536]{1,0:T(8,128)(2,1)S(1)} %add_up.22.refs_0_, s32[5]{0:T(128)S(1)} %stack.81.refs_0_.refs_1_.refs_4_, ...), custom_call_target="tpu_custom_call" | custom-call | flops 6643777536 | bytes 8126464 | tf_op jit(solution)/shard_map/attend_back/pallas_call | solution.py:118
  456.8 13.7 %collective-permute-done.66.refs_3_ = bf16[512,512]{1,0:T(8,128)(2,1)S(1)} collective-permute-done((bf16[512,512]{1,0:T(8,128)(2,1)S(1)}, bf16[512,512]{1,0:T(8,128)(2,1)S(1)}, u32[]{:S(2)}, u32[]{:S(2)}) %collective-permute-start.66) | collective-permute-done | bytes 524320 | tf_op jit(solution)/shard_map/ppermute | solution.py:66
  470.7 6.5 collective-permute-start.67
  479.6 8.7 collective-permute-done.67.refs_21_
  488.4 9.3 collective-permute-done.68.refs_22_
  504.3 10.0 %collective-permute-done.70.refs_9_.refs_3_.refs_1_ = bf16[128,1536]{1,0:T(8,128)(2,1)S(1)} collective-permute-done((bf16[128,1536]{1,0:T(8,128)(2,1)S(1)}, bf16[128,1536]{1,0:T(8,128)(2,1)S(1)}, u32[]{:S(2)}, u32[]{:S(2)}) %collective-permute-start.70) | collective-permute-done | bytes 393248 | tf_op jit(solution)/shard_map/ppermute | solution.py:72
  514.5 7.6 collective-permute-done.71.refs_10_
  522.1 6.9 hold.7
  529.1 22.2 %mlp_back.5 = (bf16[256,1536]{1,0:T(8,128)(2,1)S(1)}, bf16[256,1536]{1,0:T(8,128)(2,1)S(1)}) custom-call(bf16[2240,1536]{1,0:T(8,128)(2,1)S(1)} %get-tuple-element.158.refs_0_.refs_2_.refs_5_, s32[5]{0:T(128)S(1)} %stack.81.refs_0_.refs_1_.refs_4_, bf16[2240,1536]{1,0:T(8,128)(2,1)S(1)} %get-tuple-element.158.refs_0_.refs_2_.refs_5_, ...), custom_call_target="tpu_custom_call" | custom-call | flops 17616076800 | bytes 4718592 | tf_op jit(solution)/shard_map/mlp_back/pallas_call | solution.py:118
  551.9 12.3 %mlp.5 = (bf16[256,1536]{1,0:T(8,128)(2,1)S(1)}, bf16[256,1536]{1,0:T(8,128)(2,1)}) custom-call(bf16[256,1536]{1,0:T(8,128)(2,1)S(1)} %get-tuple-element.161.refs_0_.refs_1_.refs_14_, bf16[128,1536]{1,0:T(8,128)(2,1)S(1)} %copy-done.33, bf16[128,1536]{1,0:T(8,128)(2,1)S(1)} %copy-done.75, bf16[128,1536]{1,0:T(8,128)(2,1)S(1)} %copy-done.77, ...), custom_call_target="tpu_custom_call" | custom-call | flops 10569646080 | bytes 3145728 | tf_op jit(solution)/shard_map/mlp/pallas_call | solution.py:118
  564.6 10.9 %collective-permute-done.75.refs_16_ = bf16[128,1536]{1,0:T(8,128)(2,1)S(1)} collective-permute-done((bf16[128,1536]{1,0:T(8,128)(2,1)S(1)}, bf16[128,1536]{1,0:T(8,128)(2,1)S(1)}, u32[]{:S(2)}, u32[]{:S(2)}) %collective-permute-start.75) | collective-permute-done | bytes 393248 | tf_op jit(solution)/shard_map/ppermute | solution.py:66
  575.5 12.2 %attend_back.5 = (f32[128,1536]{1,0:T(8,128)S(1)}, bf16[128,1536]{1,0:T(8,128)(2,1)S(1)}, bf16[128,1536]{1,0:T(8,128)(2,1)S(1)}, f32[1,1536]{1,0:T(1,128)S(1)}, ...) custom-call(bf16[128,1536]{1,0:T(8,128)(2,1)S(1)} %add_up.25.refs_0_, s32[5]{0:T(128)S(1)} %stack.81.refs_0_.refs_1_.refs_4_, ...), custom_call_target="tpu_custom_call" | custom-call | flops 6643777536 | bytes 8126464 | tf_op jit(solution)/shard_map/attend_back/pallas_call | solution.py:118
  591.0 13.7 %collective-permute-done.77.refs_3_ = bf16[512,512]{1,0:T(8,128)(2,1)S(1)} collective-permute-done((bf16[512,512]{1,0:T(8,128)(2,1)S(1)}, bf16[512,512]{1,0:T(8,128)(2,1)S(1)}, u32[]{:S(2)}, u32[]{:S(2)}) %collective-permute-start.77) | collective-permute-done | bytes 524320 | tf_op jit(solution)/shard_map/ppermute | solution.py:66
  604.9 11.1 %collective-permute-start.78 = (bf16[128,512]{1,0:T(8,128)(2,1)S(1)}, bf16[128,512]{1,0:T(8,128)(2,1)S(1)}, u32[]{:S(2)}, u32[]{:S(2)}) collective-permute-start(bf16[128,512]{1,0:T(8,128)(2,1)S(1)} %get-tuple-element.170), channel_id=1, source_target_pairs={{0,4},{4,0},{8,12},{12,8},{1,5},{5,1},{9,13},{13,9},{2,6},{6,2},{1... | collective-permute-start | bytes 393224 | tf_op jit(solution)/shard_map/ppermute | solution.py:66
  619.9 6.9 collective-permute-done.79.refs_22_
  632.2 10.0 %attention_grads.1 = (bf16[384,3584]{1,0:T(8,128)(2,1)S(1)}, bf16[384,3584]{1,0:T(8,128)(2,1)S(1)}, bf16[384,3584]{1,0:T(8,128)(2,1)S(1)}, bf16[384,3584]{1,0:T(8,128)(2,1)}, f32[1,5120]{1,0:T(1,128)S(1)}) custom-call(bf16[128,1536]{1,0:T(8,128)(2,1)S(1)} %get-tuple-element.173.refs_0_.refs_4_, s32[5]{0:T(128)S(1)} %stack.81.refs_0_.refs_1_.refs_4_, ...), custom_call_target="tpu_custom_call" | custom-call | flops 4227858432 | bytes 14942208 | tf_op jit(solution)/shard_map/attention_grads/pallas_call | solution.py:118
  656.2 19.2 %weight_grads.5 = (f32[2240,1536]{1,0:T(8,128)}, f32[2240,1536]{1,0:T(8,128)}, f32[2240,1536]{1,0:T(8,128)}, f32[8,128]{1,0:T(8,128)}) custom-call(bf16[384,3584]{1,0:T(8,128)(2,1)} %copy-done.1, bf16[2048,1536]{1,0:T(8,128)(2,1)} %all-gather.5.cloned.1.call-done.refs_1_, bf16[2048,1536]{1,0:T(8,128)(2,1)} %all-gather.7.cloned.1.call-done.refs_2_, ...), custom_call_target="tpu_custom_call" | custom-call | flops 12079595520 | bytes 8847360 | tf_op jit(solution)/shard_map/weight_grads/pallas_call | solution.py:118
  688.1 73.9 %weight_grads.6 = (f32[2240,1536]{1,0:T(8,128)}, f32[2240,1536]{1,0:T(8,128)}, f32[2240,1536]{1,0:T(8,128)}, f32[8,128]{1,0:T(8,128)}) custom-call(bf16[384,3584]{1,0:T(8,128)(2,1)} %add_convert_fusion.2.refs_0_, bf16[2048,1536]{1,0:T(8,128)(2,1)} %all-gather.5.cloned.1.call-done.refs_1_, ...), custom_call_target="tpu_custom_call", output_to_operand_aliasing={{0}: (6, {}), {1}: (7, {}), {2}: (8, {})} | custom-call | flops 60397977600 | bytes 44236800 | tf_op jit(solution)/shard_map/weight_grads/pallas_call | solution.py:118
  779.4 18.4 %weight_grads.7 = (f32[2240,1536]{1,0:T(8,128)}, f32[2240,1536]{1,0:T(8,128)}, f32[2240,1536]{1,0:T(8,128)}, f32[8,128]{1,0:T(8,128)}) custom-call(bf16[96,3584]{1,0:T(8,128)(2,1)} %get-tuple-element.213.refs_0_, bf16[2048,1536]{1,0:T(8,128)(2,1)} %all-gather.5.cloned.1.call-done.refs_1_, ...), custom_call_target="tpu_custom_call", output_to_operand_aliasing={{0}: (6, {}), {1}: (7, {}), {2}: (8, {})} | custom-call | flops 12079595520 | bytes 8847360 | tf_op jit(solution)/shard_map/weight_grads/pallas_call | solution.py:118
  797.8 48.0 %weight_grads.8 = (f32[2240,1536]{1,0:T(8,128)}, f32[2240,1536]{1,0:T(8,128)}, f32[2240,1536]{1,0:T(8,128)}, f32[8,128]{1,0:T(8,128)}) custom-call(bf16[2048,1536]{1,0:T(8,128)(2,1)} %all-gather.9.cloned.1.call-done.refs_0_.refs_1_, ...), custom_call_target="tpu_custom_call", output_to_operand_aliasing={{0}: (5, {}), {1}: (6, {}), {2}: (7, {})} | custom-call | flops 36238786560 | bytes 26542080 | tf_op jit(solution)/shard_map/weight_grads/pallas_call | solution.py:118
  856.0 61.4 %weight_grads.9 = (f32[2240,1536]{1,0:T(8,128)}, f32[2240,1536]{1,0:T(8,128)}, f32[2240,1536]{1,0:T(8,128)}, f32[8,128]{1,0:T(8,128)}) custom-call(bf16[96,3584]{1,0:T(8,128)(2,1)} %add_convert_fusion.3.refs_0_.refs_2_, bf16[2048,1536]{1,0:T(8,128)(2,1)} %all-gather.9.cloned.1.call-done.refs_0_.refs_1_, ...), custom_call_target="tpu_custom_call", output_to_operand_aliasing={{0}: (6, {}), {1}: (7, {}), {2}: (8, {})} | custom-call | flops 48318382080 | bytes 35389440 | tf_op jit(solution)/shard_map/weight_grads/pallas_call | solution.py:118
  (481 shorter events, 246.0 us)
Async XLA Ops:
  7.2 649.0 %all-gather.5.cloned.1.call-start = ((), (), s32[]{:S(2)}) async-start(), calls=%async_computation | async-start | bytes 6684672 | tf_op jit(solution)/shard_map/all_gather | solution.py:1210
  13.4 13.3 %collective-permute-start.7 = (bf16[384,512]{1,0:T(8,128)(2,1)S(1)}, bf16[384,512]{1,0:T(8,128)(2,1)S(1)}, u32[]{:S(2)}, u32[]{:S(2)}) collective-permute-start(bf16[384,512]{1,0:T(8,128)(2,1)S(1)} %slice_bitcast_fusion.1.refs_6_.refs_7_.refs_16_), channel_id=1, source_target_pairs={{0,1},{1,0},{2,3},{3,2},{4,5},{5,4},{6,7},{7,6},{8,9},{9,8},{10,11... | collective-permute-start | bytes 1179656 | tf_op jit(solution)/shard_map/ppermute | solution.py:66
  16.3 53.2 %collective-permute-start.14 = (bf16[384,1536]{1,0:T(8,128)(2,1)}, bf16[384,1536]{1,0:T(8,128)(2,1)}, u32[]{:S(2)}, u32[]{:S(2)}) collective-permute-start(bf16[384,1536]{1,0:T(8,128)(2,1)} %slice_bitcast_fusion.refs_2_.refs_7_.refs_10_), channel_id=1, source_target_pairs={{0,1},{1,0},{2,3},{3,2},{4,5},{5,4},{6,7},{7,6},{8,9},{9,8},{10,11... | collective-permute-start | bytes 3538952 | tf_op jit(solution)/shard_map/ppermute | solution.py:66
  26.1 16.3 %collective-permute-start.12 = (bf16[192,1536]{1,0:T(8,128)(2,1)S(1)}, bf16[192,1536]{1,0:T(8,128)(2,1)S(1)}, u32[]{:S(2)}, u32[]{:S(2)}) collective-permute-start(bf16[192,1536]{1,0:T(8,128)(2,1)S(1)} %rows_of.2), channel_id=1, source_target_pairs={{0,2},{1,3},{2,0},{3,1},{4,6},{5,7},{6,4},{7,5},{8,10},{9,11},{10,... | collective-permute-start | bytes 1769480 | tf_op jit(solution)/shard_map/ppermute | solution.py:66
  32.6 31.4 %collective-permute-start.17 = (bf16[192,1536]{1,0:T(8,128)(2,1)S(1)}, bf16[192,1536]{1,0:T(8,128)(2,1)}, u32[]{:S(2)}, u32[]{:S(2)}) collective-permute-start(bf16[192,1536]{1,0:T(8,128)(2,1)S(1)} %rows_of.3), channel_id=1, source_target_pairs={{0,2},{1,3},{2,0},{3,1},{4,6},{5,7},{6,4},{7,5},{8,10},{9,11},{10,... | collective-permute-start | bytes 1769480 | tf_op jit(solution)/shard_map/ppermute | solution.py:66
  42.4 27.1 %collective-permute-start.13 = (bf16[192,1536]{1,0:T(8,128)(2,1)S(1)}, bf16[192,1536]{1,0:T(8,128)(2,1)}, u32[]{:S(2)}, u32[]{:S(2)}) collective-permute-start(bf16[192,1536]{1,0:T(8,128)(2,1)S(1)} %collective-permute-done.12.refs_8_.refs_11_), channel_id=1, source_target_pairs={{0,4},{4,0},{8,12},{12,8},{1,5},{5,1},{9,13},{13,9},{2,6},{6,2},{1... | collective-permute-start | bytes 1769480 | tf_op jit(solution)/shard_map/ppermute | solution.py:66
  44.0 15.9 %collective-permute-start.10 = (bf16[128,512]{1,0:T(8,128)(2,1)S(1)}, bf16[128,512]{1,0:T(8,128)(2,1)S(1)}, u32[]{:S(2)}, u32[]{:S(2)}) collective-permute-start(bf16[128,512]{1,0:T(8,128)(2,1)S(1)} %project.6.refs_0_.refs_1_), channel_id=1, source_target_pairs={{0,8},{4,12},{8,0},{12,4},{1,9},{5,13},{9,1},{13,5},{2,10},{6,14},... | collective-permute-start | bytes 393224 | tf_op jit(solution)/shard_map/ppermute | solution.py:66
  46.6 19.7 %collective-permute-start.11 = (bf16[128,512]{1,0:T(8,128)(2,1)S(1)}, bf16[128,512]{1,0:T(8,128)(2,1)S(1)}, u32[]{:S(2)}, u32[]{:S(2)}) collective-permute-start(bf16[128,512]{1,0:T(8,128)(2,1)S(1)} %project.6.refs_0_.refs_1_), channel_id=1, source_target_pairs={{0,12},{4,8},{8,4},{12,0},{1,13},{5,9},{9,5},{13,1},{2,14},{6,10},... | collective-permute-start | bytes 393224 | tf_op jit(solution)/shard_map/ppermute | solution.py:66
  64.1 16.7 %collective-permute-start.18 = (bf16[192,1536]{1,0:T(8,128)(2,1)}, bf16[192,1536]{1,0:T(8,128)(2,1)}, u32[]{:S(2)}, u32[]{:S(2)}) collective-permute-start(bf16[192,1536]{1,0:T(8,128)(2,1)} %collective-permute-done.17.refs_7_.refs_10_.refs_9_), channel_id=1, source_target_pairs={{0,4},{4,0},{8,12},{12,8},{1,5},{5,1},{9,13},{13,9},{2,6},{6,2},{1... | collective-permute-start | bytes 1769480 | tf_op jit(solution)/shard_map/ppermute | solution.py:66
  66.3 19.6 %collective-permute-start.19 = (bf16[384,1536]{1,0:T(8,128)(2,1)}, bf16[384,1536]{1,0:T(8,128)(2,1)}, u32[]{:S(2)}, u32[]{:S(2)}) collective-permute-start(bf16[384,1536]{1,0:T(8,128)(2,1)} %bitcast.98), channel_id=1, source_target_pairs={{0,1},{1,0},{2,3},{3,2},{4,5},{5,4},{6,7},{7,6},{8,9},{9,8},{10,11... | collective-permute-start | bytes 3538952 | tf_op jit(solution)/shard_map/ppermute | solution.py:66
  94.4 17.7 %collective-permute-start.26 = (bf16[128,1536]{1,0:T(8,128)(2,1)S(1)}, bf16[128,1536]{1,0:T(8,128)(2,1)S(1)}, u32[]{:S(2)}, u32[]{:S(2)}) collective-permute-start(bf16[128,1536]{1,0:T(8,128)(2,1)S(1)} %get-tuple-element.114.refs_1_.refs_5_), channel_id=1, source_target_pairs={{0,1},{1,0},{2,3},{3,2},{4,5},{5,4},{6,7},{7,6},{8,9},{9,8},{10,11... | collective-permute-start | bytes 1179656 | tf_op jit(solution)/shard_map/ppermute | solution.py:66
  166.0 15.0 %collective-permute-start = (bf16[128,1536]{1,0:T(8,128)(2,1)S(1)}, bf16[128,1536]{1,0:T(8,128)(2,1)S(1)}, u32[]{:S(2)}, u32[]{:S(2)}) collective-permute-start(bf16[128,1536]{1,0:T(8,128)(2,1)S(1)} %select_n.202.refs_9_.refs_3_.refs_2_), channel_id=1, source_target_pairs={{0,2},{1,3},{2,0},{3,1},{4,6},{5,7},{6,4},{7,5},{8,10},{9,11},{10,... | collective-permute-start | bytes 1179656 | tf_op jit(solution)/shard_map/ppermute | solution.py:66
  167.6 15.1 %collective-permute-start.35 = (bf16[512,512]{1,0:T(8,128)(2,1)S(1)}, bf16[512,512]{1,0:T(8,128)(2,1)S(1)}, u32[]{:S(2)}, u32[]{:S(2)}) collective-permute-start(bf16[512,512]{1,0:T(8,128)(2,1)S(1)} %join.4.refs_3_.refs_15_.refs_19_), channel_id=1, source_target_pairs={{0,1},{1,0},{2,3},{3,2},{4,5},{5,4},{6,7},{7,6},{8,9},{9,8},{10,11... | collective-permute-start | bytes 1572872 | tf_op jit(solution)/shard_map/ppermute | solution.py:66
  195.5 460.7 %all-gather.7.cloned.1.call-start = ((), (), s32[]{:S(2)}) async-start(), calls=%async_computation.1 | async-start | bytes 6684672 | tf_op jit(solution)/shard_map/all_gather | solution.py:1210
  196.5 18.8 %collective-permute-start.38 = (bf16[128,1536]{1,0:T(8,128)(2,1)S(1)}, bf16[128,1536]{1,0:T(8,128)(2,1)S(1)}, u32[]{:S(2)}, u32[]{:S(2)}) collective-permute-start(bf16[128,1536]{1,0:T(8,128)(2,1)S(1)} %get-tuple-element.122.refs_1_.refs_5_.refs_2_), channel_id=1, source_target_pairs={{0,1},{1,0},{2,3},{3,2},{4,5},{5,4},{6,7},{7,6},{8,9},{9,8},{10,11... | collective-permute-start | bytes 1179656 | tf_op jit(solution)/shard_map/ppermute | solution.py:66
  251.6 16.6 %collective-permute-start.42 = (bf16[256,1536]{1,0:T(8,128)(2,1)S(1)}, bf16[256,1536]{1,0:T(8,128)(2,1)S(1)}, u32[]{:S(2)}, u32[]{:S(2)}) collective-permute-start(bf16[256,1536]{1,0:T(8,128)(2,1)S(1)} %get-tuple-element.129), channel_id=1, source_target_pairs={{0,1},{1,0},{2,3},{3,2},{4,5},{5,4},{6,7},{7,6},{8,9},{9,8},{10,11... | collective-permute-start | bytes 2359304 | tf_op jit(solution)/shard_map/ppermute | solution.py:66
  291.3 13.4 %collective-permute-start.46 = (bf16[128,512]{1,0:T(8,128)(2,1)S(1)}, bf16[128,512]{1,0:T(8,128)(2,1)S(1)}, u32[]{:S(2)}, u32[]{:S(2)}) collective-permute-start(bf16[128,512]{1,0:T(8,128)(2,1)S(1)} %project.10.refs_0_.refs_1_), channel_id=1, source_target_pairs={{0,4},{4,0},{8,12},{12,8},{1,5},{5,1},{9,13},{13,9},{2,6},{6,2},{1... | collective-permute-start | bytes 393224 | tf_op jit(solution)/shard_map/ppermute | solution.py:66
  312.5 15.0 %collective-permute-start.53 = (bf16[512,512]{1,0:T(8,128)(2,1)S(1)}, bf16[512,512]{1,0:T(8,128)(2,1)}, u32[]{:S(2)}, u32[]{:S(2)}) collective-permute-start(bf16[512,512]{1,0:T(8,128)(2,1)S(1)} %join.5.refs_0_.refs_12_.refs_22_), channel_id=1, source_target_pairs={{0,2},{1,3},{2,0},{3,1},{4,6},{5,7},{6,4},{7,5},{8,10},{9,11},{10,... | collective-permute-start | bytes 1572872 | tf_op jit(solution)/shard_map/ppermute | solution.py:66
  312.9 23.9 %collective-permute-start.49 = (bf16[512,512]{1,0:T(8,128)(2,1)S(1)}, bf16[512,512]{1,0:T(8,128)(2,1)S(1)}, u32[]{:S(2)}, u32[]{:S(2)}) collective-permute-start(bf16[512,512]{1,0:T(8,128)(2,1)S(1)} %add_up.20.refs_0_), channel_id=1, source_target_pairs={{0,2},{1,3},{2,0},{3,1},{4,6},{5,7},{6,4},{7,5},{8,10},{9,11},{10,... | collective-permute-start | bytes 1572872 | tf_op jit(solution)/shard_map/ppermute | solution.py:66
  314.6 46.8 %collective-permute-start.54 = (bf16[512,512]{1,0:T(8,128)(2,1)S(1)}, bf16[512,512]{1,0:T(8,128)(2,1)}, u32[]{:S(2)}, u32[]{:S(2)}) collective-permute-start(bf16[512,512]{1,0:T(8,128)(2,1)S(1)} %join.5.refs_0_.refs_12_.refs_22_), channel_id=1, source_target_pairs={{0,1},{1,0},{2,3},{3,2},{4,5},{5,4},{6,7},{7,6},{8,9},{9,8},{10,11... | collective-permute-start | bytes 1572872 | tf_op jit(solution)/shard_map/ppermute | solution.py:66
  327.5 33.8 %collective-permute-start.55 = (bf16[512,512]{1,0:T(8,128)(2,1)}, bf16[512,512]{1,0:T(8,128)(2,1)}, u32[]{:S(2)}, u32[]{:S(2)}) collective-permute-start(bf16[512,512]{1,0:T(8,128)(2,1)} %collective-permute-done.53.refs_13_.refs_24_), channel_id=1, source_target_pairs={{0,1},{1,0},{2,3},{3,2},{4,5},{5,4},{6,7},{7,6},{8,9},{9,8},{10,11... | collective-permute-start | bytes 1572872 | tf_op jit(solution)/shard_map/ppermute | solution.py:66
  373.2 424.6 %all-gather.9.cloned.1.call-start = ((), (), s32[]{:S(2)}) async-start(), calls=%async_computation.2 | async-start | bytes 6684672 | tf_op jit(solution)/shard_map/all_gather | solution.py:1210
  373.6 20.7 %collective-permute-start.57 = (bf16[128,1536]{1,0:T(8,128)(2,1)S(1)}, bf16[128,1536]{1,0:T(8,128)(2,1)S(1)}, u32[]{:S(2)}, u32[]{:S(2)}) collective-permute-start(bf16[128,1536]{1,0:T(8,128)(2,1)S(1)} %get-tuple-element.144.refs_6_.refs_1_.refs_2_), channel_id=1, source_target_pairs={{0,2},{1,3},{2,0},{3,1},{4,6},{5,7},{6,4},{7,5},{8,10},{9,11},{10,... | collective-permute-start | bytes 1179656 | tf_op jit(solution)/shard_map/ppermute | solution.py:66
  375.4 26.1 %collective-permute-start.61 = (bf16[128,1536]{1,0:T(8,128)(2,1)S(1)}, bf16[128,1536]{1,0:T(8,128)(2,1)S(1)}, u32[]{:S(2)}, u32[]{:S(2)}) collective-permute-start(bf16[128,1536]{1,0:T(8,128)(2,1)S(1)} %select.66.refs_0_.refs_13_.refs_3_.refs_1_.refs_2_), channel_id=1, source_target_pairs={{0,1},{1,0},{2,3},{3,2},{4,5},{5,4},{6,7},{7,6},{8,9},{9,8},{10,11... | collective-permute-start | bytes 1179656 | tf_op jit(solution)/shard_map/ppermute | solution.py:66
  375.4 26.1 %collective-permute-start.58 = (bf16[128,1536]{1,0:T(8,128)(2,1)S(1)}, bf16[128,1536]{1,0:T(8,128)(2,1)S(1)}, u32[]{:S(2)}, u32[]{:S(2)}) collective-permute-start(bf16[128,1536]{1,0:T(8,128)(2,1)S(1)} %get-tuple-element.144.refs_6_.refs_1_.refs_2_), channel_id=1, source_target_pairs={{0,1},{1,0},{2,3},{3,2},{4,5},{5,4},{6,7},{7,6},{8,9},{9,8},{10,11... | collective-permute-start | bytes 1179656 | tf_op jit(solution)/shard_map/ppermute | solution.py:66
  386.1 15.4 %collective-permute-start.62 = (bf16[128,1536]{1,0:T(8,128)(2,1)S(1)}, bf16[128,1536]{1,0:T(8,128)(2,1)S(1)}, u32[]{:S(2)}, u32[]{:S(2)}) collective-permute-start(bf16[128,1536]{1,0:T(8,128)(2,1)S(1)} %collective-permute-done.60.refs_14_), channel_id=1, source_target_pairs={{0,1},{1,0},{2,3},{3,2},{4,5},{5,4},{6,7},{7,6},{8,9},{9,8},{10,11... | collective-permute-start | bytes 1179656 | tf_op jit(solution)/shard_map/ppermute | solution.py:66
  426.8 371.0 %all-gather.11.cloned.1.call-start = ((), (), s32[]{:S(2)}) async-start(), calls=%async_computation.3 | async-start | bytes 6684672 | tf_op jit(solution)/shard_map/all_gather | solution.py:1210
  456.5 14.0 %collective-permute-start.66 = (bf16[512,512]{1,0:T(8,128)(2,1)S(1)}, bf16[512,512]{1,0:T(8,128)(2,1)S(1)}, u32[]{:S(2)}, u32[]{:S(2)}) collective-permute-start(bf16[512,512]{1,0:T(8,128)(2,1)S(1)} %add_up.23.refs_0_), channel_id=1, source_target_pairs={{0,2},{1,3},{2,0},{3,1},{4,6},{5,7},{6,4},{7,5},{8,10},{9,11},{10,... | collective-permute-start | bytes 1572872 | tf_op jit(solution)/shard_map/ppermute | solution.py:66
  470.7 17.7 %collective-permute-start.67 = (bf16[128,512]{1,0:T(8,128)(2,1)S(1)}, bf16[128,512]{1,0:T(8,128)(2,1)S(1)}, u32[]{:S(2)}, u32[]{:S(2)}) collective-permute-start(bf16[128,512]{1,0:T(8,128)(2,1)S(1)} %get-tuple-element.154), channel_id=1, source_target_pairs={{0,4},{4,0},{8,12},{12,8},{1,5},{5,1},{9,13},{13,9},{2,6},{6,2},{1... | collective-permute-start | bytes 393224 | tf_op jit(solution)/shard_map/ppermute | solution.py:66
  477.2 20.4 %collective-permute-start.68 = (bf16[128,512]{1,0:T(8,128)(2,1)S(1)}, bf16[128,512]{1,0:T(8,128)(2,1)S(1)}, u32[]{:S(2)}, u32[]{:S(2)}) collective-permute-start(bf16[128,512]{1,0:T(8,128)(2,1)S(1)} %get-tuple-element.155), channel_id=1, source_target_pairs={{0,8},{4,12},{8,0},{12,4},{1,9},{5,13},{9,1},{13,5},{2,10},{6,14},... | collective-permute-start | bytes 393224 | tf_op jit(solution)/shard_map/ppermute | solution.py:66
  477.2 20.4 %collective-permute-start.69 = (bf16[128,512]{1,0:T(8,128)(2,1)S(1)}, bf16[128,512]{1,0:T(8,128)(2,1)S(1)}, u32[]{:S(2)}, u32[]{:S(2)}) collective-permute-start(bf16[128,512]{1,0:T(8,128)(2,1)S(1)} %get-tuple-element.156), channel_id=1, source_target_pairs={{0,12},{4,8},{8,4},{12,0},{1,13},{5,9},{9,5},{13,1},{2,14},{6,10},... | collective-permute-start | bytes 393224 | tf_op jit(solution)/shard_map/ppermute | solution.py:66
  514.5 14.5 %collective-permute-start.72 = (bf16[128,1536]{1,0:T(8,128)(2,1)S(1)}, bf16[128,1536]{1,0:T(8,128)(2,1)S(1)}, u32[]{:S(2)}, u32[]{:S(2)}) collective-permute-start(bf16[128,1536]{1,0:T(8,128)(2,1)S(1)} %collective-permute-done.70.refs_9_.refs_3_.refs_1_), channel_id=1, source_target_pairs={{0,1},{1,0},{2,3},{3,2},{4,5},{5,4},{6,7},{7,6},{8,9},{9,8},{10,11... | collective-permute-start | bytes 1179656 | tf_op jit(solution)/shard_map/ppermute | solution.py:66
  551.3 13.0 %collective-permute-start.74 = (bf16[256,1536]{1,0:T(8,128)(2,1)S(1)}, bf16[256,1536]{1,0:T(8,128)(2,1)S(1)}, u32[]{:S(2)}, u32[]{:S(2)}) collective-permute-start(bf16[256,1536]{1,0:T(8,128)(2,1)S(1)} %get-tuple-element.163), channel_id=1, source_target_pairs={{0,1},{1,0},{2,3},{3,2},{4,5},{5,4},{6,7},{7,6},{8,9},{9,8},{10,11... | collective-permute-start | bytes 2359304 | tf_op jit(solution)/shard_map/ppermute | solution.py:66
  590.6 14.0 %collective-permute-start.77 = (bf16[512,512]{1,0:T(8,128)(2,1)S(1)}, bf16[512,512]{1,0:T(8,128)(2,1)S(1)}, u32[]{:S(2)}, u32[]{:S(2)}) collective-permute-start(bf16[512,512]{1,0:T(8,128)(2,1)S(1)} %add_up.26.refs_0_), channel_id=1, source_target_pairs={{0,2},{1,3},{2,0},{3,1},{4,6},{5,7},{6,4},{7,5},{8,10},{9,11},{10,... | collective-permute-start | bytes 1572872 | tf_op jit(solution)/shard_map/ppermute | solution.py:66
  604.9 15.1 %collective-permute-start.78 = (bf16[128,512]{1,0:T(8,128)(2,1)S(1)}, bf16[128,512]{1,0:T(8,128)(2,1)S(1)}, u32[]{:S(2)}, u32[]{:S(2)}) collective-permute-start(bf16[128,512]{1,0:T(8,128)(2,1)S(1)} %get-tuple-element.170), channel_id=1, source_target_pairs={{0,4},{4,0},{8,12},{12,8},{1,5},{5,1},{9,13},{13,9},{2,6},{6,2},{1... | collective-permute-start | bytes 393224 | tf_op jit(solution)/shard_map/ppermute | solution.py:66
  645.9 30.8 %collective-permute-start.82 = (bf16[384,3584]{1,0:T(8,128)(2,1)}, bf16[384,3584]{1,0:T(8,128)(2,1)}, u32[]{:S(2)}, u32[]{:S(2)}) collective-permute-start(bf16[384,3584]{1,0:T(8,128)(2,1)} %get-tuple-element.190), channel_id=1, source_target_pairs={{0,1},{1,0},{2,3},{3,2},{4,5},{5,4},{6,7},{7,6},{8,9},{9,8},{10,11... | collective-permute-start | bytes 8257544 | tf_op jit(solution)/shard_map/ppermute | solution.py:66
  650.0 33.3 %collective-permute-start.81 = (bf16[384,3584]{1,0:T(8,128)(2,1)}, bf16[384,3584]{1,0:T(8,128)(2,1)}, u32[]{:S(2)}, u32[]{:S(2)}) collective-permute-start(bf16[384,3584]{1,0:T(8,128)(2,1)} %copy-done.57), channel_id=1, source_target_pairs={{0,1},{1,0},{2,3},{3,2},{4,5},{5,4},{6,7},{7,6},{8,9},{9,8},{10,11... | collective-permute-start | bytes 8257544 | tf_op jit(solution)/shard_map/ppermute | solution.py:66
  654.5 111.4 %collective-permute-start.88 = (bf16[128,1536]{1,0:T(8,128)(2,1)}, bf16[128,1536]{1,0:T(8,128)(2,1)}, u32[]{:S(2)}, u32[]{:S(2)}) collective-permute-start(bf16[128,1536]{1,0:T(8,128)(2,1)} %add_up.28.refs_0_), channel_id=1, source_target_pairs={{0,2},{1,3},{2,0},{3,1},{4,6},{5,7},{6,4},{7,5},{8,10},{9,11},{10,... | collective-permute-start | bytes 1179656 | tf_op jit(solution)/shard_map/ppermute | solution.py:66
  682.3 87.6 %collective-permute-start.83 = (bf16[384,3584]{1,0:T(8,128)(2,1)}, bf16[384,3584]{1,0:T(8,128)(2,1)}, u32[]{:S(2)}, u32[]{:S(2)}) collective-permute-start(bf16[384,3584]{1,0:T(8,128)(2,1)} %add_convert_fusion.1), channel_id=1, source_target_pairs={{0,2},{1,3},{2,0},{3,1},{4,6},{5,7},{6,4},{7,5},{8,10},{9,11},{10,... | collective-permute-start | bytes 8257544 | tf_op jit(solution)/shard_map/ppermute | solution.py:66
  683.2 80.0 %collective-permute-start.89 = (f32[40,128]{1,0:T(8,128)S(1)}, f32[40,128]{1,0:T(8,128)S(1)}, u32[]{:S(2)}, u32[]{:S(2)}) collective-permute-start(f32[40,128]{1,0:T(8,128)S(1)} %bitcast.105), channel_id=1, source_target_pairs={{0,1},{1,0},{2,3},{3,2},{4,5},{5,4},{6,7},{7,6},{8,9},{9,8},{10,11... | collective-permute-start | bytes 61448 | tf_op jit(solution)/shard_map/ppermute | solution.py:66
  767.6 87.2 %collective-permute-start.91 = (f32[40,128]{1,0:T(8,128)S(1)}, f32[40,128]{1,0:T(8,128)S(1)}, u32[]{:S(2)}, u32[]{:S(2)}) collective-permute-start(f32[40,128]{1,0:T(8,128)S(1)} %add.331), channel_id=1, source_target_pairs={{0,8},{4,12},{8,0},{12,4},{1,9},{5,13},{9,1},{13,5},{2,10},{6,14},... | collective-permute-start | bytes 61448 | tf_op jit(solution)/shard_map/ppermute | solution.py:66
  775.0 72.0 %collective-permute-start.84 = (bf16[96,3584]{1,0:T(8,128)(2,1)S(1)}, bf16[96,3584]{1,0:T(8,128)(2,1)}, u32[]{:S(2)}, u32[]{:S(2)}) collective-permute-start(bf16[96,3584]{1,0:T(8,128)(2,1)S(1)} %get-tuple-element.216), channel_id=1, source_target_pairs={{0,4},{4,0},{8,12},{12,8},{1,5},{5,1},{9,13},{13,9},{2,6},{6,2},{1... | collective-permute-start | bytes 2064392 | tf_op jit(solution)/shard_map/ppermute | solution.py:66
  776.4 70.6 %collective-permute-start.85 = (bf16[96,3584]{1,0:T(8,128)(2,1)S(1)}, bf16[96,3584]{1,0:T(8,128)(2,1)}, u32[]{:S(2)}, u32[]{:S(2)}) collective-permute-start(bf16[96,3584]{1,0:T(8,128)(2,1)S(1)} %get-tuple-element.215), channel_id=1, source_target_pairs={{0,8},{4,12},{8,0},{12,4},{1,9},{5,13},{9,1},{13,5},{2,10},{6,14},... | collective-permute-start | bytes 2064392 | tf_op jit(solution)/shard_map/ppermute | solution.py:66
  779.3 67.7 %collective-permute-start.86 = (bf16[96,3584]{1,0:T(8,128)(2,1)S(1)}, bf16[96,3584]{1,0:T(8,128)(2,1)}, u32[]{:S(2)}, u32[]{:S(2)}) collective-permute-start(bf16[96,3584]{1,0:T(8,128)(2,1)S(1)} %get-tuple-element.214), channel_id=1, source_target_pairs={{0,12},{4,8},{8,4},{12,0},{1,13},{5,9},{9,5},{13,1},{2,14},{6,10},... | collective-permute-start | bytes 2064392 | tf_op jit(solution)/shard_map/ppermute | solution.py:66
  850.4 76.1 %collective-permute-start.93 = (bf16[96,3584]{1,0:T(8,128)(2,1)}, bf16[96,3584]{1,0:T(8,128)(2,1)S(1)}, u32[]{:S(2)}, u32[]{:S(2)}) collective-permute-start(bf16[96,3584]{1,0:T(8,128)(2,1)} %add_convert_fusion.3.refs_0_.refs_2_), channel_id=1, source_target_pairs={{0,4},{4,0},{8,12},{12,8},{1,5},{5,1},{9,13},{13,9},{2,6},{6,2},{1... | collective-permute-start | bytes 2064392 | tf_op jit(solution)/shard_map/ppermute | solution.py:66
  850.9 75.6 %collective-permute-start.94 = (bf16[96,3584]{1,0:T(8,128)(2,1)}, bf16[96,3584]{1,0:T(8,128)(2,1)S(1)}, u32[]{:S(2)}, u32[]{:S(2)}) collective-permute-start(bf16[96,3584]{1,0:T(8,128)(2,1)} %add_convert_fusion.3.refs_0_.refs_2_), channel_id=1, source_target_pairs={{0,8},{4,12},{8,0},{12,4},{1,9},{5,13},{9,1},{13,5},{2,10},{6,14},... | collective-permute-start | bytes 2064392 | tf_op jit(solution)/shard_map/ppermute | solution.py:66
  854.7 71.8 %collective-permute-start.95 = (bf16[96,3584]{1,0:T(8,128)(2,1)}, bf16[96,3584]{1,0:T(8,128)(2,1)}, u32[]{:S(2)}, u32[]{:S(2)}) collective-permute-start(bf16[96,3584]{1,0:T(8,128)(2,1)} %add_convert_fusion.3.refs_0_.refs_2_), channel_id=1, source_target_pairs={{0,12},{4,8},{8,4},{12,0},{1,13},{5,9},{9,5},{13,1},{2,14},{6,10},... | collective-permute-start | bytes 2064392 | tf_op jit(solution)/shard_map/ppermute | solution.py:66
  855.5 68.6 %collective-permute-start.92 = (f32[40,128]{1,0:T(8,128)S(1)}, f32[40,128]{1,0:T(8,128)S(1)}, u32[]{:S(2)}, u32[]{:S(2)}) collective-permute-start(f32[40,128]{1,0:T(8,128)S(1)} %add_add_fusion), channel_id=1, source_target_pairs={{0,4},{4,0},{8,12},{12,8},{1,5},{5,1},{9,13},{13,9},{2,6},{6,2},{1... | collective-permute-start | bytes 61448 | tf_op jit(solution)/shard_map/ppermute | solution.py:66
  (153 other events, 3228.5 us)
Sparse Core Ops, SparseCore 0:
  195.6 65.4 all-gather.4
  373.4 64.9 all-gather.6
  440.7 69.4 all-gather.8
  650.1 78.4 all-gather.10

commit v4 on v3

--- a/solution.py
+++ b/solution.py
@@ -23,9 +23,10 @@
 LAG = 1
 FORWARD = "KJQAMRY"
 SEQUENCE = (
-    "K0 J0 Q0 A0 H M0 R0 Y0 K1 Q1 J1 A1 H M1 R1 "
-    "B0 Y1 S0 K2 T0 D0 J2 Q2 E0 P0 A2 G1 H "
-    "B1 S1 T1 D1 E1 P1 G2 H B2 M2 S2 T2 D2 E2 P2 "
+    "K0", "J0", "Q0", "A0", "H", "M0", "R0", "Y0", "K1", "Q1", "J1", "A1",
+    "H", "M1", "R1", "B0", "Y1", "S0", "K2", "T0", "D0", "J2", "Q2", "E0",
+    "P0", "A2", "G1", "H", "B1", "S1", "T1", "D1", "E1", "P1", "G2", "H",
+    "B2", "M2", "S2", "T2", "D2", "E2", "P2",
 )
 ROWS = 16
 UNITS = 512
@@ -1189,7 +1190,7 @@
         yield "P"
 
     running = {}
-    for name in SEQUENCE.split():
+    for name in SEQUENCE:
         if name == "H":
             near_weights[:] = hold(gate, up, down)
             continue

time: 947 us -> 947 us (level)
  no operation moved by 1% of the time
where the time goes in v4:
time: 947 us; the launch traced here: 937 us
  Pallas kernels  474 us (50%)
  waiting for transfers between devices  282 us (30%)
  starting transfers between devices  103 us (11%)
  local copies, waits for them, and re-layouts  40.1 us (4%)
  other arithmetic  22 us (2%)
  between operations  15.9 us (2%)
    pallas_call x59, Pallas kernels, call(): pl.pallas_call(body, out_shape=out_shape, in_specs=[*[ANY] * len(waits),...  474 us
    ppermute x92, waiting for transfers between devices, exchange(): return lax.ppermute(block, axis, [(i, i ^ mask) for i in range(size)])  257 us
    ppermute x92, starting transfers between devices, exchange(): return lax.ppermute(block, axis, [(i, i ^ mask) for i in range(size)])  91.3 us
    ppermute x4, waiting for transfers between devices, passed_along(): return lax.ppermute(block, axis, route)  25.6 us
    unnamed x209, local copies, waits for them, and re-layouts  23.2 us
  transfers between devices with their start and end apart: 100, of which 44 were waited for; matrix products, arithmetic and copies ran while one was open for 4% of the time, Pallas kernels for 47%

profile of v4, /device:TPU:0, one launch (start us, length us, event | category | flops | bytes accessed | tf_op | source)
XLA Modules:
  0.0 937.4 jit_solution(17775724603572576547)
XLA Ops:
  34.4 8.0 collective-permute-done.12.refs_8_.refs_11_
  46.8 13.1 %collective-permute-done.10.refs_3_ = bf16[128,512]{1,0:T(8,128)(2,1)S(1)} collective-permute-done((bf16[128,512]{1,0:T(8,128)(2,1)S(1)}, bf16[128,512]{1,0:T(8,128)(2,1)S(1)}, u32[]{:S(2)}, u32[]{:S(2)}) %collective-permute-start.10) | collective-permute-done | bytes 131104 | tf_op jit(solution)/shard_map/ppermute | solution.py:67
  70.0 10.8 %collective-permute-done.22.refs_13_.refs_23_ = bf16[512,512]{1,0:T(8,128)(2,1)S(1)} collective-permute-done((bf16[512,512]{1,0:T(8,128)(2,1)S(1)}, bf16[512,512]{1,0:T(8,128)(2,1)S(1)}, u32[]{:S(2)}, u32[]{:S(2)}) %collective-permute-start.22) | collective-permute-done | bytes 524320 | tf_op jit(solution)/shard_map/ppermute | solution.py:67
  94.4 10.6 %collective-permute-done.25.refs_2_.refs_7_ = bf16[128,1536]{1,0:T(8,128)(2,1)S(1)} collective-permute-done((bf16[128,1536]{1,0:T(8,128)(2,1)S(1)}, bf16[128,1536]{1,0:T(8,128)(2,1)S(1)}, u32[]{:S(2)}, u32[]{:S(2)}) %collective-permute-start.25) | collective-permute-done | bytes 393248 | tf_op jit(solution)/shard_map/ppermute | solution.py:67
  105.0 7.0 hold.4
  112.1 11.4 %mlp.3 = (bf16[256,1536]{1,0:T(8,128)(2,1)S(1)}, bf16[256,1536]{1,0:T(8,128)(2,1)S(1)}) custom-call(bf16[2240,1536]{1,0:T(8,128)(2,1)S(1)} %get-tuple-element.113.refs_0_.refs_5_, bf16[128,1536]{1,0:T(8,128)(2,1)S(1)} %get-tuple-element.114.refs_1_.refs_5_, bf16[128,1536]{1,0:T(8,128)(2,1)S(1)} %collective-permute-done.25.refs_2_.refs_7_, ...), custom_call_target="tpu_custom_call" | custom-call | flops 10569646080 | bytes 3145728 | tf_op jit(solution)/shard_map/mlp/pallas_call | solution.py:119
  126.6 10.9 %collective-permute-done.29.refs_4_ = bf16[128,1536]{1,0:T(8,128)(2,1)S(1)} collective-permute-done((bf16[128,1536]{1,0:T(8,128)(2,1)S(1)}, bf16[128,1536]{1,0:T(8,128)(2,1)S(1)}, u32[]{:S(2)}, u32[]{:S(2)}) %collective-permute-start.29) | collective-permute-done | bytes 393248 | tf_op jit(solution)/shard_map/ppermute | solution.py:67
  141.3 7.9 collective-permute-done.30.refs_12_.refs_14_.refs_20_.refs_24_
  167.6 9.3 collective-permute-done.34.refs_16_.refs_20_
  185.0 7.0 attend.4
  196.5 10.6 %collective-permute-done.37.refs_2_.refs_6_ = bf16[128,1536]{1,0:T(8,128)(2,1)S(1)} collective-permute-done((bf16[128,1536]{1,0:T(8,128)(2,1)S(1)}, bf16[128,1536]{1,0:T(8,128)(2,1)S(1)}, u32[]{:S(2)}, u32[]{:S(2)}) %collective-permute-start.37) | collective-permute-done | bytes 393248 | tf_op jit(solution)/shard_map/ppermute | solution.py:67
  208.3 6.9 hold.5
  215.3 11.5 %mlp.4 = (bf16[256,1536]{1,0:T(8,128)(2,1)S(1)}, bf16[256,1536]{1,0:T(8,128)(2,1)S(1)}) custom-call(bf16[2240,1536]{1,0:T(8,128)(2,1)S(1)} %get-tuple-element.121.refs_0_.refs_5_.refs_2_, bf16[128,1536]{1,0:T(8,128)(2,1)S(1)} %get-tuple-element.122.refs_1_.refs_5_.refs_2_, bf16[128,1536]{1,0:T(8,128)(2,1)S(1)} %collective-permute-done.37.refs_2_.refs_6_, ...), custom_call_target="tpu_custom_call" | custom-call | flops 10569646080 | bytes 3145728 | tf_op jit(solution)/shard_map/mlp/pallas_call | solution.py:119
  229.3 22.2 %mlp_back.3 = (bf16[256,1536]{1,0:T(8,128)(2,1)S(1)}, bf16[256,1536]{1,0:T(8,128)(2,1)S(1)}) custom-call(bf16[128,1536]{1,0:T(8,128)(2,1)S(1)} %add_up.17.refs_0_, s32[5]{0:T(128)S(1)} %stack.81.refs_0_.refs_1_.refs_4_, bf16[2240,1536]{1,0:T(8,128)(2,1)S(1)} %get-tuple-element.121.refs_0_.refs_5_.refs_2_, ...), custom_call_target="tpu_custom_call" | custom-call | flops 17616076800 | bytes 4718592 | tf_op jit(solution)/shard_map/mlp_back/pallas_call | solution.py:119
  252.7 10.5 %collective-permute-done.41.refs_4_ = bf16[128,1536]{1,0:T(8,128)(2,1)S(1)} collective-permute-done((bf16[128,1536]{1,0:T(8,128)(2,1)S(1)}, bf16[128,1536]{1,0:T(8,128)(2,1)S(1)}, u32[]{:S(2)}, u32[]{:S(2)}) %collective-permute-start.41) | collective-permute-done | bytes 393248 | tf_op jit(solution)/shard_map/ppermute | solution.py:67
  268.7 7.3 collective-permute-done.43.refs_11_.refs_13_.refs_16_.refs_25_
  278.5 12.0 %attend_back.3 = (f32[128,1536]{1,0:T(8,128)S(1)}, bf16[128,1536]{1,0:T(8,128)(2,1)S(1)}, bf16[128,1536]{1,0:T(8,128)(2,1)S(1)}, f32[1,1536]{1,0:T(1,128)S(1)}, ...) custom-call(bf16[128,512]{1,0:T(8,128)(2,1)S(1)} %project.10.refs_0_.refs_1_, ...), custom_call_target="tpu_custom_call" | custom-call | flops 6643777536 | bytes 8126464 | tf_op jit(solution)/shard_map/attend_back/pallas_call | solution.py:119
  291.3 8.5 collective-permute-start.46
  304.7 7.7 collective-permute-done.47.refs_3_
  314.6 12.9 %collective-permute-done.53.refs_13_.refs_24_ = bf16[512,512]{1,0:T(8,128)(2,1)} collective-permute-done((bf16[512,512]{1,0:T(8,128)(2,1)S(1)}, bf16[512,512]{1,0:T(8,128)(2,1)}, u32[]{:S(2)}, u32[]{:S(2)}) %collective-permute-start.53) | collective-permute-done | bytes 524320 | tf_op jit(solution)/shard_map/ppermute | solution.py:67
  344.4 7.6 collective-permute-done.51.refs_22_
  363.3 6.9 attend.5
  375.9 10.2 %collective-permute-done.60.refs_14_ = bf16[128,1536]{1,0:T(8,128)(2,1)S(1)} collective-permute-done((bf16[128,1536]{1,0:T(8,128)(2,1)S(1)}, bf16[128,1536]{1,0:T(8,128)(2,1)S(1)}, u32[]{:S(2)}, u32[]{:S(2)}) %collective-permute-start.60) | collective-permute-done | bytes 393248 | tf_op jit(solution)/shard_map/ppermute | solution.py:67
  386.1 8.2 collective-permute-done.57.refs_8_.refs_2_
  394.3 7.1 hold.6
  402.4 22.7 %mlp_back.4 = (bf16[256,1536]{1,0:T(8,128)(2,1)S(1)}, bf16[256,1536]{1,0:T(8,128)(2,1)}) custom-call(bf16[2240,1536]{1,0:T(8,128)(2,1)S(1)} %get-tuple-element.141.refs_0_.refs_2_, s32[5]{0:T(128)S(1)} %stack.81.refs_0_.refs_1_.refs_4_, bf16[2240,1536]{1,0:T(8,128)(2,1)S(1)} %get-tuple-element.141.refs_0_.refs_2_, ...), custom_call_target="tpu_custom_call" | custom-call | flops 17616076800 | bytes 4718592 | tf_op jit(solution)/shard_map/mlp_back/pallas_call | solution.py:119
  429.8 11.1 %collective-permute-done.64.refs_16_ = bf16[128,1536]{1,0:T(8,128)(2,1)S(1)} collective-permute-done((bf16[128,1536]{1,0:T(8,128)(2,1)S(1)}, bf16[128,1536]{1,0:T(8,128)(2,1)S(1)}, u32[]{:S(2)}, u32[]{:S(2)}) %collective-permute-start.64) | collective-permute-done | bytes 393248 | tf_op jit(solution)/shard_map/ppermute | solution.py:67
  440.9 12.7 %attend_back.4 = (f32[128,1536]{1,0:T(8,128)S(1)}, bf16[128,1536]{1,0:T(8,128)(2,1)S(1)}, bf16[128,1536]{1,0:T(8,128)(2,1)S(1)}, f32[1,1536]{1,0:T(1,128)S(1)}, ...) custom-call(bf16[128,1536]{1,0:T(8,128)(2,1)S(1)} %add_up.22.refs_0_, s32[5]{0:T(128)S(1)} %stack.81.refs_0_.refs_1_.refs_4_, ...), custom_call_target="tpu_custom_call" | custom-call | flops 6643777536 | bytes 8126464 | tf_op jit(solution)/shard_map/attend_back/pallas_call | solution.py:119
  456.8 13.7 %collective-permute-done.66.refs_3_ = bf16[512,512]{1,0:T(8,128)(2,1)S(1)} collective-permute-done((bf16[512,512]{1,0:T(8,128)(2,1)S(1)}, bf16[512,512]{1,0:T(8,128)(2,1)S(1)}, u32[]{:S(2)}, u32[]{:S(2)}) %collective-permute-start.66) | collective-permute-done | bytes 524320 | tf_op jit(solution)/shard_map/ppermute | solution.py:67
  470.7 6.5 collective-permute-start.67
  479.6 8.7 collective-permute-done.67.refs_21_
  488.4 9.3 collective-permute-done.68.refs_22_
  504.3 10.0 %collective-permute-done.70.refs_9_.refs_3_.refs_1_ = bf16[128,1536]{1,0:T(8,128)(2,1)S(1)} collective-permute-done((bf16[128,1536]{1,0:T(8,128)(2,1)S(1)}, bf16[128,1536]{1,0:T(8,128)(2,1)S(1)}, u32[]{:S(2)}, u32[]{:S(2)}) %collective-permute-start.70) | collective-permute-done | bytes 393248 | tf_op jit(solution)/shard_map/ppermute | solution.py:73
  514.5 7.6 collective-permute-done.71.refs_10_
  522.1 6.9 hold.7
  529.1 22.2 %mlp_back.5 = (bf16[256,1536]{1,0:T(8,128)(2,1)S(1)}, bf16[256,1536]{1,0:T(8,128)(2,1)S(1)}) custom-call(bf16[2240,1536]{1,0:T(8,128)(2,1)S(1)} %get-tuple-element.158.refs_0_.refs_2_.refs_5_, s32[5]{0:T(128)S(1)} %stack.81.refs_0_.refs_1_.refs_4_, bf16[2240,1536]{1,0:T(8,128)(2,1)S(1)} %get-tuple-element.158.refs_0_.refs_2_.refs_5_, ...), custom_call_target="tpu_custom_call" | custom-call | flops 17616076800 | bytes 4718592 | tf_op jit(solution)/shard_map/mlp_back/pallas_call | solution.py:119
  551.9 12.3 %mlp.5 = (bf16[256,1536]{1,0:T(8,128)(2,1)S(1)}, bf16[256,1536]{1,0:T(8,128)(2,1)}) custom-call(bf16[256,1536]{1,0:T(8,128)(2,1)S(1)} %get-tuple-element.161.refs_0_.refs_1_.refs_14_, bf16[128,1536]{1,0:T(8,128)(2,1)S(1)} %copy-done.33, bf16[128,1536]{1,0:T(8,128)(2,1)S(1)} %copy-done.75, bf16[128,1536]{1,0:T(8,128)(2,1)S(1)} %copy-done.77, ...), custom_call_target="tpu_custom_call" | custom-call | flops 10569646080 | bytes 3145728 | tf_op jit(solution)/shard_map/mlp/pallas_call | solution.py:119
  564.6 10.9 %collective-permute-done.75.refs_16_ = bf16[128,1536]{1,0:T(8,128)(2,1)S(1)} collective-permute-done((bf16[128,1536]{1,0:T(8,128)(2,1)S(1)}, bf16[128,1536]{1,0:T(8,128)(2,1)S(1)}, u32[]{:S(2)}, u32[]{:S(2)}) %collective-permute-start.75) | collective-permute-done | bytes 393248 | tf_op jit(solution)/shard_map/ppermute | solution.py:67
  575.5 12.2 %attend_back.5 = (f32[128,1536]{1,0:T(8,128)S(1)}, bf16[128,1536]{1,0:T(8,128)(2,1)S(1)}, bf16[128,1536]{1,0:T(8,128)(2,1)S(1)}, f32[1,1536]{1,0:T(1,128)S(1)}, ...) custom-call(bf16[128,1536]{1,0:T(8,128)(2,1)S(1)} %add_up.25.refs_0_, s32[5]{0:T(128)S(1)} %stack.81.refs_0_.refs_1_.refs_4_, ...), custom_call_target="tpu_custom_call" | custom-call | flops 6643777536 | bytes 8126464 | tf_op jit(solution)/shard_map/attend_back/pallas_call | solution.py:119
  591.0 13.7 %collective-permute-done.77.refs_3_ = bf16[512,512]{1,0:T(8,128)(2,1)S(1)} collective-permute-done((bf16[512,512]{1,0:T(8,128)(2,1)S(1)}, bf16[512,512]{1,0:T(8,128)(2,1)S(1)}, u32[]{:S(2)}, u32[]{:S(2)}) %collective-permute-start.77) | collective-permute-done | bytes 524320 | tf_op jit(solution)/shard_map/ppermute | solution.py:67
  604.9 11.1 %collective-permute-start.78 = (bf16[128,512]{1,0:T(8,128)(2,1)S(1)}, bf16[128,512]{1,0:T(8,128)(2,1)S(1)}, u32[]{:S(2)}, u32[]{:S(2)}) collective-permute-start(bf16[128,512]{1,0:T(8,128)(2,1)S(1)} %get-tuple-element.170), channel_id=1, source_target_pairs={{0,4},{4,0},{8,12},{12,8},{1,5},{5,1},{9,13},{13,9},{2,6},{6,2},{1... | collective-permute-start | bytes 393224 | tf_op jit(solution)/shard_map/ppermute | solution.py:67
  619.9 6.9 collective-permute-done.79.refs_22_
  632.2 10.0 %attention_grads.1 = (bf16[384,3584]{1,0:T(8,128)(2,1)S(1)}, bf16[384,3584]{1,0:T(8,128)(2,1)S(1)}, bf16[384,3584]{1,0:T(8,128)(2,1)S(1)}, bf16[384,3584]{1,0:T(8,128)(2,1)}, f32[1,5120]{1,0:T(1,128)S(1)}) custom-call(bf16[128,1536]{1,0:T(8,128)(2,1)S(1)} %get-tuple-element.173.refs_0_.refs_4_, s32[5]{0:T(128)S(1)} %stack.81.refs_0_.refs_1_.refs_4_, ...), custom_call_target="tpu_custom_call" | custom-call | flops 4227858432 | bytes 14942208 | tf_op jit(solution)/shard_map/attention_grads/pallas_call | solution.py:119
  656.2 19.2 %weight_grads.5 = (f32[2240,1536]{1,0:T(8,128)}, f32[2240,1536]{1,0:T(8,128)}, f32[2240,1536]{1,0:T(8,128)}, f32[8,128]{1,0:T(8,128)}) custom-call(bf16[384,3584]{1,0:T(8,128)(2,1)} %copy-done.1, bf16[2048,1536]{1,0:T(8,128)(2,1)} %all-gather.5.cloned.1.call-done.refs_1_, bf16[2048,1536]{1,0:T(8,128)(2,1)} %all-gather.7.cloned.1.call-done.refs_2_, ...), custom_call_target="tpu_custom_call" | custom-call | flops 12079595520 | bytes 8847360 | tf_op jit(solution)/shard_map/weight_grads/pallas_call | solution.py:119
  688.1 73.9 %weight_grads.6 = (f32[2240,1536]{1,0:T(8,128)}, f32[2240,1536]{1,0:T(8,128)}, f32[2240,1536]{1,0:T(8,128)}, f32[8,128]{1,0:T(8,128)}) custom-call(bf16[384,3584]{1,0:T(8,128)(2,1)} %add_convert_fusion.2.refs_0_, bf16[2048,1536]{1,0:T(8,128)(2,1)} %all-gather.5.cloned.1.call-done.refs_1_, ...), custom_call_target="tpu_custom_call", output_to_operand_aliasing={{0}: (6, {}), {1}: (7, {}), {2}: (8, {})} | custom-call | flops 60397977600 | bytes 44236800 | tf_op jit(solution)/shard_map/weight_grads/pallas_call | solution.py:119
  779.4 18.4 %weight_grads.7 = (f32[2240,1536]{1,0:T(8,128)}, f32[2240,1536]{1,0:T(8,128)}, f32[2240,1536]{1,0:T(8,128)}, f32[8,128]{1,0:T(8,128)}) custom-call(bf16[96,3584]{1,0:T(8,128)(2,1)} %get-tuple-element.213.refs_0_, bf16[2048,1536]{1,0:T(8,128)(2,1)} %all-gather.5.cloned.1.call-done.refs_1_, ...), custom_call_target="tpu_custom_call", output_to_operand_aliasing={{0}: (6, {}), {1}: (7, {}), {2}: (8, {})} | custom-call | flops 12079595520 | bytes 8847360 | tf_op jit(solution)/shard_map/weight_grads/pallas_call | solution.py:119
  797.8 48.0 %weight_grads.8 = (f32[2240,1536]{1,0:T(8,128)}, f32[2240,1536]{1,0:T(8,128)}, f32[2240,1536]{1,0:T(8,128)}, f32[8,128]{1,0:T(8,128)}) custom-call(bf16[2048,1536]{1,0:T(8,128)(2,1)} %all-gather.9.cloned.1.call-done.refs_0_.refs_1_, ...), custom_call_target="tpu_custom_call", output_to_operand_aliasing={{0}: (5, {}), {1}: (6, {}), {2}: (7, {})} | custom-call | flops 36238786560 | bytes 26542080 | tf_op jit(solution)/shard_map/weight_grads/pallas_call | solution.py:119
  856.0 61.4 %weight_grads.9 = (f32[2240,1536]{1,0:T(8,128)}, f32[2240,1536]{1,0:T(8,128)}, f32[2240,1536]{1,0:T(8,128)}, f32[8,128]{1,0:T(8,128)}) custom-call(bf16[96,3584]{1,0:T(8,128)(2,1)} %add_convert_fusion.3.refs_0_.refs_2_, bf16[2048,1536]{1,0:T(8,128)(2,1)} %all-gather.9.cloned.1.call-done.refs_0_.refs_1_, ...), custom_call_target="tpu_custom_call", output_to_operand_aliasing={{0}: (6, {}), {1}: (7, {}), {2}: (8, {})} | custom-call | flops 48318382080 | bytes 35389440 | tf_op jit(solution)/shard_map/weight_grads/pallas_call | solution.py:119
  (481 shorter events, 246.0 us)
Async XLA Ops:
  7.2 649.0 %all-gather.5.cloned.1.call-start = ((), (), s32[]{:S(2)}) async-start(), calls=%async_computation | async-start | bytes 6684672 | tf_op jit(solution)/shard_map/all_gather | solution.py:1211
  13.4 13.3 %collective-permute-start.7 = (bf16[384,512]{1,0:T(8,128)(2,1)S(1)}, bf16[384,512]{1,0:T(8,128)(2,1)S(1)}, u32[]{:S(2)}, u32[]{:S(2)}) collective-permute-start(bf16[384,512]{1,0:T(8,128)(2,1)S(1)} %slice_bitcast_fusion.1.refs_6_.refs_7_.refs_16_), channel_id=1, source_target_pairs={{0,1},{1,0},{2,3},{3,2},{4,5},{5,4},{6,7},{7,6},{8,9},{9,8},{10,11... | collective-permute-start | bytes 1179656 | tf_op jit(solution)/shard_map/ppermute | solution.py:67
  16.3 53.2 %collective-permute-start.14 = (bf16[384,1536]{1,0:T(8,128)(2,1)}, bf16[384,1536]{1,0:T(8,128)(2,1)}, u32[]{:S(2)}, u32[]{:S(2)}) collective-permute-start(bf16[384,1536]{1,0:T(8,128)(2,1)} %slice_bitcast_fusion.refs_2_.refs_7_.refs_10_), channel_id=1, source_target_pairs={{0,1},{1,0},{2,3},{3,2},{4,5},{5,4},{6,7},{7,6},{8,9},{9,8},{10,11... | collective-permute-start | bytes 3538952 | tf_op jit(solution)/shard_map/ppermute | solution.py:67
  26.1 16.3 %collective-permute-start.12 = (bf16[192,1536]{1,0:T(8,128)(2,1)S(1)}, bf16[192,1536]{1,0:T(8,128)(2,1)S(1)}, u32[]{:S(2)}, u32[]{:S(2)}) collective-permute-start(bf16[192,1536]{1,0:T(8,128)(2,1)S(1)} %rows_of.2), channel_id=1, source_target_pairs={{0,2},{1,3},{2,0},{3,1},{4,6},{5,7},{6,4},{7,5},{8,10},{9,11},{10,... | collective-permute-start | bytes 1769480 | tf_op jit(solution)/shard_map/ppermute | solution.py:67
  32.6 31.4 %collective-permute-start.17 = (bf16[192,1536]{1,0:T(8,128)(2,1)S(1)}, bf16[192,1536]{1,0:T(8,128)(2,1)}, u32[]{:S(2)}, u32[]{:S(2)}) collective-permute-start(bf16[192,1536]{1,0:T(8,128)(2,1)S(1)} %rows_of.3), channel_id=1, source_target_pairs={{0,2},{1,3},{2,0},{3,1},{4,6},{5,7},{6,4},{7,5},{8,10},{9,11},{10,... | collective-permute-start | bytes 1769480 | tf_op jit(solution)/shard_map/ppermute | solution.py:67
  42.4 27.1 %collective-permute-start.13 = (bf16[192,1536]{1,0:T(8,128)(2,1)S(1)}, bf16[192,1536]{1,0:T(8,128)(2,1)}, u32[]{:S(2)}, u32[]{:S(2)}) collective-permute-start(bf16[192,1536]{1,0:T(8,128)(2,1)S(1)} %collective-permute-done.12.refs_8_.refs_11_), channel_id=1, source_target_pairs={{0,4},{4,0},{8,12},{12,8},{1,5},{5,1},{9,13},{13,9},{2,6},{6,2},{1... | collective-permute-start | bytes 1769480 | tf_op jit(solution)/shard_map/ppermute | solution.py:67
  44.0 15.9 %collective-permute-start.10 = (bf16[128,512]{1,0:T(8,128)(2,1)S(1)}, bf16[128,512]{1,0:T(8,128)(2,1)S(1)}, u32[]{:S(2)}, u32[]{:S(2)}) collective-permute-start(bf16[128,512]{1,0:T(8,128)(2,1)S(1)} %project.6.refs_0_.refs_1_), channel_id=1, source_target_pairs={{0,8},{4,12},{8,0},{12,4},{1,9},{5,13},{9,1},{13,5},{2,10},{6,14},... | collective-permute-start | bytes 393224 | tf_op jit(solution)/shard_map/ppermute | solution.py:67
  46.6 19.7 %collective-permute-start.11 = (bf16[128,512]{1,0:T(8,128)(2,1)S(1)}, bf16[128,512]{1,0:T(8,128)(2,1)S(1)}, u32[]{:S(2)}, u32[]{:S(2)}) collective-permute-start(bf16[128,512]{1,0:T(8,128)(2,1)S(1)} %project.6.refs_0_.refs_1_), channel_id=1, source_target_pairs={{0,12},{4,8},{8,4},{12,0},{1,13},{5,9},{9,5},{13,1},{2,14},{6,10},... | collective-permute-start | bytes 393224 | tf_op jit(solution)/shard_map/ppermute | solution.py:67
  64.1 16.7 %collective-permute-start.18 = (bf16[192,1536]{1,0:T(8,128)(2,1)}, bf16[192,1536]{1,0:T(8,128)(2,1)}, u32[]{:S(2)}, u32[]{:S(2)}) collective-permute-start(bf16[192,1536]{1,0:T(8,128)(2,1)} %collective-permute-done.17.refs_7_.refs_10_.refs_9_), channel_id=1, source_target_pairs={{0,4},{4,0},{8,12},{12,8},{1,5},{5,1},{9,13},{13,9},{2,6},{6,2},{1... | collective-permute-start | bytes 1769480 | tf_op jit(solution)/shard_map/ppermute | solution.py:67
  66.3 19.6 %collective-permute-start.19 = (bf16[384,1536]{1,0:T(8,128)(2,1)}, bf16[384,1536]{1,0:T(8,128)(2,1)}, u32[]{:S(2)}, u32[]{:S(2)}) collective-permute-start(bf16[384,1536]{1,0:T(8,128)(2,1)} %bitcast.98), channel_id=1, source_target_pairs={{0,1},{1,0},{2,3},{3,2},{4,5},{5,4},{6,7},{7,6},{8,9},{9,8},{10,11... | collective-permute-start | bytes 3538952 | tf_op jit(solution)/shard_map/ppermute | solution.py:67
  94.4 17.7 %collective-permute-start.26 = (bf16[128,1536]{1,0:T(8,128)(2,1)S(1)}, bf16[128,1536]{1,0:T(8,128)(2,1)S(1)}, u32[]{:S(2)}, u32[]{:S(2)}) collective-permute-start(bf16[128,1536]{1,0:T(8,128)(2,1)S(1)} %get-tuple-element.114.refs_1_.refs_5_), channel_id=1, source_target_pairs={{0,1},{1,0},{2,3},{3,2},{4,5},{5,4},{6,7},{7,6},{8,9},{9,8},{10,11... | collective-permute-start | bytes 1179656 | tf_op jit(solution)/shard_map/ppermute | solution.py:67
  166.0 15.0 %collective-permute-start = (bf16[128,1536]{1,0:T(8,128)(2,1)S(1)}, bf16[128,1536]{1,0:T(8,128)(2,1)S(1)}, u32[]{:S(2)}, u32[]{:S(2)}) collective-permute-start(bf16[128,1536]{1,0:T(8,128)(2,1)S(1)} %select_n.202.refs_9_.refs_3_.refs_2_), channel_id=1, source_target_pairs={{0,2},{1,3},{2,0},{3,1},{4,6},{5,7},{6,4},{7,5},{8,10},{9,11},{10,... | collective-permute-start | bytes 1179656 | tf_op jit(solution)/shard_map/ppermute | solution.py:67
  167.6 15.1 %collective-permute-start.35 = (bf16[512,512]{1,0:T(8,128)(2,1)S(1)}, bf16[512,512]{1,0:T(8,128)(2,1)S(1)}, u32[]{:S(2)}, u32[]{:S(2)}) collective-permute-start(bf16[512,512]{1,0:T(8,128)(2,1)S(1)} %join.4.refs_3_.refs_15_.refs_19_), channel_id=1, source_target_pairs={{0,1},{1,0},{2,3},{3,2},{4,5},{5,4},{6,7},{7,6},{8,9},{9,8},{10,11... | collective-permute-start | bytes 1572872 | tf_op jit(solution)/shard_map/ppermute | solution.py:67
  195.5 460.7 %all-gather.7.cloned.1.call-start = ((), (), s32[]{:S(2)}) async-start(), calls=%async_computation.1 | async-start | bytes 6684672 | tf_op jit(solution)/shard_map/all_gather | solution.py:1211
  196.5 18.8 %collective-permute-start.38 = (bf16[128,1536]{1,0:T(8,128)(2,1)S(1)}, bf16[128,1536]{1,0:T(8,128)(2,1)S(1)}, u32[]{:S(2)}, u32[]{:S(2)}) collective-permute-start(bf16[128,1536]{1,0:T(8,128)(2,1)S(1)} %get-tuple-element.122.refs_1_.refs_5_.refs_2_), channel_id=1, source_target_pairs={{0,1},{1,0},{2,3},{3,2},{4,5},{5,4},{6,7},{7,6},{8,9},{9,8},{10,11... | collective-permute-start | bytes 1179656 | tf_op jit(solution)/shard_map/ppermute | solution.py:67
  251.6 16.6 %collective-permute-start.42 = (bf16[256,1536]{1,0:T(8,128)(2,1)S(1)}, bf16[256,1536]{1,0:T(8,128)(2,1)S(1)}, u32[]{:S(2)}, u32[]{:S(2)}) collective-permute-start(bf16[256,1536]{1,0:T(8,128)(2,1)S(1)} %get-tuple-element.129), channel_id=1, source_target_pairs={{0,1},{1,0},{2,3},{3,2},{4,5},{5,4},{6,7},{7,6},{8,9},{9,8},{10,11... | collective-permute-start | bytes 2359304 | tf_op jit(solution)/shard_map/ppermute | solution.py:67
  291.3 13.4 %collective-permute-start.46 = (bf16[128,512]{1,0:T(8,128)(2,1)S(1)}, bf16[128,512]{1,0:T(8,128)(2,1)S(1)}, u32[]{:S(2)}, u32[]{:S(2)}) collective-permute-start(bf16[128,512]{1,0:T(8,128)(2,1)S(1)} %project.10.refs_0_.refs_1_), channel_id=1, source_target_pairs={{0,4},{4,0},{8,12},{12,8},{1,5},{5,1},{9,13},{13,9},{2,6},{6,2},{1... | collective-permute-start | bytes 393224 | tf_op jit(solution)/shard_map/ppermute | solution.py:67
  312.5 15.0 %collective-permute-start.53 = (bf16[512,512]{1,0:T(8,128)(2,1)S(1)}, bf16[512,512]{1,0:T(8,128)(2,1)}, u32[]{:S(2)}, u32[]{:S(2)}) collective-permute-start(bf16[512,512]{1,0:T(8,128)(2,1)S(1)} %join.5.refs_0_.refs_12_.refs_22_), channel_id=1, source_target_pairs={{0,2},{1,3},{2,0},{3,1},{4,6},{5,7},{6,4},{7,5},{8,10},{9,11},{10,... | collective-permute-start | bytes 1572872 | tf_op jit(solution)/shard_map/ppermute | solution.py:67
  312.9 23.9 %collective-permute-start.49 = (bf16[512,512]{1,0:T(8,128)(2,1)S(1)}, bf16[512,512]{1,0:T(8,128)(2,1)S(1)}, u32[]{:S(2)}, u32[]{:S(2)}) collective-permute-start(bf16[512,512]{1,0:T(8,128)(2,1)S(1)} %add_up.20.refs_0_), channel_id=1, source_target_pairs={{0,2},{1,3},{2,0},{3,1},{4,6},{5,7},{6,4},{7,5},{8,10},{9,11},{10,... | collective-permute-start | bytes 1572872 | tf_op jit(solution)/shard_map/ppermute | solution.py:67
  314.6 46.8 %collective-permute-start.54 = (bf16[512,512]{1,0:T(8,128)(2,1)S(1)}, bf16[512,512]{1,0:T(8,128)(2,1)}, u32[]{:S(2)}, u32[]{:S(2)}) collective-permute-start(bf16[512,512]{1,0:T(8,128)(2,1)S(1)} %join.5.refs_0_.refs_12_.refs_22_), channel_id=1, source_target_pairs={{0,1},{1,0},{2,3},{3,2},{4,5},{5,4},{6,7},{7,6},{8,9},{9,8},{10,11... | collective-permute-start | bytes 1572872 | tf_op jit(solution)/shard_map/ppermute | solution.py:67
  327.5 33.8 %collective-permute-start.55 = (bf16[512,512]{1,0:T(8,128)(2,1)}, bf16[512,512]{1,0:T(8,128)(2,1)}, u32[]{:S(2)}, u32[]{:S(2)}) collective-permute-start(bf16[512,512]{1,0:T(8,128)(2,1)} %collective-permute-done.53.refs_13_.refs_24_), channel_id=1, source_target_pairs={{0,1},{1,0},{2,3},{3,2},{4,5},{5,4},{6,7},{7,6},{8,9},{9,8},{10,11... | collective-permute-start | bytes 1572872 | tf_op jit(solution)/shard_map/ppermute | solution.py:67
  373.2 424.6 %all-gather.9.cloned.1.call-start = ((), (), s32[]{:S(2)}) async-start(), calls=%async_computation.2 | async-start | bytes 6684672 | tf_op jit(solution)/shard_map/all_gather | solution.py:1211
  373.6 20.7 %collective-permute-start.57 = (bf16[128,1536]{1,0:T(8,128)(2,1)S(1)}, bf16[128,1536]{1,0:T(8,128)(2,1)S(1)}, u32[]{:S(2)}, u32[]{:S(2)}) collective-permute-start(bf16[128,1536]{1,0:T(8,128)(2,1)S(1)} %get-tuple-element.144.refs_6_.refs_1_.refs_2_), channel_id=1, source_target_pairs={{0,2},{1,3},{2,0},{3,1},{4,6},{5,7},{6,4},{7,5},{8,10},{9,11},{10,... | collective-permute-start | bytes 1179656 | tf_op jit(solution)/shard_map/ppermute | solution.py:67
  375.4 26.1 %collective-permute-start.61 = (bf16[128,1536]{1,0:T(8,128)(2,1)S(1)}, bf16[128,1536]{1,0:T(8,128)(2,1)S(1)}, u32[]{:S(2)}, u32[]{:S(2)}) collective-permute-start(bf16[128,1536]{1,0:T(8,128)(2,1)S(1)} %select.66.refs_0_.refs_13_.refs_3_.refs_1_.refs_2_), channel_id=1, source_target_pairs={{0,1},{1,0},{2,3},{3,2},{4,5},{5,4},{6,7},{7,6},{8,9},{9,8},{10,11... | collective-permute-start | bytes 1179656 | tf_op jit(solution)/shard_map/ppermute | solution.py:67
  375.4 26.1 %collective-permute-start.58 = (bf16[128,1536]{1,0:T(8,128)(2,1)S(1)}, bf16[128,1536]{1,0:T(8,128)(2,1)S(1)}, u32[]{:S(2)}, u32[]{:S(2)}) collective-permute-start(bf16[128,1536]{1,0:T(8,128)(2,1)S(1)} %get-tuple-element.144.refs_6_.refs_1_.refs_2_), channel_id=1, source_target_pairs={{0,1},{1,0},{2,3},{3,2},{4,5},{5,4},{6,7},{7,6},{8,9},{9,8},{10,11... | collective-permute-start | bytes 1179656 | tf_op jit(solution)/shard_map/ppermute | solution.py:67
  386.1 15.4 %collective-permute-start.62 = (bf16[128,1536]{1,0:T(8,128)(2,1)S(1)}, bf16[128,1536]{1,0:T(8,128)(2,1)S(1)}, u32[]{:S(2)}, u32[]{:S(2)}) collective-permute-start(bf16[128,1536]{1,0:T(8,128)(2,1)S(1)} %collective-permute-done.60.refs_14_), channel_id=1, source_target_pairs={{0,1},{1,0},{2,3},{3,2},{4,5},{5,4},{6,7},{7,6},{8,9},{9,8},{10,11... | collective-permute-start | bytes 1179656 | tf_op jit(solution)/shard_map/ppermute | solution.py:67
  426.8 371.0 %all-gather.11.cloned.1.call-start = ((), (), s32[]{:S(2)}) async-start(), calls=%async_computation.3 | async-start | bytes 6684672 | tf_op jit(solution)/shard_map/all_gather | solution.py:1211
  456.5 14.0 %collective-permute-start.66 = (bf16[512,512]{1,0:T(8,128)(2,1)S(1)}, bf16[512,512]{1,0:T(8,128)(2,1)S(1)}, u32[]{:S(2)}, u32[]{:S(2)}) collective-permute-start(bf16[512,512]{1,0:T(8,128)(2,1)S(1)} %add_up.23.refs_0_), channel_id=1, source_target_pairs={{0,2},{1,3},{2,0},{3,1},{4,6},{5,7},{6,4},{7,5},{8,10},{9,11},{10,... | collective-permute-start | bytes 1572872 | tf_op jit(solution)/shard_map/ppermute | solution.py:67
  470.7 17.7 %collective-permute-start.67 = (bf16[128,512]{1,0:T(8,128)(2,1)S(1)}, bf16[128,512]{1,0:T(8,128)(2,1)S(1)}, u32[]{:S(2)}, u32[]{:S(2)}) collective-permute-start(bf16[128,512]{1,0:T(8,128)(2,1)S(1)} %get-tuple-element.154), channel_id=1, source_target_pairs={{0,4},{4,0},{8,12},{12,8},{1,5},{5,1},{9,13},{13,9},{2,6},{6,2},{1... | collective-permute-start | bytes 393224 | tf_op jit(solution)/shard_map/ppermute | solution.py:67
  477.2 20.4 %collective-permute-start.68 = (bf16[128,512]{1,0:T(8,128)(2,1)S(1)}, bf16[128,512]{1,0:T(8,128)(2,1)S(1)}, u32[]{:S(2)}, u32[]{:S(2)}) collective-permute-start(bf16[128,512]{1,0:T(8,128)(2,1)S(1)} %get-tuple-element.155), channel_id=1, source_target_pairs={{0,8},{4,12},{8,0},{12,4},{1,9},{5,13},{9,1},{13,5},{2,10},{6,14},... | collective-permute-start | bytes 393224 | tf_op jit(solution)/shard_map/ppermute | solution.py:67
  477.2 20.4 %collective-permute-start.69 = (bf16[128,512]{1,0:T(8,128)(2,1)S(1)}, bf16[128,512]{1,0:T(8,128)(2,1)S(1)}, u32[]{:S(2)}, u32[]{:S(2)}) collective-permute-start(bf16[128,512]{1,0:T(8,128)(2,1)S(1)} %get-tuple-element.156), channel_id=1, source_target_pairs={{0,12},{4,8},{8,4},{12,0},{1,13},{5,9},{9,5},{13,1},{2,14},{6,10},... | collective-permute-start | bytes 393224 | tf_op jit(solution)/shard_map/ppermute | solution.py:67
  514.5 14.5 %collective-permute-start.72 = (bf16[128,1536]{1,0:T(8,128)(2,1)S(1)}, bf16[128,1536]{1,0:T(8,128)(2,1)S(1)}, u32[]{:S(2)}, u32[]{:S(2)}) collective-permute-start(bf16[128,1536]{1,0:T(8,128)(2,1)S(1)} %collective-permute-done.70.refs_9_.refs_3_.refs_1_), channel_id=1, source_target_pairs={{0,1},{1,0},{2,3},{3,2},{4,5},{5,4},{6,7},{7,6},{8,9},{9,8},{10,11... | collective-permute-start | bytes 1179656 | tf_op jit(solution)/shard_map/ppermute | solution.py:67
  551.3 13.0 %collective-permute-start.74 = (bf16[256,1536]{1,0:T(8,128)(2,1)S(1)}, bf16[256,1536]{1,0:T(8,128)(2,1)S(1)}, u32[]{:S(2)}, u32[]{:S(2)}) collective-permute-start(bf16[256,1536]{1,0:T(8,128)(2,1)S(1)} %get-tuple-element.163), channel_id=1, source_target_pairs={{0,1},{1,0},{2,3},{3,2},{4,5},{5,4},{6,7},{7,6},{8,9},{9,8},{10,11... | collective-permute-start | bytes 2359304 | tf_op jit(solution)/shard_map/ppermute | solution.py:67
  590.6 14.0 %collective-permute-start.77 = (bf16[512,512]{1,0:T(8,128)(2,1)S(1)}, bf16[512,512]{1,0:T(8,128)(2,1)S(1)}, u32[]{:S(2)}, u32[]{:S(2)}) collective-permute-start(bf16[512,512]{1,0:T(8,128)(2,1)S(1)} %add_up.26.refs_0_), channel_id=1, source_target_pairs={{0,2},{1,3},{2,0},{3,1},{4,6},{5,7},{6,4},{7,5},{8,10},{9,11},{10,... | collective-permute-start | bytes 1572872 | tf_op jit(solution)/shard_map/ppermute | solution.py:67
  604.9 15.1 %collective-permute-start.78 = (bf16[128,512]{1,0:T(8,128)(2,1)S(1)}, bf16[128,512]{1,0:T(8,128)(2,1)S(1)}, u32[]{:S(2)}, u32[]{:S(2)}) collective-permute-start(bf16[128,512]{1,0:T(8,128)(2,1)S(1)} %get-tuple-element.170), channel_id=1, source_target_pairs={{0,4},{4,0},{8,12},{12,8},{1,5},{5,1},{9,13},{13,9},{2,6},{6,2},{1... | collective-permute-start | bytes 393224 | tf_op jit(solution)/shard_map/ppermute | solution.py:67
  645.9 30.8 %collective-permute-start.82 = (bf16[384,3584]{1,0:T(8,128)(2,1)}, bf16[384,3584]{1,0:T(8,128)(2,1)}, u32[]{:S(2)}, u32[]{:S(2)}) collective-permute-start(bf16[384,3584]{1,0:T(8,128)(2,1)} %get-tuple-element.190), channel_id=1, source_target_pairs={{0,1},{1,0},{2,3},{3,2},{4,5},{5,4},{6,7},{7,6},{8,9},{9,8},{10,11... | collective-permute-start | bytes 8257544 | tf_op jit(solution)/shard_map/ppermute | solution.py:67
  650.0 33.3 %collective-permute-start.81 = (bf16[384,3584]{1,0:T(8,128)(2,1)}, bf16[384,3584]{1,0:T(8,128)(2,1)}, u32[]{:S(2)}, u32[]{:S(2)}) collective-permute-start(bf16[384,3584]{1,0:T(8,128)(2,1)} %copy-done.57), channel_id=1, source_target_pairs={{0,1},{1,0},{2,3},{3,2},{4,5},{5,4},{6,7},{7,6},{8,9},{9,8},{10,11... | collective-permute-start | bytes 8257544 | tf_op jit(solution)/shard_map/ppermute | solution.py:67
  654.5 111.4 %collective-permute-start.88 = (bf16[128,1536]{1,0:T(8,128)(2,1)}, bf16[128,1536]{1,0:T(8,128)(2,1)}, u32[]{:S(2)}, u32[]{:S(2)}) collective-permute-start(bf16[128,1536]{1,0:T(8,128)(2,1)} %add_up.28.refs_0_), channel_id=1, source_target_pairs={{0,2},{1,3},{2,0},{3,1},{4,6},{5,7},{6,4},{7,5},{8,10},{9,11},{10,... | collective-permute-start | bytes 1179656 | tf_op jit(solution)/shard_map/ppermute | solution.py:67
  682.3 87.6 %collective-permute-start.83 = (bf16[384,3584]{1,0:T(8,128)(2,1)}, bf16[384,3584]{1,0:T(8,128)(2,1)}, u32[]{:S(2)}, u32[]{:S(2)}) collective-permute-start(bf16[384,3584]{1,0:T(8,128)(2,1)} %add_convert_fusion.1), channel_id=1, source_target_pairs={{0,2},{1,3},{2,0},{3,1},{4,6},{5,7},{6,4},{7,5},{8,10},{9,11},{10,... | collective-permute-start | bytes 8257544 | tf_op jit(solution)/shard_map/ppermute | solution.py:67
  683.2 80.0 %collective-permute-start.89 = (f32[40,128]{1,0:T(8,128)S(1)}, f32[40,128]{1,0:T(8,128)S(1)}, u32[]{:S(2)}, u32[]{:S(2)}) collective-permute-start(f32[40,128]{1,0:T(8,128)S(1)} %bitcast.105), channel_id=1, source_target_pairs={{0,1},{1,0},{2,3},{3,2},{4,5},{5,4},{6,7},{7,6},{8,9},{9,8},{10,11... | collective-permute-start | bytes 61448 | tf_op jit(solution)/shard_map/ppermute | solution.py:67
  767.6 87.2 %collective-permute-start.91 = (f32[40,128]{1,0:T(8,128)S(1)}, f32[40,128]{1,0:T(8,128)S(1)}, u32[]{:S(2)}, u32[]{:S(2)}) collective-permute-start(f32[40,128]{1,0:T(8,128)S(1)} %add.331), channel_id=1, source_target_pairs={{0,8},{4,12},{8,0},{12,4},{1,9},{5,13},{9,1},{13,5},{2,10},{6,14},... | collective-permute-start | bytes 61448 | tf_op jit(solution)/shard_map/ppermute | solution.py:67
  775.0 72.0 %collective-permute-start.84 = (bf16[96,3584]{1,0:T(8,128)(2,1)S(1)}, bf16[96,3584]{1,0:T(8,128)(2,1)}, u32[]{:S(2)}, u32[]{:S(2)}) collective-permute-start(bf16[96,3584]{1,0:T(8,128)(2,1)S(1)} %get-tuple-element.216), channel_id=1, source_target_pairs={{0,4},{4,0},{8,12},{12,8},{1,5},{5,1},{9,13},{13,9},{2,6},{6,2},{1... | collective-permute-start | bytes 2064392 | tf_op jit(solution)/shard_map/ppermute | solution.py:67
  776.4 70.6 %collective-permute-start.85 = (bf16[96,3584]{1,0:T(8,128)(2,1)S(1)}, bf16[96,3584]{1,0:T(8,128)(2,1)}, u32[]{:S(2)}, u32[]{:S(2)}) collective-permute-start(bf16[96,3584]{1,0:T(8,128)(2,1)S(1)} %get-tuple-element.215), channel_id=1, source_target_pairs={{0,8},{4,12},{8,0},{12,4},{1,9},{5,13},{9,1},{13,5},{2,10},{6,14},... | collective-permute-start | bytes 2064392 | tf_op jit(solution)/shard_map/ppermute | solution.py:67
  779.3 67.7 %collective-permute-start.86 = (bf16[96,3584]{1,0:T(8,128)(2,1)S(1)}, bf16[96,3584]{1,0:T(8,128)(2,1)}, u32[]{:S(2)}, u32[]{:S(2)}) collective-permute-start(bf16[96,3584]{1,0:T(8,128)(2,1)S(1)} %get-tuple-element.214), channel_id=1, source_target_pairs={{0,12},{4,8},{8,4},{12,0},{1,13},{5,9},{9,5},{13,1},{2,14},{6,10},... | collective-permute-start | bytes 2064392 | tf_op jit(solution)/shard_map/ppermute | solution.py:67
  850.4 76.1 %collective-permute-start.93 = (bf16[96,3584]{1,0:T(8,128)(2,1)}, bf16[96,3584]{1,0:T(8,128)(2,1)S(1)}, u32[]{:S(2)}, u32[]{:S(2)}) collective-permute-start(bf16[96,3584]{1,0:T(8,128)(2,1)} %add_convert_fusion.3.refs_0_.refs_2_), channel_id=1, source_target_pairs={{0,4},{4,0},{8,12},{12,8},{1,5},{5,1},{9,13},{13,9},{2,6},{6,2},{1... | collective-permute-start | bytes 2064392 | tf_op jit(solution)/shard_map/ppermute | solution.py:67
  850.9 75.6 %collective-permute-start.94 = (bf16[96,3584]{1,0:T(8,128)(2,1)}, bf16[96,3584]{1,0:T(8,128)(2,1)S(1)}, u32[]{:S(2)}, u32[]{:S(2)}) collective-permute-start(bf16[96,3584]{1,0:T(8,128)(2,1)} %add_convert_fusion.3.refs_0_.refs_2_), channel_id=1, source_target_pairs={{0,8},{4,12},{8,0},{12,4},{1,9},{5,13},{9,1},{13,5},{2,10},{6,14},... | collective-permute-start | bytes 2064392 | tf_op jit(solution)/shard_map/ppermute | solution.py:67
  854.7 71.8 %collective-permute-start.95 = (bf16[96,3584]{1,0:T(8,128)(2,1)}, bf16[96,3584]{1,0:T(8,128)(2,1)}, u32[]{:S(2)}, u32[]{:S(2)}) collective-permute-start(bf16[96,3584]{1,0:T(8,128)(2,1)} %add_convert_fusion.3.refs_0_.refs_2_), channel_id=1, source_target_pairs={{0,12},{4,8},{8,4},{12,0},{1,13},{5,9},{9,5},{13,1},{2,14},{6,10},... | collective-permute-start | bytes 2064392 | tf_op jit(solution)/shard_map/ppermute | solution.py:67
  855.5 68.6 %collective-permute-start.92 = (f32[40,128]{1,0:T(8,128)S(1)}, f32[40,128]{1,0:T(8,128)S(1)}, u32[]{:S(2)}, u32[]{:S(2)}) collective-permute-start(f32[40,128]{1,0:T(8,128)S(1)} %add_add_fusion), channel_id=1, source_target_pairs={{0,4},{4,0},{8,12},{12,8},{1,5},{5,1},{9,13},{13,9},{2,6},{6,2},{1... | collective-permute-start | bytes 61448 | tf_op jit(solution)/shard_map/ppermute | solution.py:67
  (153 other events, 3228.5 us)
Sparse Core Ops, SparseCore 0:
  195.6 65.4 all-gather.4
  373.4 64.9 all-gather.6
  440.7 69.4 all-gather.8
  650.1 78.4 all-gather.10
